TPU v7x, 256 devices: a whole 4x4x8 slice. The times are simulated.
256 devices in a mesh: batch: 32 (over z, y), space: 8 (over x, core).
Axes of the slice: x: 4, y: 4, z: 8, core: 2. Of those that a mesh axis runs over, the one named last changes fastest.
Arguments:
- features: bfloat16 [32, 96, 72, 1024], P('batch', 'space'), may hold values from -600 to 600
- depth_one: bfloat16 [3, 3, 1024], replicated, may hold values from -2 to 2
- gain_one: float32 [1024], replicated, may hold values from 0.25 to 1.75
- shift_one: float32 [1024], replicated, may hold values from -3 to 3
- point_one: bfloat16 [1024, 1536], replicated, may hold values from -0.1875 to 0.1875
- gain_two: float32 [1536], replicated, may hold values from 0.25 to 1.75
- shift_two: float32 [1536], replicated, may hold values from -3 to 3
- depth_two: bfloat16 [3, 3, 1536], replicated, may hold values from -2 to 2
- gain_three: float32 [1536], replicated, may hold values from 0.25 to 1.75
- shift_three: float32 [1536], replicated, may hold values from -3 to 3
- point_two: bfloat16 [1536, 2048], replicated, may hold values from -0.15625 to 0.15625
- gain_four: float32 [2048], replicated, may hold values from 0.25 to 1.75
- shift_four: float32 [2048], replicated, may hold values from -3 to 3
Outputs:
- exit_map: bfloat16 [32, 96, 72, 2048], P('batch', 'space')
All inputs are finite; a program needn't handle non-finite values.
Results may differ from a plain program's by a relative error of at most 0.0079.
Values may be sent and summed in bfloat16 or wider, within the bound.
No kernel may reach another device: no remote copies, remote signals or barrier semaphores. Data moves between devices by JAX's collectives and lax.ppermute only.
A program may use at most 64 MiB of HBM per device.

v0:
```python
import functools

import jax
import jax.numpy as jnp
from jax import lax
from jax.sharding import Mesh
from jax.sharding import PartitionSpec as P

RATE = 2
BATCH = ("batch_0", "batch_1")
SPACE = ("space_0", "space_1")
BATCH_SPACE = ("batch_0", "batch_1", "space_0", "space_1")


epsilon = 1e-05


def padded_2(cells, sides, width):
    for axis, dim in sides:
        count = lax.axis_size(axis)
        ends = count - 1
        head = lax.slice_in_dim(cells, 0, width, axis=dim)
        tail = lax.slice_in_dim(cells, cells.shape[dim] - width, cells.shape[dim], axis=dim)
        cells = jnp.concatenate(
            [
                lax.ppermute(tail, axis, [(i, (i + 1) % count) for i in range(ends)]),
                cells,
                lax.ppermute(head, axis, [((i + 1) % count, i) for i in range(ends)]),
            ],
            axis=dim,
        )
    return cells


def one_axis_at_a_time(value, axes):
    return functools.reduce(lax.psum, axes, value)


def dilated_padded(padded, weight, span_rows, span_cols):
    summed = jnp.zeros((padded.shape[0], span_rows, span_cols, padded.shape[3]), jnp.float32)
    for tap_row in range(3):
        for tap_col in range(3):
            window = padded[
                :,
                tap_row * RATE : tap_row * RATE + span_rows,
                tap_col * RATE : tap_col * RATE + span_cols,
                :,
            ]
            summed = summed + window.astype(jnp.float32) * weight[tap_row, tap_col].astype(
                jnp.float32
            )
    return summed


def local_sums(values):
    return (jnp.sum(values, axis=(0, 1, 2)), jnp.sum(values * values, axis=(0, 1, 2)))


def scaled(values, totals, pixels, gain, offset):
    average = totals[0] / pixels
    variance = totals[1] / pixels - average * average
    factor = gain * lax.rsqrt(variance + epsilon)
    return jnp.maximum((values - average) * factor + offset, 0.0).astype(jnp.bfloat16)


def project(values, weight):
    shape = values.shape
    flat = values.reshape(shape[0] * shape[1] * shape[2], shape[3])
    result = jnp.dot(flat, weight, preferred_element_type=jnp.float32)
    return result.reshape(shape[0], shape[1], shape[2], weight.shape[1])


def per_device(
    features,
    depth_one,
    gain_one,
    shift_one,
    point_one,
    gain_two,
    shift_two,
    depth_two,
    gain_three,
    shift_three,
    point_two,
    gain_four,
    shift_four,
):
    span_rows = features.shape[1]
    span_cols = features.shape[2]
    n_batch = lax.axis_size(BATCH)
    n_space = lax.axis_size(SPACE)
    all_pixels = features.shape[0] * span_rows * span_cols * n_batch * n_space
    padded = padded_2(features, ((SPACE, 1),), RATE)
    padded = jnp.pad(padded, ((0, 0), (0, 0), (RATE, RATE), (0, 0)))
    first = dilated_padded(padded, depth_one, span_rows, span_cols)
    totals = jax.tree.map(lambda part: one_axis_at_a_time(part, BATCH_SPACE), local_sums(first))
    act_one = scaled(first, totals, all_pixels, gain_one, shift_one)
    second = project(act_one, point_one)
    totals = jax.tree.map(lambda part: one_axis_at_a_time(part, BATCH_SPACE), local_sums(second))
    act_two = scaled(second, totals, all_pixels, gain_two, shift_two)
    padded = padded_2(act_two, ((SPACE, 1),), RATE)
    padded = jnp.pad(padded, ((0, 0), (0, 0), (RATE, RATE), (0, 0)))
    third = dilated_padded(padded, depth_two, span_rows, span_cols)
    totals = jax.tree.map(lambda part: one_axis_at_a_time(part, BATCH_SPACE), local_sums(third))
    act_three = scaled(third, totals, all_pixels, gain_three, shift_three)
    fourth = project(act_three, point_two)
    totals = jax.tree.map(lambda part: one_axis_at_a_time(part, BATCH_SPACE), local_sums(fourth))
    return scaled(fourth, totals, all_pixels, gain_four, shift_four)


def solution(mesh):
    finer = Mesh(mesh.devices.reshape(8, 4, 4, 2), ("batch_0", "batch_1", "space_0", "space_1"))
    placed = (
        P(BATCH, SPACE, None, None),
        P(),
        P(),
        P(),
        P(),
        P(),
        P(),
        P(),
        P(),
        P(),
        P(),
        P(),
        P(),
    )
    return jax.shard_map(
        per_device,
        mesh=finer,
        in_specs=placed,
        out_specs=P(BATCH, SPACE, None, None),
        check_vma=False,
    )
```

profile of v0, /device:TPU:2, one launch (start us, length us, event | category | flops | bytes accessed | tf_op | source)
XLA Modules:
  0.0 293.7 jit_solution(15984649310484246818)
XLA Ops:
  0.0 0.0 copy-start
  0.0 0.0 copy-start.1
  0.0 1.2 fusion.17
  1.3 2.1 collective-permute-start
  3.3 3.6 %collective-permute-start.1 = (bf16[1,2,72,1024]{3,2,1,0:T(8,128)(2,1)S(1)}, bf16[1,2,72,1024]{3,2,1,0:T(8,128)(2,1)S(1)}, u32[]{:S(2)}, u32[]{:S(2)}) collective-permute-start(bf16[1,2,72,1024]{3,2,1,0:T(8,128)(2,1)S(1)} %get-tuple-element.59), channel_id=1, source_target_pairs={{1,0},{2,1},{3,2},{4,3},{5,4},{6,5},{7,6},{9,8},{10,9},{11,10},{12... | collective-permute-start | bytes 884744 | tf_op jit(solution)/shard_map/ppermute | solution.py:28
  7.0 0.9 slice_convert_fusion.8
  7.9 1.6 collective-permute-done
  9.4 1.8 collective-permute-done.1
  11.2 2.3 fusion.11
  13.5 0.0 copy-done.1
  13.5 0.0 copy-start.10
  13.6 0.0 copy-start.9
  13.6 5.5 %fusion.15 = (f32[1024]{0:T(1024)S(1)}, f32[1024]{0:T(1024)S(1)}, f32[1,12,72,1024]{3,2,1,0:T(8,128)}) fusion(f32[1024]{0:T(1024)S(1)} %bitcast.28, bf16[1,16,76,1024]{3,2,1,0:T(8,128)(2,1)S(1)} %fusion.11, f32[1024]{0:T(1024)S(1)} %bitcast.29, bf16[1,2,72,1024]{3,2,1,0:T(8,128)(2,1)S(1)} %collective-permute-done.1, ...), kind=kLoop, calls=%fused_computation.59 | loop fusion | flops 27424768 | bytes 16560128 | tf_op jit(solution)/shard_map/reduce_sum | solution.py:56
  19.0 20.3 %all-reduce.5 = (f32[1024]{0:T(1024)S(1)}, f32[1024]{0:T(1024)S(1)}) all-reduce(f32[1024]{0:T(1024)S(1)} %get-tuple-element.12, f32[1024]{0:T(1024)S(1)} %get-tuple-element.11), channel_id=1, replica_groups=mesh['batch_0'=8,'batch_1'=4,'space_0'=4,'space_1'=2] {'batch_0'}, use_global_device_ids=true, to_apply=%region_6.7 | all-reduce | flops 2048 | bytes 16384 | tf_op jit(solution)/shard_map/psum | solution.py:36
  39.3 10.9 %all-reduce.13 = (f32[1024]{0:T(1024)S(1)}, f32[1024]{0:T(1024)S(1)}) all-reduce(f32[1024]{0:T(1024)S(1)} %get-tuple-element.28, f32[1024]{0:T(1024)S(1)} %get-tuple-element.29), channel_id=1, replica_groups=mesh['batch_0'=8,'batch_1'=4,'space_0'=4,'space_1'=2] {'batch_1'}, use_global_device_ids=true, to_apply=%region_7.8 | all-reduce | flops 2048 | bytes 16384 | tf_op jit(solution)/shard_map/psum | solution.py:36
  50.2 8.7 %all-reduce.9 = (f32[1024]{0:T(1024)S(1)}, f32[1024]{0:T(1024)S(1)}) all-reduce(f32[1024]{0:T(1024)S(1)} %get-tuple-element.44, f32[1024]{0:T(1024)S(1)} %get-tuple-element.45), channel_id=1, replica_groups=mesh['batch_0'=8,'batch_1'=4,'space_0'=4,'space_1'=2] {'space_0'}, use_global_device_ids=true, to_apply=%region_8.9 | all-reduce | flops 2048 | bytes 16384 | tf_op jit(solution)/shard_map/psum | solution.py:36
  58.9 2.5 all-reduce.17
  61.4 0.0 copy-done.10
  61.4 0.0 copy-done.9
  61.4 2.6 maximum_convert_fusion.3
  64.0 0.0 copy-done
  64.0 0.0 copy-start.6
  64.0 0.0 copy-start.3
  64.0 4.7 %fusion.14 = (f32[1536]{0:T(1024)S(1)}, f32[1536]{0:T(1024)S(1)}, f32[864,1536]{1,0:T(8,128)}) fusion(bf16[864,1024]{1,0:T(8,128)(2,1)S(1)} %bitcast.20, bf16[1024,1536]{1,0:T(8,128)(2,1)S(1)} %copy-done), kind=kOutput, calls=%fused_computation.58 | convolution fusion | flops 2721887232 | bytes 10235904 | tf_op jit(solution)/shard_map/dot_general | solution.py:69
  68.8 27.0 %all-reduce.4 = (f32[1536]{0:T(1024)S(1)}, f32[1536]{0:T(1024)S(1)}) all-reduce(f32[1536]{0:T(1024)S(1)} %get-tuple-element.10, f32[1536]{0:T(1024)S(1)} %get-tuple-element.9), channel_id=1, replica_groups=mesh['batch_0'=8,'batch_1'=4,'space_0'=4,'space_1'=2] {'batch_0'}, use_global_device_ids=true, to_apply=%region_16.17 | all-reduce | flops 3072 | bytes 24576 | tf_op jit(solution)/shard_map/psum | solution.py:36
  95.8 14.3 %all-reduce.12 = (f32[1536]{0:T(1024)S(1)}, f32[1536]{0:T(1024)S(1)}) all-reduce(f32[1536]{0:T(1024)S(1)} %get-tuple-element.26, f32[1536]{0:T(1024)S(1)} %get-tuple-element.27), channel_id=1, replica_groups=mesh['batch_0'=8,'batch_1'=4,'space_0'=4,'space_1'=2] {'batch_1'}, use_global_device_ids=true, to_apply=%region_17.18 | all-reduce | flops 3072 | bytes 24576 | tf_op jit(solution)/shard_map/psum | solution.py:36
  110.1 15.3 %all-reduce.8 = (f32[1536]{0:T(1024)S(1)}, f32[1536]{0:T(1024)S(1)}) all-reduce(f32[1536]{0:T(1024)S(1)} %get-tuple-element.42, f32[1536]{0:T(1024)S(1)} %get-tuple-element.43), channel_id=1, replica_groups=mesh['batch_0'=8,'batch_1'=4,'space_0'=4,'space_1'=2] {'space_0'}, use_global_device_ids=true, to_apply=%region_18.19 | all-reduce | flops 3072 | bytes 24576 | tf_op jit(solution)/shard_map/psum | solution.py:36
  125.4 3.3 %all-reduce.16 = (f32[1536]{0:T(1024)S(1)}, f32[1536]{0:T(1024)S(1)}) all-reduce(f32[1536]{0:T(1024)S(1)} %get-tuple-element.34, f32[1536]{0:T(1024)S(1)} %get-tuple-element.35), channel_id=1, replica_groups=mesh['batch_0'=8,'batch_1'=4,'space_0'=4,'space_1'=2] {'space_1'}, use_global_device_ids=true, to_apply=%region_19.20 | all-reduce | flops 3072 | bytes 24576 | tf_op jit(solution)/shard_map/psum | solution.py:36
  128.7 0.0 copy-done.6
  128.8 0.0 copy-done.3
  128.8 0.0 copy-start.2
  128.8 3.3 %maximum_convert_fusion.2 = bf16[1,12,72,1536]{3,2,1,0:T(8,128)(2,1)S(1)} fusion(f32[1,12,72,1536]{3,2,1,0:T(8,128)} %bitcast.18, f32[1536]{0:T(1024)S(1)} %copy-done.3, f32[1536]{0:T(1024)S(1)} %get-tuple-element.74, f32[1536]{0:T(1024)S(1)} %get-tuple-element.73), kind=kLoop, calls=%fused_computation.10 | loop fusion | flops 6635520 | bytes 7981056 | tf_op jit(solution)/shard_map/convert_element_type | solution.py:63
  132.1 0.1 fusion.16
  132.2 2.2 collective-permute-start.2
  134.4 3.3 %collective-permute-start.3 = (bf16[1,2,72,1536]{3,2,1,0:T(8,128)(2,1)S(1)}, bf16[1,2,72,1536]{3,2,1,0:T(8,128)(2,1)S(1)}, u32[]{:S(2)}, u32[]{:S(2)}) collective-permute-start(bf16[1,2,72,1536]{3,2,1,0:T(8,128)(2,1)S(1)} %get-tuple-element.57), channel_id=1, source_target_pairs={{1,0},{2,1},{3,2},{4,3},{5,4},{6,5},{7,6},{9,8},{10,9},{11,10},{12... | collective-permute-start | bytes 1327112 | tf_op jit(solution)/shard_map/ppermute | solution.py:28
  137.8 0.0 copy-done.2
  137.8 0.1 convert_reduce_fusion.8
  137.9 3.9 %collective-permute-done.2 = bf16[1,2,72,1536]{3,2,1,0:T(8,128)(2,1)S(1)} collective-permute-done((bf16[1,2,72,1536]{3,2,1,0:T(8,128)(2,1)S(1)}, bf16[1,2,72,1536]{3,2,1,0:T(8,128)(2,1)S(1)}, u32[]{:S(2)}, u32[]{:S(2)}) %collective-permute-start.2) | collective-permute-done | bytes 442400 | tf_op jit(solution)/shard_map/ppermute | solution.py:26
  141.8 1.8 collective-permute-done.3
  143.6 1.7 fusion.6
  145.3 0.0 copy-start.7
  145.3 0.0 copy-start.4
  145.3 7.6 %fusion.13 = (f32[1536]{0:T(1024)S(1)}, f32[1536]{0:T(1024)S(1)}, f32[1,12,72,1536]{3,2,1,0:T(8,128)}) fusion(f32[1536]{0:T(1024)S(1)} %get-tuple-element.20, bf16[1,16,76,1536]{3,2,1,0:T(8,128)(2,1)S(1)} %fusion.6, f32[1536]{0:T(1024)S(1)} %get-tuple-element.21, bf16[1,2,72,1536]{3,2,1,0:T(8,128)(2,1)S(1)} %collective-permute-done.3, ...), kind=kLoop, calls=%fused_computation.57 | loop fusion | flops 41137152 | bytes 24840192 | tf_op jit(solution)/shard_map/reduce_sum | solution.py:56
  152.9 27.5 %all-reduce.3 = (f32[1536]{0:T(1024)S(1)}, f32[1536]{0:T(1024)S(1)}) all-reduce(f32[1536]{0:T(1024)S(1)} %get-tuple-element.8, f32[1536]{0:T(1024)S(1)} %get-tuple-element.7), channel_id=1, replica_groups=mesh['batch_0'=8,'batch_1'=4,'space_0'=4,'space_1'=2] {'batch_0'}, use_global_device_ids=true, to_apply=%region_26.27 | all-reduce | flops 3072 | bytes 24576 | tf_op jit(solution)/shard_map/psum | solution.py:36
  180.5 15.4 %all-reduce.11 = (f32[1536]{0:T(1024)S(1)}, f32[1536]{0:T(1024)S(1)}) all-reduce(f32[1536]{0:T(1024)S(1)} %get-tuple-element.24, f32[1536]{0:T(1024)S(1)} %get-tuple-element.25), channel_id=1, replica_groups=mesh['batch_0'=8,'batch_1'=4,'space_0'=4,'space_1'=2] {'batch_1'}, use_global_device_ids=true, to_apply=%region_27.28 | all-reduce | flops 3072 | bytes 24576 | tf_op jit(solution)/shard_map/psum | solution.py:36
  195.9 13.3 %all-reduce.7 = (f32[1536]{0:T(1024)S(1)}, f32[1536]{0:T(1024)S(1)}) all-reduce(f32[1536]{0:T(1024)S(1)} %get-tuple-element.40, f32[1536]{0:T(1024)S(1)} %get-tuple-element.41), channel_id=1, replica_groups=mesh['batch_0'=8,'batch_1'=4,'space_0'=4,'space_1'=2] {'space_0'}, use_global_device_ids=true, to_apply=%region_28.29 | all-reduce | flops 3072 | bytes 24576 | tf_op jit(solution)/shard_map/psum | solution.py:36
  209.2 3.3 %all-reduce.15 = (f32[1536]{0:T(1024)S(1)}, f32[1536]{0:T(1024)S(1)}) all-reduce(f32[1536]{0:T(1024)S(1)} %get-tuple-element.32, f32[1536]{0:T(1024)S(1)} %get-tuple-element.33), channel_id=1, replica_groups=mesh['batch_0'=8,'batch_1'=4,'space_0'=4,'space_1'=2] {'space_1'}, use_global_device_ids=true, to_apply=%region_29.30 | all-reduce | flops 3072 | bytes 24576 | tf_op jit(solution)/shard_map/psum | solution.py:36
  212.5 0.0 copy-done.7
  212.5 0.0 copy-done.4
  212.5 3.3 %maximum_convert_fusion.1 = bf16[1,12,72,1536]{3,2,1,0:T(8,128)(2,1)S(1)} fusion(f32[1,12,72,1536]{3,2,1,0:T(8,128)} %get-tuple-element.54, f32[1536]{0:T(1024)S(1)} %copy-done.4, f32[1536]{0:T(1024)S(1)} %get-tuple-element.72, f32[1536]{0:T(1024)S(1)} %get-tuple-element.71), kind=kLoop, calls=%fused_computation.7 | loop fusion | flops 6635520 | bytes 7981056 | tf_op jit(solution)/shard_map/convert_element_type | solution.py:63
  215.8 0.0 copy-start.8
  215.8 0.0 copy-start.5
  215.8 10.8 %fusion.12 = (f32[2048]{0:T(1024)S(1)}, f32[2048]{0:T(1024)S(1)}, f32[864,2048]{1,0:T(8,128)}) fusion(bf16[864,1536]{1,0:T(8,128)(2,1)S(1)} %bitcast.19, bf16[1536,2048]{1,0:T(8,128)(2,1)} %param.23), kind=kOutput, calls=%fused_computation.56 | convolution fusion | flops 5441122304 | bytes 16039936 | tf_op jit(solution)/shard_map/dot_general | solution.py:69
  226.6 27.0 %all-reduce.2 = (f32[2048]{0:T(1024)S(1)}, f32[2048]{0:T(1024)S(1)}) all-reduce(f32[2048]{0:T(1024)S(1)} %get-tuple-element.6, f32[2048]{0:T(1024)S(1)} %get-tuple-element.5), channel_id=1, replica_groups=mesh['batch_0'=8,'batch_1'=4,'space_0'=4,'space_1'=2] {'batch_0'}, use_global_device_ids=true, to_apply=%region_36.37 | all-reduce | flops 4096 | bytes 32768 | tf_op jit(solution)/shard_map/psum | solution.py:36
  253.7 14.3 %all-reduce.10 = (f32[2048]{0:T(1024)S(1)}, f32[2048]{0:T(1024)S(1)}) all-reduce(f32[2048]{0:T(1024)S(1)} %get-tuple-element.22, f32[2048]{0:T(1024)S(1)} %get-tuple-element.23), channel_id=1, replica_groups=mesh['batch_0'=8,'batch_1'=4,'space_0'=4,'space_1'=2] {'batch_1'}, use_global_device_ids=true, to_apply=%region_37.38 | all-reduce | flops 4096 | bytes 32768 | tf_op jit(solution)/shard_map/psum | solution.py:36
  268.0 16.4 %all-reduce.6 = (f32[2048]{0:T(1024)S(1)}, f32[2048]{0:T(1024)S(1)}) all-reduce(f32[2048]{0:T(1024)S(1)} %get-tuple-element.38, f32[2048]{0:T(1024)S(1)} %get-tuple-element.39), channel_id=1, replica_groups=mesh['batch_0'=8,'batch_1'=4,'space_0'=4,'space_1'=2] {'space_0'}, use_global_device_ids=true, to_apply=%region_38.39 | all-reduce | flops 4096 | bytes 32768 | tf_op jit(solution)/shard_map/psum | solution.py:36
  284.4 3.3 %all-reduce.14 = (f32[2048]{0:T(1024)S(1)}, f32[2048]{0:T(1024)S(1)}) all-reduce(f32[2048]{0:T(1024)S(1)} %get-tuple-element.30, f32[2048]{0:T(1024)S(1)} %get-tuple-element.31), channel_id=1, replica_groups=mesh['batch_0'=8,'batch_1'=4,'space_0'=4,'space_1'=2] {'space_1'}, use_global_device_ids=true, to_apply=%region_39.40 | all-reduce | flops 4096 | bytes 32768 | tf_op jit(solution)/shard_map/psum | solution.py:36
  287.7 0.0 copy-done.8
  287.7 0.0 copy-done.5
  287.7 6.0 %maximum_convert_fusion = bf16[1,12,72,2048]{3,2,1,0:T(8,128)(2,1)} fusion(f32[1,12,72,2048]{3,2,1,0:T(8,128)} %bitcast.17, f32[2048]{0:T(1024)S(1)} %copy-done.5, f32[2048]{0:T(1024)S(1)} %get-tuple-element.70, f32[2048]{0:T(1024)S(1)} %get-tuple-element.69), kind=kLoop, calls=%fused_computation.5 | loop fusion | flops 8847360 | bytes 10641408 | tf_op jit(solution)/shard_map/convert_element_type | solution.py:63
  (4 shorter events, 0.0 us)
Async XLA Ops:
  0.0 64.0 %copy-start = (bf16[1024,1536]{1,0:T(8,128)(2,1)S(1)}, bf16[1024,1536]{1,0:T(8,128)(2,1)}, u32[]{:S(2)}) copy-start(bf16[1024,1536]{1,0:T(8,128)(2,1)} %param.17) | copy-start | bytes 9437188
  0.0 13.5 %copy-start.1 = (bf16[1,12,72,1024]{3,2,1,0:T(8,128)(2,1)S(1)}, bf16[1,12,72,1024]{3,2,1,0:T(8,128)(2,1)}, u32[]{:S(2)}) copy-start(bf16[1,12,72,1024]{3,2,1,0:T(8,128)(2,1)} %param.13) | copy-start | bytes 5308420
  1.3 8.2 %collective-permute-start = (bf16[1,2,72,1024]{3,2,1,0:T(8,128)(2,1)S(1)}, bf16[1,2,72,1024]{3,2,1,0:T(8,128)(2,1)S(1)}, u32[]{:S(2)}, u32[]{:S(2)}) collective-permute-start(bf16[1,2,72,1024]{3,2,1,0:T(8,128)(2,1)S(1)} %get-tuple-element.58), channel_id=1, source_target_pairs={{0,1},{1,2},{2,3},{3,4},{4,5},{5,6},{6,7},{8,9},{9,10},{10,11},{11... | collective-permute-start | bytes 884744 | tf_op jit(solution)/shard_map/ppermute | solution.py:26
  3.3 7.9 %collective-permute-start.1 = (bf16[1,2,72,1024]{3,2,1,0:T(8,128)(2,1)S(1)}, bf16[1,2,72,1024]{3,2,1,0:T(8,128)(2,1)S(1)}, u32[]{:S(2)}, u32[]{:S(2)}) collective-permute-start(bf16[1,2,72,1024]{3,2,1,0:T(8,128)(2,1)S(1)} %get-tuple-element.59), channel_id=1, source_target_pairs={{1,0},{2,1},{3,2},{4,3},{5,4},{6,5},{7,6},{9,8},{10,9},{11,10},{12... | collective-permute-start | bytes 884744 | tf_op jit(solution)/shard_map/ppermute | solution.py:28
  13.5 47.8 %copy-start.10 = (f32[1024]{0:T(1024)S(1)}, f32[1024]{0:T(1024)}, u32[]{:S(2)}) copy-start(f32[1024]{0:T(1024)} %param.15) | copy-start | bytes 12292
  13.6 47.9 %copy-start.9 = (f32[1024]{0:T(1024)S(1)}, f32[1024]{0:T(1024)}, u32[]{:S(2)}) copy-start(f32[1024]{0:T(1024)} %param.16) | copy-start | bytes 12292
  64.0 64.7 %copy-start.6 = (f32[1536]{0:T(1024)S(1)}, f32[1536]{0:T(1024)}, u32[]{:S(2)}) copy-start(f32[1536]{0:T(1024)} %param.18) | copy-start | bytes 18436
  64.0 64.7 %copy-start.3 = (f32[1536]{0:T(1024)S(1)}, f32[1536]{0:T(1024)}, u32[]{:S(2)}) copy-start(f32[1536]{0:T(1024)} %param.19) | copy-start | bytes 18436
  128.8 9.0 %copy-start.2 = (bf16[3,3,1536]{2,1,0:T(4,128)(2,1)S(1)}, bf16[3,3,1536]{2,1,0:T(4,128)(2,1)}, u32[]{:S(2)}) copy-start(bf16[3,3,1536]{2,1,0:T(4,128)(2,1)} %param.20) | copy-start | bytes 82948
  132.2 9.6 %collective-permute-start.2 = (bf16[1,2,72,1536]{3,2,1,0:T(8,128)(2,1)S(1)}, bf16[1,2,72,1536]{3,2,1,0:T(8,128)(2,1)S(1)}, u32[]{:S(2)}, u32[]{:S(2)}) collective-permute-start(bf16[1,2,72,1536]{3,2,1,0:T(8,128)(2,1)S(1)} %get-tuple-element.56), channel_id=1, source_target_pairs={{0,1},{1,2},{2,3},{3,4},{4,5},{5,6},{6,7},{8,9},{9,10},{10,11},{11... | collective-permute-start | bytes 1327112 | tf_op jit(solution)/shard_map/ppermute | solution.py:26
  134.4 9.1 %collective-permute-start.3 = (bf16[1,2,72,1536]{3,2,1,0:T(8,128)(2,1)S(1)}, bf16[1,2,72,1536]{3,2,1,0:T(8,128)(2,1)S(1)}, u32[]{:S(2)}, u32[]{:S(2)}) collective-permute-start(bf16[1,2,72,1536]{3,2,1,0:T(8,128)(2,1)S(1)} %get-tuple-element.57), channel_id=1, source_target_pairs={{1,0},{2,1},{3,2},{4,3},{5,4},{6,5},{7,6},{9,8},{10,9},{11,10},{12... | collective-permute-start | bytes 1327112 | tf_op jit(solution)/shard_map/ppermute | solution.py:28
  145.3 67.2 %copy-start.7 = (f32[1536]{0:T(1024)S(1)}, f32[1536]{0:T(1024)}, u32[]{:S(2)}) copy-start(f32[1536]{0:T(1024)} %param.21) | copy-start | bytes 18436
  145.3 67.2 %copy-start.4 = (f32[1536]{0:T(1024)S(1)}, f32[1536]{0:T(1024)}, u32[]{:S(2)}) copy-start(f32[1536]{0:T(1024)} %param.22) | copy-start | bytes 18436
  215.8 71.9 %copy-start.8 = (f32[2048]{0:T(1024)S(1)}, f32[2048]{0:T(1024)}, u32[]{:S(2)}) copy-start(f32[2048]{0:T(1024)} %param.24) | copy-start | bytes 24580
  215.8 71.9 %copy-start.5 = (f32[2048]{0:T(1024)S(1)}, f32[2048]{0:T(1024)}, u32[]{:S(2)}) copy-start(f32[2048]{0:T(1024)} %param.25) | copy-start | bytes 24580
where the time goes:
time: 297 us; the launch traced here: 294 us
  blocking collectives  223 us (75%)
  other arithmetic  33.4 us (11%)
  matrix products  15.5 us (5%)
  starting transfers between devices  11.3 us (4%)
  waiting for transfers between devices  8.96 us (3%)
    psum x16, blocking collectives, one_axis_at_a_time(): return functools.reduce(lax.psum, axes, value)  223 us
    dot_general x2, matrix products, project(): result = jnp.dot(flat, weight, preferred_element_type=jnp.float32)  15.5 us
    convert_element_type x4, other arithmetic, scaled(): jnp.maximum((values - average) * factor + offset, 0.0).astype(jnp.bfloat16)  15.2 us
    reduce_sum x2, other arithmetic, local_sums(): jnp.sum(values, axis=(0, 1, 2))  13.1 us
    ppermute x2, starting transfers between devices, padded_2(): lax.ppermute(head, axis, [((i + 1) % count, i) for i in range(ends)])  6.96 us
  transfers between devices with their start and end apart: 4, of which 4 were waited for; matrix products, arithmetic and copies ran while one was open for 0% of the time, Pallas kernels for 0%

commit v1 on v0

--- a/solution.py
+++ b/solution.py
@@ -1,5 +1,3 @@
-import functools
-
 import jax
 import jax.numpy as jnp
 from jax import lax
@@ -9,7 +7,6 @@
 RATE = 2
 BATCH = ("batch_0", "batch_1")
 SPACE = ("space_0", "space_1")
-BATCH_SPACE = ("batch_0", "batch_1", "space_0", "space_1")
 
 
 epsilon = 1e-05
@@ -32,8 +29,18 @@
     return cells
 
 
-def one_axis_at_a_time(value, axes):
-    return functools.reduce(lax.psum, axes, value)
+def shared_over(value, axes):
+    count = lax.axis_size(axes)
+    copies = jnp.broadcast_to(value[None], (count,) + value.shape)
+    return jnp.sum(lax.all_to_all(copies, axes, 0, 0), axis=0)
+
+
+def global_sums(parts):
+    value = jnp.stack(parts).reshape(-1, 128)
+    value = value + lax.ppermute(value, "space_1", [(0, 1), (1, 0)])
+    value = shared_over(value, ("batch_1", "space_0"))
+    value = shared_over(value, ("batch_0",))
+    return value.reshape(2, -1)
 
 
 def dilated_padded(padded, weight, span_rows, span_cols):
@@ -93,18 +100,18 @@
     padded = padded_2(features, ((SPACE, 1),), RATE)
     padded = jnp.pad(padded, ((0, 0), (0, 0), (RATE, RATE), (0, 0)))
     first = dilated_padded(padded, depth_one, span_rows, span_cols)
-    totals = jax.tree.map(lambda part: one_axis_at_a_time(part, BATCH_SPACE), local_sums(first))
+    totals = global_sums(local_sums(first))
     act_one = scaled(first, totals, all_pixels, gain_one, shift_one)
     second = project(act_one, point_one)
-    totals = jax.tree.map(lambda part: one_axis_at_a_time(part, BATCH_SPACE), local_sums(second))
+    totals = global_sums(local_sums(second))
     act_two = scaled(second, totals, all_pixels, gain_two, shift_two)
     padded = padded_2(act_two, ((SPACE, 1),), RATE)
     padded = jnp.pad(padded, ((0, 0), (0, 0), (RATE, RATE), (0, 0)))
     third = dilated_padded(padded, depth_two, span_rows, span_cols)
-    totals = jax.tree.map(lambda part: one_axis_at_a_time(part, BATCH_SPACE), local_sums(third))
+    totals = global_sums(local_sums(third))
     act_three = scaled(third, totals, all_pixels, gain_three, shift_three)
     fourth = project(act_three, point_two)
-    totals = jax.tree.map(lambda part: one_axis_at_a_time(part, BATCH_SPACE), local_sums(fourth))
+    totals = global_sums(local_sums(fourth))
     return scaled(fourth, totals, all_pixels, gain_four, shift_four)
 
 

time: 297 us -> 179 us (0.60)
  blocking collectives: 223 us -> 99.6 us
  waiting for transfers between devices: 8.96 us -> 13 us
    psum x16 -> x0, blocking collectives: 223 us -> none  [one_axis_at_a_time(): return functools.reduce(lax.psum, axes, value)]
    all_to_all x0 -> x8, blocking collectives: none -> 99.6 us  [shared_over(): return jnp.sum(lax.all_to_all(copies, axes, 0, 0), axis=0)]
    ppermute x0 -> x4, waiting for transfers between devices: none -> 4 us  [global_sums(): value = value + lax.ppermute(value, 'space_1', [(0, 1), (1, 0)])]
  transfers between devices with their start and end apart: 4 -> 8, of which waited for: 4 -> 8; matrix products, arithmetic and copies ran while one was open for 0% -> 1% of each run, Pallas kernels for 0% -> 0%
where the time goes in v1:
time: 179 us; the launch traced here: 178 us
  blocking collectives  99.6 us (56%)
  other arithmetic  33.7 us (19%)
  matrix products  15.5 us (9%)
  starting transfers between devices  14.1 us (8%)
  waiting for transfers between devices  13 us (7%)
    all_to_all x8, blocking collectives, shared_over(): return jnp.sum(lax.all_to_all(copies, axes, 0, 0), axis=0)  99.6 us
    dot_general x2, matrix products, project(): result = jnp.dot(flat, weight, preferred_element_type=jnp.float32)  15.5 us
    convert_element_type x4, other arithmetic, scaled(): jnp.maximum((values - average) * factor + offset, 0.0).astype(jnp.bfloat16)  15.2 us
    reduce_sum x2, other arithmetic, local_sums(): jnp.sum(values, axis=(0, 1, 2))  13.1 us
    ppermute x2, starting transfers between devices, padded_2(): lax.ppermute(head, axis, [((i + 1) % count, i) for i in range(ends)])  7.28 us
    ppermute x2, waiting for transfers between devices, padded_2(): lax.ppermute(tail, axis, [(i, (i + 1) % count) for i in range(ends)])  5.45 us
    concatenate x2, other arithmetic, padded_2(): jnp.concatenate([lax.ppermute(tail, axis, [(i, (i + 1) % count) for i in...  4.05 us
    ppermute x4, waiting for transfers between devices, global_sums(): value = value + lax.ppermute(value, 'space_1', [(0, 1), (1, 0)])  4 us
  transfers between devices with their start and end apart: 8, of which 8 were waited for; matrix products, arithmetic and copies ran while one was open for 1% of the time, Pallas kernels for 0%

profile of v1, /device:TPU:2, one launch (start us, length us, event | category | flops | bytes accessed | tf_op | source)
XLA Modules:
  0.0 177.9 jit_solution(17664080650732403883)
XLA Ops:
  0.0 0.0 copy-start
  0.0 0.0 copy-start.1
  0.0 1.2 fusion.41
  1.3 2.1 %collective-permute-start = (bf16[1,2,72,1024]{3,2,1,0:T(8,128)(2,1)S(1)}, bf16[1,2,72,1024]{3,2,1,0:T(8,128)(2,1)S(1)}, u32[]{:S(2)}, u32[]{:S(2)}) collective-permute-start(bf16[1,2,72,1024]{3,2,1,0:T(8,128)(2,1)S(1)} %get-tuple-element.26), channel_id=1, source_target_pairs={{0,1},{1,2},{2,3},{3,4},{4,5},{5,6},{6,7},{8,9},{9,10},{10,11},{11... | collective-permute-start | bytes 884744 | tf_op jit(solution)/shard_map/ppermute | solution.py:23
  3.3 3.6 %collective-permute-start.1 = (bf16[1,2,72,1024]{3,2,1,0:T(8,128)(2,1)S(1)}, bf16[1,2,72,1024]{3,2,1,0:T(8,128)(2,1)S(1)}, u32[]{:S(2)}, u32[]{:S(2)}) collective-permute-start(bf16[1,2,72,1024]{3,2,1,0:T(8,128)(2,1)S(1)} %get-tuple-element.27), channel_id=1, source_target_pairs={{1,0},{2,1},{3,2},{4,3},{5,4},{6,5},{7,6},{9,8},{10,9},{11,10},{12... | collective-permute-start | bytes 884744 | tf_op jit(solution)/shard_map/ppermute | solution.py:25
  7.0 0.9 slice_convert_fusion.8
  7.9 1.6 collective-permute-done
  9.4 1.8 collective-permute-done.1
  11.2 2.3 %fusion.11 = bf16[1,16,76,1024]{3,2,1,0:T(8,128)(2,1)S(1)} fusion(bf16[1,2,72,1024]{3,2,1,0:T(8,128)(2,1)S(1)} %collective-permute-done.1, bf16[1,12,72,1024]{3,2,1,0:T(8,128)(2,1)} %param.13, bf16[1,2,72,1024]{3,2,1,0:T(8,128)(2,1)S(1)} %collective-permute-done), kind=kLoop, calls=%fused_computation.27 | loop fusion | flops 14942208 | bytes 4849664 | tf_op jit(solution)/shard_map/concatenate | solution.py:21
  13.5 0.0 copy-done.1
  13.5 0.0 copy-start.10
  13.6 0.0 copy-start.9
  13.6 5.5 %fusion.39 = (f32[1024]{0:T(1024)S(1)}, f32[1024]{0:T(1024)S(1)}, f32[1,12,72,1024]{3,2,1,0:T(8,128)}) fusion(f32[1024]{0:T(1024)S(1)} %bitcast.88, bf16[1,16,76,1024]{3,2,1,0:T(8,128)(2,1)S(1)} %fusion.11, f32[1024]{0:T(1024)S(1)} %bitcast.89, bf16[1,2,72,1024]{3,2,1,0:T(8,128)(2,1)S(1)} %collective-permute-done.1, ...), kind=kLoop, calls=%fused_computation.87 | loop fusion | flops 27424768 | bytes 16560128 | tf_op jit(solution)/shard_map/reduce_sum | solution.py:63
  19.1 1.9 %collective-permute-start.2 = (f32[16,128]{1,0:T(8,128)S(1)}, f32[16,128]{1,0:T(8,128)S(1)}, u32[]{:S(2)}, u32[]{:S(2)}) collective-permute-start(f32[16,128]{1,0:T(8,128)S(1)} %reshape.355), channel_id=1, source_target_pairs={{0,1},{1,0},{2,3},{3,2},{4,5},{5,4},{6,7},{7,6},{8,9},{9,8},{10,11... | collective-permute-start | bytes 24584 | tf_op jit(solution)/shard_map/ppermute | solution.py:40
  20.9 0.8 collective-permute-done.2
  21.8 13.6 %all_to_all.40 = f32[16,16,128]{2,1,0:T(8,128)S(1)} all-to-all(f32[16,16,128]{2,1,0:T(8,128)S(1)} %broadcast_in_dim.16), channel_id=1, replica_groups=mesh['batch_0'=8,'batch_1'=4,'space_0'=4,'space_1'=2] {'batch_1','space_0'}, dimensions={0} | all-to-all | bytes 262144 | tf_op jit(solution)/shard_map/all_to_all | solution.py:35
  35.4 16.6 %all_to_all.41 = f32[8,16,128]{2,1,0:T(8,128)S(1)} all-to-all(f32[8,16,128]{2,1,0:T(8,128)S(1)} %broadcast_in_dim.17), channel_id=1, replica_groups=mesh['batch_0'=8,'batch_1'=4,'space_0'=4,'space_1'=2] {'batch_0'}, dimensions={0} | all-to-all | bytes 131072 | tf_op jit(solution)/shard_map/all_to_all | solution.py:35
  52.1 0.0 copy-done.10
  52.1 0.0 copy-done.9
  52.1 2.6 %maximum_convert_fusion.3 = bf16[1,12,72,1024]{3,2,1,0:T(8,128)(2,1)S(1)} fusion(f32[1,12,72,1024]{3,2,1,0:T(8,128)} %get-tuple-element.23, f32[1024]{0:T(1024)S(1)} %copy-done.9, f32[1024]{0:T(1024)S(1)} %fusion.34, f32[1024]{0:T(1024)S(1)} %fusion.35), kind=kLoop, calls=%fused_computation.18 | loop fusion | flops 4423680 | bytes 5320704 | tf_op jit(solution)/shard_map/convert_element_type | solution.py:70
  54.7 0.0 copy-done
  54.7 0.0 copy-start.6
  54.7 0.0 copy-start.3
  54.7 4.7 %fusion.38 = (f32[1536]{0:T(1024)S(1)}, f32[1536]{0:T(1024)S(1)}, f32[864,1536]{1,0:T(8,128)}) fusion(bf16[864,1024]{1,0:T(8,128)(2,1)S(1)} %bitcast.80, bf16[1024,1536]{1,0:T(8,128)(2,1)S(1)} %copy-done), kind=kOutput, calls=%fused_computation.86 | convolution fusion | flops 2721887232 | bytes 10235904 | tf_op jit(solution)/shard_map/dot_general | solution.py:76
  59.5 0.1 collective-permute-start.3
  59.6 1.2 collective-permute-done.3
  60.8 11.4 %all_to_all.42 = f32[16,24,128]{2,1,0:T(8,128)S(1)} all-to-all(f32[16,24,128]{2,1,0:T(8,128)S(1)} %broadcast_in_dim.18), channel_id=1, replica_groups=mesh['batch_0'=8,'batch_1'=4,'space_0'=4,'space_1'=2] {'batch_1','space_0'}, dimensions={0} | all-to-all | bytes 393216 | tf_op jit(solution)/shard_map/all_to_all | solution.py:35
  72.3 11.1 %all_to_all.43 = f32[8,24,128]{2,1,0:T(8,128)S(1)} all-to-all(f32[8,24,128]{2,1,0:T(8,128)S(1)} %broadcast_in_dim.19), channel_id=1, replica_groups=mesh['batch_0'=8,'batch_1'=4,'space_0'=4,'space_1'=2] {'batch_0'}, dimensions={0} | all-to-all | bytes 196608 | tf_op jit(solution)/shard_map/all_to_all | solution.py:35
  83.4 0.0 copy-done.6
  83.4 0.0 copy-done.3
  83.5 0.0 copy-start.2
  83.5 3.3 %maximum_convert_fusion.2 = bf16[1,12,72,1536]{3,2,1,0:T(8,128)(2,1)S(1)} fusion(f32[1,12,72,1536]{3,2,1,0:T(8,128)} %bitcast.78, f32[1536]{0:T(1024)S(1)} %copy-done.3, f32[1536]{0:T(1024)S(1)} %fusion.28, f32[1536]{0:T(1024)S(1)} %fusion.29), kind=kLoop, calls=%fused_computation.10 | loop fusion | flops 6635520 | bytes 7981056 | tf_op jit(solution)/shard_map/convert_element_type | solution.py:70
  86.8 0.1 fusion.40
  86.9 1.9 %collective-permute-start.4 = (bf16[1,2,72,1536]{3,2,1,0:T(8,128)(2,1)S(1)}, bf16[1,2,72,1536]{3,2,1,0:T(8,128)(2,1)S(1)}, u32[]{:S(2)}, u32[]{:S(2)}) collective-permute-start(bf16[1,2,72,1536]{3,2,1,0:T(8,128)(2,1)S(1)} %get-tuple-element.24), channel_id=1, source_target_pairs={{0,1},{1,2},{2,3},{3,4},{4,5},{5,6},{6,7},{8,9},{9,10},{10,11},{11... | collective-permute-start | bytes 1327112 | tf_op jit(solution)/shard_map/ppermute | solution.py:23
  88.8 3.6 %collective-permute-start.5 = (bf16[1,2,72,1536]{3,2,1,0:T(8,128)(2,1)S(1)}, bf16[1,2,72,1536]{3,2,1,0:T(8,128)(2,1)S(1)}, u32[]{:S(2)}, u32[]{:S(2)}) collective-permute-start(bf16[1,2,72,1536]{3,2,1,0:T(8,128)(2,1)S(1)} %get-tuple-element.25), channel_id=1, source_target_pairs={{1,0},{2,1},{3,2},{4,3},{5,4},{6,5},{7,6},{9,8},{10,9},{11,10},{12... | collective-permute-start | bytes 1327112 | tf_op jit(solution)/shard_map/ppermute | solution.py:25
  92.4 0.0 copy-done.2
  92.5 0.1 convert_reduce_fusion.8
  92.6 3.9 %collective-permute-done.4 = bf16[1,2,72,1536]{3,2,1,0:T(8,128)(2,1)S(1)} collective-permute-done((bf16[1,2,72,1536]{3,2,1,0:T(8,128)(2,1)S(1)}, bf16[1,2,72,1536]{3,2,1,0:T(8,128)(2,1)S(1)}, u32[]{:S(2)}, u32[]{:S(2)}) %collective-permute-start.4) | collective-permute-done | bytes 442400 | tf_op jit(solution)/shard_map/ppermute | solution.py:23
  96.5 1.8 collective-permute-done.5
  98.2 1.7 fusion.6
  100.0 0.0 copy-start.7
  100.0 0.0 copy-start.4
  100.0 7.6 %fusion.37 = (f32[1536]{0:T(1024)S(1)}, f32[1536]{0:T(1024)S(1)}, f32[1,12,72,1536]{3,2,1,0:T(8,128)}) fusion(f32[1536]{0:T(1024)S(1)} %get-tuple-element.20, bf16[1,16,76,1536]{3,2,1,0:T(8,128)(2,1)S(1)} %fusion.6, f32[1536]{0:T(1024)S(1)} %get-tuple-element.21, bf16[1,2,72,1536]{3,2,1,0:T(8,128)(2,1)S(1)} %collective-permute-done.5, ...), kind=kLoop, calls=%fused_computation.85 | loop fusion | flops 41137152 | bytes 24840192 | tf_op jit(solution)/shard_map/reduce_sum | solution.py:63
  107.7 0.8 collective-permute-start.6
  108.5 0.8 collective-permute-done.6
  109.4 12.3 %all_to_all.44 = f32[16,24,128]{2,1,0:T(8,128)S(1)} all-to-all(f32[16,24,128]{2,1,0:T(8,128)S(1)} %broadcast_in_dim.20), channel_id=1, replica_groups=mesh['batch_0'=8,'batch_1'=4,'space_0'=4,'space_1'=2] {'batch_1','space_0'}, dimensions={0} | all-to-all | bytes 393216 | tf_op jit(solution)/shard_map/all_to_all | solution.py:35
  121.7 11.1 %all_to_all.45 = f32[8,24,128]{2,1,0:T(8,128)S(1)} all-to-all(f32[8,24,128]{2,1,0:T(8,128)S(1)} %broadcast_in_dim.21), channel_id=1, replica_groups=mesh['batch_0'=8,'batch_1'=4,'space_0'=4,'space_1'=2] {'batch_0'}, dimensions={0} | all-to-all | bytes 196608 | tf_op jit(solution)/shard_map/all_to_all | solution.py:35
  132.8 0.0 copy-done.7
  132.9 0.0 copy-done.4
  132.9 3.3 %maximum_convert_fusion.1 = bf16[1,12,72,1536]{3,2,1,0:T(8,128)(2,1)S(1)} fusion(f32[1,12,72,1536]{3,2,1,0:T(8,128)} %get-tuple-element.22, f32[1536]{0:T(1024)S(1)} %copy-done.4, f32[1536]{0:T(1024)S(1)} %fusion.22, f32[1536]{0:T(1024)S(1)} %fusion.23), kind=kLoop, calls=%fused_computation.7 | loop fusion | flops 6635520 | bytes 7981056 | tf_op jit(solution)/shard_map/convert_element_type | solution.py:70
  136.2 0.0 copy-start.8
  136.2 0.0 copy-start.5
  136.2 10.8 %fusion.36 = (f32[2048]{0:T(1024)S(1)}, f32[2048]{0:T(1024)S(1)}, f32[864,2048]{1,0:T(8,128)}) fusion(bf16[864,1536]{1,0:T(8,128)(2,1)S(1)} %bitcast.79, bf16[1536,2048]{1,0:T(8,128)(2,1)} %param.23), kind=kOutput, calls=%fused_computation.84 | convolution fusion | flops 5441122304 | bytes 16039936 | tf_op jit(solution)/shard_map/dot_general | solution.py:76
  147.0 0.1 collective-permute-start.7
  147.1 1.2 collective-permute-done.7
  148.3 12.0 %all_to_all.46 = f32[16,32,128]{2,1,0:T(8,128)S(1)} all-to-all(f32[16,32,128]{2,1,0:T(8,128)S(1)} %broadcast_in_dim.22), channel_id=1, replica_groups=mesh['batch_0'=8,'batch_1'=4,'space_0'=4,'space_1'=2] {'batch_1','space_0'}, dimensions={0} | all-to-all | bytes 524288 | tf_op jit(solution)/shard_map/all_to_all | solution.py:35
  160.4 11.5 %all_to_all.47 = f32[8,32,128]{2,1,0:T(8,128)S(1)} all-to-all(f32[8,32,128]{2,1,0:T(8,128)S(1)} %broadcast_in_dim.23), channel_id=1, replica_groups=mesh['batch_0'=8,'batch_1'=4,'space_0'=4,'space_1'=2] {'batch_0'}, dimensions={0} | all-to-all | bytes 262144 | tf_op jit(solution)/shard_map/all_to_all | solution.py:35
  171.9 0.0 copy-done.8
  171.9 0.0 copy-done.5
  171.9 6.0 %maximum_convert_fusion = bf16[1,12,72,2048]{3,2,1,0:T(8,128)(2,1)} fusion(f32[1,12,72,2048]{3,2,1,0:T(8,128)} %bitcast.77, f32[2048]{0:T(1024)S(1)} %copy-done.5, f32[2048]{0:T(1024)S(1)} %fusion.16, f32[2048]{0:T(1024)S(1)} %fusion.17), kind=kLoop, calls=%fused_computation.5 | loop fusion | flops 8847360 | bytes 10641408 | tf_op jit(solution)/shard_map/convert_element_type | solution.py:70
  (40 shorter events, 0.4 us)
Async XLA Ops:
  0.0 54.7 %copy-start = (bf16[1024,1536]{1,0:T(8,128)(2,1)S(1)}, bf16[1024,1536]{1,0:T(8,128)(2,1)}, u32[]{:S(2)}) copy-start(bf16[1024,1536]{1,0:T(8,128)(2,1)} %param.17) | copy-start | bytes 9437188
  0.0 13.5 %copy-start.1 = (bf16[1,12,72,1024]{3,2,1,0:T(8,128)(2,1)S(1)}, bf16[1,12,72,1024]{3,2,1,0:T(8,128)(2,1)}, u32[]{:S(2)}) copy-start(bf16[1,12,72,1024]{3,2,1,0:T(8,128)(2,1)} %param.13) | copy-start | bytes 5308420
  1.3 8.2 %collective-permute-start = (bf16[1,2,72,1024]{3,2,1,0:T(8,128)(2,1)S(1)}, bf16[1,2,72,1024]{3,2,1,0:T(8,128)(2,1)S(1)}, u32[]{:S(2)}, u32[]{:S(2)}) collective-permute-start(bf16[1,2,72,1024]{3,2,1,0:T(8,128)(2,1)S(1)} %get-tuple-element.26), channel_id=1, source_target_pairs={{0,1},{1,2},{2,3},{3,4},{4,5},{5,6},{6,7},{8,9},{9,10},{10,11},{11... | collective-permute-start | bytes 884744 | tf_op jit(solution)/shard_map/ppermute | solution.py:23
  3.3 7.9 %collective-permute-start.1 = (bf16[1,2,72,1024]{3,2,1,0:T(8,128)(2,1)S(1)}, bf16[1,2,72,1024]{3,2,1,0:T(8,128)(2,1)S(1)}, u32[]{:S(2)}, u32[]{:S(2)}) collective-permute-start(bf16[1,2,72,1024]{3,2,1,0:T(8,128)(2,1)S(1)} %get-tuple-element.27), channel_id=1, source_target_pairs={{1,0},{2,1},{3,2},{4,3},{5,4},{6,5},{7,6},{9,8},{10,9},{11,10},{12... | collective-permute-start | bytes 884744 | tf_op jit(solution)/shard_map/ppermute | solution.py:25
  13.5 38.5 %copy-start.10 = (f32[1024]{0:T(1024)S(1)}, f32[1024]{0:T(1024)}, u32[]{:S(2)}) copy-start(f32[1024]{0:T(1024)} %param.15) | copy-start | bytes 12292
  13.6 38.6 %copy-start.9 = (f32[1024]{0:T(1024)S(1)}, f32[1024]{0:T(1024)}, u32[]{:S(2)}) copy-start(f32[1024]{0:T(1024)} %param.16) | copy-start | bytes 12292
  19.1 2.7 %collective-permute-start.2 = (f32[16,128]{1,0:T(8,128)S(1)}, f32[16,128]{1,0:T(8,128)S(1)}, u32[]{:S(2)}, u32[]{:S(2)}) collective-permute-start(f32[16,128]{1,0:T(8,128)S(1)} %reshape.355), channel_id=1, source_target_pairs={{0,1},{1,0},{2,3},{3,2},{4,5},{5,4},{6,7},{7,6},{8,9},{9,8},{10,11... | collective-permute-start | bytes 24584 | tf_op jit(solution)/shard_map/ppermute | solution.py:40
  54.7 28.7 %copy-start.6 = (f32[1536]{0:T(1024)S(1)}, f32[1536]{0:T(1024)}, u32[]{:S(2)}) copy-start(f32[1536]{0:T(1024)} %param.18) | copy-start | bytes 18436
  54.7 28.7 %copy-start.3 = (f32[1536]{0:T(1024)S(1)}, f32[1536]{0:T(1024)}, u32[]{:S(2)}) copy-start(f32[1536]{0:T(1024)} %param.19) | copy-start | bytes 18436
  59.5 1.3 collective-permute-start.3
  83.5 9.0 %copy-start.2 = (bf16[3,3,1536]{2,1,0:T(4,128)(2,1)S(1)}, bf16[3,3,1536]{2,1,0:T(4,128)(2,1)}, u32[]{:S(2)}) copy-start(bf16[3,3,1536]{2,1,0:T(4,128)(2,1)} %param.20) | copy-start | bytes 82948
  86.9 9.6 %collective-permute-start.4 = (bf16[1,2,72,1536]{3,2,1,0:T(8,128)(2,1)S(1)}, bf16[1,2,72,1536]{3,2,1,0:T(8,128)(2,1)S(1)}, u32[]{:S(2)}, u32[]{:S(2)}) collective-permute-start(bf16[1,2,72,1536]{3,2,1,0:T(8,128)(2,1)S(1)} %get-tuple-element.24), channel_id=1, source_target_pairs={{0,1},{1,2},{2,3},{3,4},{4,5},{5,6},{6,7},{8,9},{9,10},{10,11},{11... | collective-permute-start | bytes 1327112 | tf_op jit(solution)/shard_map/ppermute | solution.py:23
  88.8 9.4 %collective-permute-start.5 = (bf16[1,2,72,1536]{3,2,1,0:T(8,128)(2,1)S(1)}, bf16[1,2,72,1536]{3,2,1,0:T(8,128)(2,1)S(1)}, u32[]{:S(2)}, u32[]{:S(2)}) collective-permute-start(bf16[1,2,72,1536]{3,2,1,0:T(8,128)(2,1)S(1)} %get-tuple-element.25), channel_id=1, source_target_pairs={{1,0},{2,1},{3,2},{4,3},{5,4},{6,5},{7,6},{9,8},{10,9},{11,10},{12... | collective-permute-start | bytes 1327112 | tf_op jit(solution)/shard_map/ppermute | solution.py:25
  100.0 32.9 %copy-start.7 = (f32[1536]{0:T(1024)S(1)}, f32[1536]{0:T(1024)}, u32[]{:S(2)}) copy-start(f32[1536]{0:T(1024)} %param.21) | copy-start | bytes 18436
  100.0 32.9 %copy-start.4 = (f32[1536]{0:T(1024)S(1)}, f32[1536]{0:T(1024)}, u32[]{:S(2)}) copy-start(f32[1536]{0:T(1024)} %param.22) | copy-start | bytes 18436
  107.7 1.7 collective-permute-start.6
  136.2 35.7 %copy-start.8 = (f32[2048]{0:T(1024)S(1)}, f32[2048]{0:T(1024)}, u32[]{:S(2)}) copy-start(f32[2048]{0:T(1024)} %param.24) | copy-start | bytes 24580
  136.2 35.7 %copy-start.5 = (f32[2048]{0:T(1024)S(1)}, f32[2048]{0:T(1024)}, u32[]{:S(2)}) copy-start(f32[2048]{0:T(1024)} %param.25) | copy-start | bytes 24580
  147.0 1.3 collective-permute-start.7

commit v2 on v0

v2 whole, which is shorter than its diff:
```python
import functools

import jax
import jax.numpy as jnp
from jax import lax
from jax.experimental import pallas as pl
from jax.experimental.pallas import tpu as pltpu
from jax.sharding import Mesh
from jax.sharding import PartitionSpec as P

RATE = 2
LANES = 128
BATCH = ("batch_0", "batch_1")
SPACE = ("space_0", "space_1")

epsilon = 1e-05

VMEM = pl.BlockSpec(memory_space=pltpu.VMEM)
HBM = pl.BlockSpec(memory_space=pltpu.HBM)


def kernel_call(body, outs, n_in, limit, scratch=(), flops=0, moved=0):
    return pl.pallas_call(
        body,
        out_shape=[pltpu.VMEM(shape, dtype) for shape, dtype in outs],
        in_specs=[VMEM] * n_in,
        out_specs=[VMEM] * len(outs),
        scratch_shapes=list(scratch),
        compiler_params=pltpu.CompilerParams(vmem_limit_bytes=limit),
        cost_estimate=pl.CostEstimate(flops=flops, bytes_accessed=moved, transcendentals=0),
    )


def moved_down(row):
    gap = jnp.zeros((RATE, row.shape[1]), row.dtype)
    return jnp.concatenate([gap, row[: row.shape[0] - RATE]], axis=0)


def moved_up(row):
    gap = jnp.zeros((RATE, row.shape[1]), row.dtype)
    return jnp.concatenate([row[RATE:], gap], axis=0)


def taps_of(filter_ref, lanes):
    return [filter_ref[tap, :, lanes].astype(jnp.float32) for tap in range(3)]


def dilated_row(rows, taps):
    sides = []
    for tap_col in range(3):
        side = None
        for tap_row in range(3):
            term = rows[tap_row] * taps[tap_row][tap_col : tap_col + 1]
            side = term if side is None else side + term
        sides.append(side)
    return sides[1] + moved_down(sides[0]) + moved_up(sides[2])


def summed_rows(value):
    return jnp.sum(value.reshape(value.shape[0] // 8, 8, value.shape[1]), axis=0)


def store_sums(sums_ref, lanes, total, squares):
    sums_ref[0:1, lanes] = jnp.sum(total, axis=0, keepdims=True)
    sums_ref[1:2, lanes] = jnp.sum(squares, axis=0, keepdims=True)


def dilated_rows(row_at, rows, taps, out_ref, lanes):
    total = squares = None
    for place, row in enumerate(rows):
        value = dilated_row([row_at(row - RATE), row_at(row), row_at(row + RATE)], taps)
        out_ref[place, :, lanes] = value
        part, part_squares = summed_rows(value), summed_rows(value * value)
        total = part if total is None else total + part
        squares = part_squares if squares is None else squares + part_squares
    return total, squares


def inner_body(x_hbm, filter_hbm, out_ref, sums_ref, x_ref, filter_ref, arrived, filter_arrived):
    count, _, depth = x_ref.shape
    wide = depth // arrived.shape[0]

    def piece(place):
        lanes = pl.ds(place * wide, wide)
        return pltpu.make_async_copy(
            x_hbm.at[0, :, :, lanes], x_ref.at[:, :, lanes], arrived.at[place]
        )

    taps_copy = pltpu.make_async_copy(filter_hbm, filter_ref, filter_arrived)
    taps_copy.start()
    for place in range(arrived.shape[0]):
        piece(place).start()
    taps_copy.wait()
    for place in range(arrived.shape[0]):
        piece(place).wait()

        @pl.loop(place * wide // LANES, (place + 1) * wide // LANES)
        def _(block):
            lanes = pl.ds(pl.multiple_of(block * LANES, LANES), LANES)
            total, squares = dilated_rows(
                lambda row: x_ref[row, :, lanes].astype(jnp.float32),
                range(RATE, count - RATE),
                taps_of(filter_ref, lanes),
                out_ref,
                lanes,
            )
            store_sums(sums_ref, lanes, total, squares)


def edge_starts(count):
    core = lax.axis_index("space_1")
    return (1 - core) * (count - RATE), core * (count - RATE)


def edge_rows_body(x_hbm, chip_ref, cross_ref, arrived):
    starts = edge_starts(x_hbm.shape[1])
    copies = [
        pltpu.make_async_copy(x_hbm.at[0, pl.ds(start, RATE)], out_ref, arrived.at[place])
        for place, (start, out_ref) in enumerate(zip(starts, (chip_ref, cross_ref)))
    ]
    for copy in copies:
        copy.start()
    for copy in copies:
        copy.wait()


def edge_body(x_ref, chip_ref, cross_ref, filter_ref, inner_ref, out_ref, sums_ref):
    count = x_ref.shape[0]
    core = lax.axis_index("space_1")

    @pl.loop(0, x_ref.shape[2] // LANES)
    def _(block):
        lanes = pl.ds(pl.multiple_of(block * LANES, LANES), LANES)

        @functools.cache
        def row_at(row):
            if row < 0:
                return halo_row(chip_ref, cross_ref, core == 1, row + RATE, lanes)
            if row >= count:
                return halo_row(chip_ref, cross_ref, core == 0, row - count, lanes)
            return x_ref[row, :, lanes].astype(jnp.float32)

        rows = (*range(RATE), *range(count - RATE, count))
        total, squares = dilated_rows(row_at, rows, taps_of(filter_ref, lanes), out_ref, lanes)
        store_sums(sums_ref, lanes, total, squares)
        sums_ref[:, lanes] = sums_ref[:, lanes] + inner_ref[:, lanes]


def store_terms(terms_ref, parts_ref, gain_ref, shift_ref, pixels):
    for block in range(gain_ref.shape[0]):
        lanes = slice(block * LANES, (block + 1) * LANES)
        sums = jnp.sum(parts_ref[:, :, lanes], axis=0)
        average = sums[0:1] / pixels
        variance = sums[1:2] / pixels - average * average
        factor = gain_ref[block : block + 1] * lax.rsqrt(variance + epsilon)
        terms_ref[0:1, lanes] = factor
        terms_ref[1:2, lanes] = shift_ref[block : block + 1] - average * factor


def halo_row(chip_ref, cross_ref, chip_holds, row, lanes):
    return jnp.where(chip_holds, chip_ref[row, :, lanes], cross_ref[row, :, lanes]).astype(jnp.float32)


def third_body(
    pixels, u_ref, chip_ref, cross_ref, parts_ref, gain_ref, shift_ref, filter_ref,
    out_ref, sums_ref, terms_ref,
):
    count = u_ref.shape[0]
    store_terms(terms_ref, parts_ref, gain_ref, shift_ref, pixels)

    @pl.loop(0, u_ref.shape[2] // LANES)
    def _(block):
        lanes = pl.ds(pl.multiple_of(block * LANES, LANES), LANES)
        taps = taps_of(filter_ref, lanes)
        factor = terms_ref[0:1, lanes]
        offset = terms_ref[1:2, lanes]
        core = lax.axis_index("space_1")
        strip = lax.axis_index(SPACE)
        above = (strip > 0).astype(jnp.float32)
        below = (strip < lax.axis_size(SPACE) - 1).astype(jnp.float32)

        @functools.cache
        def row_at(row):
            if row < 0:
                value = halo_row(chip_ref, cross_ref, core == 1, row + RATE, lanes)
                value = value * (factor * above) + offset * above
            elif row >= count:
                value = halo_row(chip_ref, cross_ref, core == 0, row - count, lanes)
                value = value * (factor * below) + offset * below
            else:
                value = u_ref[row, :, lanes] * factor + offset
            return jnp.maximum(value, 0.0).astype(jnp.bfloat16).astype(jnp.float32)

        total, squares = dilated_rows(row_at, range(count), taps, out_ref, lanes)
        store_sums(sums_ref, lanes, total, squares)


def project_body(pixels, places, n_parts, n_edges, *refs):
    part_refs = refs[:n_parts]
    parts_ref, gain_ref, shift_ref, weight_hbm, out_ref, sums_ref = refs[n_parts : n_parts + 6]
    edge_refs = refs[n_parts + 6 : n_parts + 6 + n_edges]
    terms_ref, act_ref, weight_ref, arrived = refs[n_parts + 6 + n_edges :]
    count, cols, width = out_ref.shape
    depth = act_ref.shape[1]
    wide = width // arrived.shape[0]

    def piece(block, lanes):
        return pltpu.make_async_copy(
            weight_hbm.at[:, lanes], weight_ref.at[:, lanes], arrived.at[block]
        )

    for block in range(arrived.shape[0]):
        piece(block, pl.ds(block * wide, wide)).start()
    store_terms(terms_ref, parts_ref, gain_ref, shift_ref, pixels)
    pair = 2
    for u_ref, first_row in zip(part_refs, places):

        @pl.loop(0, u_ref.shape[0] // pair)
        def _(step):
            factor = terms_ref[0:1]
            offset = terms_ref[1:2]
            value = u_ref[pl.ds(step * pair, pair)].reshape(pair * cols, depth)
            row = first_row + step * pair
            if len(places) > 1 and first_row == 0:
                row = step * (count - pair)
            act_ref[pl.ds(pl.multiple_of(row * cols, pair * cols), pair * cols)] = jnp.maximum(
                value * factor + offset, 0.0
            ).astype(jnp.bfloat16)

    @pl.loop(0, arrived.shape[0])
    def _(block):
        lanes = pl.ds(pl.multiple_of(block * wide, wide), wide)
        piece(block, lanes).wait()
        result = jnp.dot(act_ref[...], weight_ref[:, lanes], preferred_element_type=jnp.float32)
        store_sums(sums_ref, lanes, summed_rows(result), summed_rows(result * result))
        result = result.reshape(count, cols, wide)
        out_ref[:, :, lanes] = result
        for edge_ref, start in zip(edge_refs, edge_starts(count)):
            edge_ref[:, :, lanes] = out_ref[pl.ds(start, RATE), :, lanes]


def last_body(pixels, u_ref, parts_ref, gain_ref, shift_ref, out_ref, terms_ref):
    @pl.when(pl.program_id(0) == 0)
    def _():
        store_terms(terms_ref, parts_ref, gain_ref, shift_ref, pixels)

    rows = out_ref.shape[1]
    value = u_ref[pl.ds(pl.program_id(0) * rows, rows)]
    out_ref[0] = jnp.maximum(value * terms_ref[0:1] + terms_ref[1:2], 0.0).astype(jnp.bfloat16)


def dilated_inner(x, weight):
    rows, cols, depth = x.shape[1:]
    inner = rows - 2 * RATE
    return pl.pallas_call(
        inner_body,
        out_shape=[
            pltpu.VMEM((inner, cols, depth), jnp.float32),
            pltpu.VMEM((2, depth), jnp.float32),
            pltpu.VMEM((rows, cols, depth), x.dtype),
            pltpu.VMEM(weight.shape, weight.dtype),
        ],
        in_specs=[HBM] * 2,
        out_specs=[VMEM] * 4,
        scratch_shapes=[pltpu.SemaphoreType.DMA((4,)), pltpu.SemaphoreType.DMA],
        compiler_params=pltpu.CompilerParams(vmem_limit_bytes=12 << 20),
        cost_estimate=pl.CostEstimate(
            flops=20 * inner * cols * depth, bytes_accessed=6 * rows * cols * depth, transcendentals=0
        ),
    )(x, weight)


def kept_in_hbm(array):
    return pltpu.with_memory_space_constraint(array, pltpu.HBM)


def edge_rows(x):
    edge = (RATE,) + x.shape[2:]
    return pl.pallas_call(
        edge_rows_body,
        out_shape=[pltpu.VMEM(edge, x.dtype)] * 2,
        in_specs=[HBM],
        out_specs=[VMEM] * 2,
        scratch_shapes=[pltpu.SemaphoreType.DMA((2,))],
        compiler_params=pltpu.CompilerParams(vmem_limit_bytes=4 << 20),
    )(x)


def dilated_edges(x, chip, cross, weight, inner_sums):
    cols, depth = x.shape[1:]
    return kernel_call(
        edge_body,
        [((2 * RATE, cols, depth), jnp.float32), ((2, depth), jnp.float32)],
        5,
        12 << 20,
        flops=40 * RATE * cols * depth,
        moved=20 * RATE * cols * depth,
    )(x, chip, cross, weight, inner_sums)


def project(pixels, pieces, places, parts, gain, shift, weight, edges):
    rows = sum(piece.shape[0] for piece in pieces)
    cols, depth = pieces[0].shape[1:]
    width = weight.shape[1]
    outs = [((rows, cols, width), jnp.float32), ((2, width), jnp.float32)]
    outs += [((RATE, cols, width), jnp.float32)] * edges
    return pl.pallas_call(
        functools.partial(project_body, pixels, places, len(pieces), edges),
        out_shape=[pltpu.VMEM(shape, dtype) for shape, dtype in outs],
        in_specs=[VMEM] * (len(pieces) + 3) + [HBM],
        out_specs=[VMEM] * len(outs),
        scratch_shapes=[
            pltpu.VMEM((2, depth), jnp.float32),
            pltpu.VMEM((rows * cols, depth), jnp.bfloat16),
            pltpu.VMEM((depth, width), jnp.bfloat16),
            pltpu.SemaphoreType.DMA((width // 256,)),
        ],
        compiler_params=pltpu.CompilerParams(vmem_limit_bytes=24 << 20),
        cost_estimate=pl.CostEstimate(
            flops=2 * rows * cols * depth * width,
            bytes_accessed=4 * rows * cols * (depth + width) + 2 * depth * width,
            transcendentals=0,
        ),
    )(*pieces, parts, gain, shift, weight)


def dilated_second(pixels, u, chip, cross, parts, gain, shift, weight):
    rows, cols, depth = u.shape
    return kernel_call(
        functools.partial(third_body, pixels),
        [((rows, cols, depth), jnp.float32), ((2, depth), jnp.float32)],
        7,
        16 << 20,
        scratch=[pltpu.VMEM((2, depth), jnp.float32)],
        flops=26 * rows * cols * depth,
        moved=8 * rows * cols * depth,
    )(u, chip, cross, parts, gain, shift, weight)


def last_norm(pixels, u, parts, gain, shift):
    rows, cols, depth = u.shape
    return pl.pallas_call(
        functools.partial(last_body, pixels),
        grid=(rows // 3,),
        out_shape=jax.ShapeDtypeStruct((1, rows, cols, depth), jnp.bfloat16),
        in_specs=[VMEM] * 4,
        out_specs=pl.BlockSpec((1, 3, cols, depth), lambda row: (0, row, 0, 0)),
        scratch_shapes=[pltpu.VMEM((2, depth), jnp.float32)],
        compiler_params=pltpu.CompilerParams(vmem_limit_bytes=20 << 20),
        cost_estimate=pl.CostEstimate(
            flops=3 * rows * cols * depth, bytes_accessed=6 * rows * cols * depth, transcendentals=0
        ),
    )(u, parts, gain, shift)


def pair_body(own_ref, other_ref, out_ref):
    out_ref[...] = jnp.broadcast_to((own_ref[...] + other_ref[...])[None], out_ref.shape)


def group_body(parts_ref, out_ref):
    out_ref[...] = jnp.broadcast_to(jnp.sum(parts_ref[...], axis=0)[None], out_ref.shape)


def gathered_sums(value):
    plane, line = ("batch_1", "space_0"), ("batch_0",)
    other = lax.ppermute(value, "space_1", [(0, 1), (1, 0)])
    shape = (lax.axis_size(plane),) + value.shape
    (copies,) = kernel_call(pair_body, [(shape, jnp.float32)], 2, 2 << 20)(value, other)
    parts = lax.all_to_all(copies, plane, 0, 0)
    shape = (lax.axis_size(line),) + value.shape
    (copies,) = kernel_call(group_body, [(shape, jnp.float32)], 1, 2 << 20)(parts)
    return lax.all_to_all(copies, line, 0, 0)


def from_neighbours(chip, cross):
    ends = [pair for i in range(1, lax.axis_size(SPACE) - 1, 2) for pair in ((i, i + 1), (i + 1, i))]
    chip = lax.ppermute(chip, "space_1", [(0, 1), (1, 0)])
    return chip, lax.ppermute(cross, SPACE, ends)


def per_device(
    features,
    depth_one,
    gain_one,
    shift_one,
    point_one,
    gain_two,
    shift_two,
    depth_two,
    gain_three,
    shift_three,
    point_two,
    gain_four,
    shift_four,
):
    rows, cols = features.shape[1:3]
    pixels = rows * cols * lax.axis_size(BATCH) * lax.axis_size(SPACE)
    names = (gain_one, shift_one, gain_two, shift_two, gain_three, shift_three, gain_four, shift_four)
    terms = [term.reshape(-1, LANES) for term in names]
    features, depth_one = kept_in_hbm(features), kept_in_hbm(depth_one)
    halo = from_neighbours(*edge_rows(features))
    inner, inner_sums, x, taps = dilated_inner(features, depth_one)
    edges, sums = dilated_edges(x, *halo, taps, inner_sums)
    parts = gathered_sums(sums)
    second, sums, chip, cross = project(
        pixels, (edges, inner), (0, RATE), parts, *terms[0:2], kept_in_hbm(point_one), 2
    )
    halo = from_neighbours(chip, cross)
    parts = gathered_sums(sums)
    third, sums = dilated_second(pixels, second, *halo, parts, *terms[2:4], depth_two)
    parts = gathered_sums(sums)
    fourth, sums = project(pixels, (third,), (0,), parts, *terms[4:6], kept_in_hbm(point_two), 0)
    parts = gathered_sums(sums)
    return last_norm(pixels, fourth, parts, *terms[6:8])


def solution(mesh):
    finer = Mesh(mesh.devices.reshape(8, 4, 4, 2), ("batch_0", "batch_1", "space_0", "space_1"))
    placed = (P(BATCH, SPACE, None, None),) + (P(),) * 12
    return jax.shard_map(
        per_device,
        mesh=finer,
        in_specs=placed,
        out_specs=P(BATCH, SPACE, None, None),
        check_vma=False,
    )
```

time: 297 us -> 144 us (0.48); the launches traced: 294 us -> 144 us
  blocking collectives: 223 us -> 102 us
  other arithmetic: 33.4 us -> 0 us
  Pallas kernels: 0 us -> 27.7 us
  matrix products: 15.5 us -> 0 us
  waiting for transfers between devices: 8.96 us -> 5.54 us
    psum x16 -> x0, blocking collectives: 223 us -> none  [one_axis_at_a_time(): return functools.reduce(lax.psum, axes, value)]
    all_to_all x0 -> x8, blocking collectives: none -> 102 us  [the longest x4 51.6 us: gathered_sums(): parts = lax.all_to_all(copies, plane, 0, 0)]
    pallas_call x0 -> x15, Pallas kernels: none -> 27.7 us  [the longest x2 13.3 us: project(): pl.pallas_call(functools.partial(project_body, pixels, places, len(pieces...]
    convert_element_type x6 -> x0, other arithmetic: 16.2 us -> none  [the longest x4 15.2 us: scaled(): jnp.maximum((values - average) * factor + offset, 0.0).astype(jnp.bfloat16)]
    dot_general x2 -> x0, matrix products: 15.5 us -> none  [project(): result = jnp.dot(flat, weight, preferred_element_type=jnp.float32)]
    reduce_sum x2 -> x0, other arithmetic: 13.1 us -> none  [local_sums(): jnp.sum(values, axis=(0, 1, 2))]
    concatenate x2 -> x0, other arithmetic: 4.05 us -> none  [padded_2(): jnp.concatenate([lax.ppermute(tail, axis, [(i, (i + 1) % count) for i in...]
    ppermute x4 -> x8, waiting for transfers between devices: 8.96 us -> 5.54 us  [the longest x4 4.56 us: gathered_sums(): other = lax.ppermute(value, 'space_1', [(0, 1), (1, 0)])]
  transfers between devices with their start and end apart: 4 -> 8, of which waited for: 4 -> 5; matrix products, arithmetic and copies ran while one was open for 0% -> 0% of each run, Pallas kernels for 0% -> 2%
where the time goes in v2:
time: 144 us
  blocking collectives  102 us (71%)
  Pallas kernels  27.7 us (19%)
  starting transfers between devices  8.38 us (6%)
  waiting for transfers between devices  5.54 us (4%)
    all_to_all x4, blocking collectives, gathered_sums(): parts = lax.all_to_all(copies, plane, 0, 0)  51.6 us
    all_to_all x4, blocking collectives, gathered_sums(): return lax.all_to_all(copies, line, 0, 0)  50.3 us
    pallas_call x2, Pallas kernels, project(): pl.pallas_call(functools.partial(project_body, pixels, places, len(pieces...  13.3 us
    ppermute x2, starting transfers between devices, from_neighbours(): return (chip, lax.ppermute(cross, SPACE, ends))  7.72 us
    pallas_call x1, Pallas kernels, dilated_second(): kernel_call(functools.partial(third_body, pixels), [((rows, cols, depth),...  5.51 us
    ppermute x4, waiting for transfers between devices, gathered_sums(): other = lax.ppermute(value, 'space_1', [(0, 1), (1, 0)])  4.56 us
    pallas_call x1, Pallas kernels, dilated_inner(): pl.pallas_call(inner_body, out_shape=[pltpu.VMEM((inner, cols, depth), jn...  3.4 us
  transfers between devices with their start and end apart: 8, of which 5 were waited for; matrix products, arithmetic and copies ran while one was open for 0% of the time, Pallas kernels for 2%

profile of v2, /device:TPU:2, one launch (start us, length us, event | category | flops | bytes accessed | tf_op | source)
XLA Modules:
  0.0 143.8 jit_solution(7964499433835144198)
XLA Ops:
  0.0 0.0 copy-start.8
  0.0 0.0 copy-start.7
  0.0 1.1 shard_map.128
  1.1 0.1 collective-permute-start
  1.2 4.3 %collective-permute-start.1 = (bf16[2,72,1024]{2,1,0:T(8,128)(2,1)S(1)}, bf16[2,72,1024]{2,1,0:T(8,128)(2,1)S(1)}, u32[]{:S(2)}, u32[]{:S(2)}) collective-permute-start(bf16[2,72,1024]{2,1,0:T(8,128)(2,1)S(1)} %get-tuple-element.23), channel_id=1, source_target_pairs={{1,2},{2,1},{3,4},{4,3},{5,6},{6,5},{9,10},{10,9},{11,12},{12,11},... | collective-permute-start | bytes 884744 | tf_op jit(solution)/shard_map/ppermute | solution.py:378
  5.5 3.4 %shard_map.127 = (f32[8,72,1024]{2,1,0:T(8,128)S(1)}, f32[2,1024]{1,0:T(2,128)S(1)}, bf16[12,72,1024]{2,1,0:T(8,128)(2,1)S(1)}, bf16[3,3,1024]{2,1,0:T(4,128)(2,1)S(1)}) custom-call(bf16[1,12,72,1024]{3,2,1,0:T(8,128)(2,1)} %x_hbm.3, bf16[3,3,1024]{2,1,0:T(4,128)(2,1)} %filter_hbm.1), custom_call_target="tpu_custom_call" | custom-call | flops 11796480 | bytes 5308416 | tf_op jit(solution)/shard_map/pallas_call | solution.py:255
  8.9 0.0 collective-permute-done.chip_ref
  8.9 1.0 collective-permute-done.1.cross_ref
  9.9 1.4 shard_map.129
  11.3 0.2 collective-permute-start.2
  11.5 1.1 collective-permute-done.2.other_ref
  12.6 13.4 %all_to_all.40.parts_ref = f32[16,2,1024]{2,1,0:T(2,128)S(1)} all-to-all(f32[16,2,1024]{2,1,0:T(2,128)S(1)} %shard_map.130), channel_id=1, replica_groups=mesh['batch_0'=8,'batch_1'=4,'space_0'=4,'space_1'=2] {'batch_1','space_0'}, dimensions={0} | all-to-all | bytes 262144 | tf_op jit(solution)/shard_map/all_to_all | solution.py:369
  26.0 0.1 shard_map.131
  26.0 16.6 %all_to_all.41.refs_2_ = f32[8,2,1024]{2,1,0:T(2,128)S(1)} all-to-all(f32[8,2,1024]{2,1,0:T(2,128)S(1)} %shard_map.131), channel_id=1, replica_groups=mesh['batch_0'=8,'batch_1'=4,'space_0'=4,'space_1'=2] {'batch_0'}, dimensions={0} | all-to-all | bytes 131072 | tf_op jit(solution)/shard_map/all_to_all | solution.py:372
  42.7 0.0 copy-done.8
  42.7 0.0 copy-done.7
  42.7 0.0 copy-start
  42.7 0.0 copy-start.1
  42.7 0.0 copy-start.2
  42.7 5.0 %shard_map.132 = (f32[12,72,1536]{2,1,0:T(8,128)S(1)}, f32[2,1536]{1,0:T(2,128)S(1)}, f32[2,72,1536]{2,1,0:T(8,128)S(1)}, f32[2,72,1536]{2,1,0:T(8,128)S(1)}) custom-call(f32[4,72,1024]{2,1,0:T(8,128)S(1)} %get-tuple-element.26.refs_0_, f32[8,72,1024]{2,1,0:T(8,128)S(1)} %get-tuple-element.27.refs_1_, f32[8,2,1024]{2,1,0:T(2,128)S(1)} %all_to_all.41.refs_2_, ...), custom_call_target="tpu_custom_call" | custom-call | flops 2717908992 | bytes 11993088 | tf_op jit(solution)/shard_map/pallas_call | solution.py:307
  47.7 0.1 collective-permute-start.3
  47.8 3.5 %collective-permute-start.4 = (f32[2,72,1536]{2,1,0:T(8,128)S(1)}, f32[2,72,1536]{2,1,0:T(8,128)S(1)}, u32[]{:S(2)}, u32[]{:S(2)}) collective-permute-start(f32[2,72,1536]{2,1,0:T(8,128)S(1)} %get-tuple-element.31), channel_id=1, source_target_pairs={{1,2},{2,1},{3,4},{4,3},{5,6},{6,5},{9,10},{10,9},{11,12},{12,11},... | collective-permute-start | bytes 2654216 | tf_op jit(solution)/shard_map/ppermute | solution.py:378
  51.3 0.1 collective-permute-start.5
  51.4 1.2 collective-permute-done.5.other_ref
  52.6 13.0 %all_to_all.42.parts_ref = f32[16,2,1536]{2,1,0:T(2,128)S(1)} all-to-all(f32[16,2,1536]{2,1,0:T(2,128)S(1)} %shard_map.133), channel_id=1, replica_groups=mesh['batch_0'=8,'batch_1'=4,'space_0'=4,'space_1'=2] {'batch_1','space_0'}, dimensions={0} | all-to-all | bytes 393216 | tf_op jit(solution)/shard_map/all_to_all | solution.py:369
  65.6 0.1 shard_map.134
  65.7 11.1 %all_to_all.43.parts_ref = f32[8,2,1536]{2,1,0:T(2,128)S(1)} all-to-all(f32[8,2,1536]{2,1,0:T(2,128)S(1)} %shard_map.134), channel_id=1, replica_groups=mesh['batch_0'=8,'batch_1'=4,'space_0'=4,'space_1'=2] {'batch_0'}, dimensions={0} | all-to-all | bytes 196608 | tf_op jit(solution)/shard_map/all_to_all | solution.py:372
  76.8 0.0 collective-permute-done.3.chip_ref
  76.8 0.0 collective-permute-done.4.cross_ref
  76.8 0.0 copy-done
  76.8 0.0 copy-done.1
  76.8 0.0 copy-done.2
  76.8 0.0 copy-start.5
  76.8 0.0 copy-start.6
  76.8 5.5 %shard_map.135 = (f32[12,72,1536]{2,1,0:T(8,128)S(1)}, f32[2,1536]{1,0:T(2,128)S(1)}) custom-call(f32[12,72,1536]{2,1,0:T(8,128)S(1)} %get-tuple-element.29.u_ref, f32[2,72,1536]{2,1,0:T(8,128)S(1)} %collective-permute-done.3.chip_ref, f32[2,72,1536]{2,1,0:T(8,128)S(1)} %collective-permute-done.4.cross_ref, f32[8,2,1536]{2,1,0:T(2,128)S(1)} %all_to_all.43.parts_ref, ...), custom_call_target="tpu_custom_call" | custom-call | flops 34504704 | bytes 10616832 | tf_op jit(solution)/shard_map/pallas_call | solution.py:329
  82.4 0.1 collective-permute-start.6
  82.5 1.2 collective-permute-done.6.other_ref
  83.6 13.2 %all_to_all.44.parts_ref = f32[16,2,1536]{2,1,0:T(2,128)S(1)} all-to-all(f32[16,2,1536]{2,1,0:T(2,128)S(1)} %shard_map.136), channel_id=1, replica_groups=mesh['batch_0'=8,'batch_1'=4,'space_0'=4,'space_1'=2] {'batch_1','space_0'}, dimensions={0} | all-to-all | bytes 393216 | tf_op jit(solution)/shard_map/all_to_all | solution.py:369
  96.8 0.1 shard_map.137
  96.9 11.1 %all_to_all.45.refs_1_ = f32[8,2,1536]{2,1,0:T(2,128)S(1)} all-to-all(f32[8,2,1536]{2,1,0:T(2,128)S(1)} %shard_map.137), channel_id=1, replica_groups=mesh['batch_0'=8,'batch_1'=4,'space_0'=4,'space_1'=2] {'batch_0'}, dimensions={0} | all-to-all | bytes 196608 | tf_op jit(solution)/shard_map/all_to_all | solution.py:372
  108.0 0.0 copy-done.5
  108.0 0.0 copy-done.6
  108.0 0.0 copy-start.3
  108.0 0.0 copy-start.4
  108.0 8.3 %shard_map.138 = (f32[12,72,2048]{2,1,0:T(8,128)S(1)}, f32[2,2048]{1,0:T(2,128)S(1)}) custom-call(f32[12,72,1536]{2,1,0:T(8,128)S(1)} %get-tuple-element.33.refs_0_, f32[8,2,1536]{2,1,0:T(2,128)S(1)} %all_to_all.45.refs_1_, f32[12,128]{1,0:T(8,128)S(1)} %bitcast.12, f32[12,128]{1,0:T(8,128)S(1)} %bitcast.13, bf16[1536,2048]{1,0:T(8,128)(2,1)} %refs_4_.1), custom_call_target="tpu_custom_call" | custom-call | flops 5435817984 | bytes 18677760 | tf_op jit(solution)/shard_map/pallas_call | solution.py:307
  116.3 0.1 collective-permute-start.7
  116.4 1.2 collective-permute-done.7.other_ref
  117.6 12.0 %all_to_all.46.parts_ref = f32[16,2,2048]{2,1,0:T(2,128)S(1)} all-to-all(f32[16,2,2048]{2,1,0:T(2,128)S(1)} %shard_map.139), channel_id=1, replica_groups=mesh['batch_0'=8,'batch_1'=4,'space_0'=4,'space_1'=2] {'batch_1','space_0'}, dimensions={0} | all-to-all | bytes 524288 | tf_op jit(solution)/shard_map/all_to_all | solution.py:369
  129.6 0.1 shard_map.140
  129.7 11.5 %all_to_all.47.parts_ref = f32[8,2,2048]{2,1,0:T(2,128)S(1)} all-to-all(f32[8,2,2048]{2,1,0:T(2,128)S(1)} %shard_map.140), channel_id=1, replica_groups=mesh['batch_0'=8,'batch_1'=4,'space_0'=4,'space_1'=2] {'batch_0'}, dimensions={0} | all-to-all | bytes 262144 | tf_op jit(solution)/shard_map/all_to_all | solution.py:372
  141.2 0.0 copy-done.3
  141.2 0.0 copy-done.4
  141.2 2.6 %shard_map.141 = bf16[1,12,72,2048]{3,2,1,0:T(8,128)(2,1)} custom-call(f32[12,72,2048]{2,1,0:T(8,128)S(1)} %get-tuple-element.35.u_ref, f32[8,2,2048]{2,1,0:T(2,128)S(1)} %all_to_all.47.parts_ref, f32[16,128]{1,0:T(8,128)S(1)} %bitcast.10, f32[16,128]{1,0:T(8,128)S(1)} %bitcast.11), custom_call_target="tpu_custom_call" | custom-call | flops 5308416 | bytes 10616832 | tf_op jit(solution)/shard_map/pallas_call | solution.py:342
  (4 shorter events, 0.1 us)
Async XLA Ops:
  0.0 42.7 %copy-start.8 = (f32[1024]{0:T(1024)S(1)}, f32[1024]{0:T(1024)}, u32[]{:S(2)}) copy-start(f32[1024]{0:T(1024)} %param.16) | copy-start | bytes 12292
  0.0 42.7 %copy-start.7 = (f32[1024]{0:T(1024)S(1)}, f32[1024]{0:T(1024)}, u32[]{:S(2)}) copy-start(f32[1024]{0:T(1024)} %param.15) | copy-start | bytes 12292
  1.1 7.8 %collective-permute-start = (bf16[2,72,1024]{2,1,0:T(8,128)(2,1)S(1)}, bf16[2,72,1024]{2,1,0:T(8,128)(2,1)S(1)}, u32[]{:S(2)}, u32[]{:S(2)}) collective-permute-start(bf16[2,72,1024]{2,1,0:T(8,128)(2,1)S(1)} %get-tuple-element.22), channel_id=1, source_target_pairs={{0,1},{1,0},{2,3},{3,2},{4,5},{5,4},{6,7},{7,6},{8,9},{9,8},{10,11... | collective-permute-start | bytes 884744 | tf_op jit(solution)/shard_map/ppermute | solution.py:377
  1.2 8.7 %collective-permute-start.1 = (bf16[2,72,1024]{2,1,0:T(8,128)(2,1)S(1)}, bf16[2,72,1024]{2,1,0:T(8,128)(2,1)S(1)}, u32[]{:S(2)}, u32[]{:S(2)}) collective-permute-start(bf16[2,72,1024]{2,1,0:T(8,128)(2,1)S(1)} %get-tuple-element.23), channel_id=1, source_target_pairs={{1,2},{2,1},{3,4},{4,3},{5,6},{6,5},{9,10},{10,9},{11,12},{12,11},... | collective-permute-start | bytes 884744 | tf_op jit(solution)/shard_map/ppermute | solution.py:378
  11.3 1.3 collective-permute-start.2
  42.7 34.1 %copy-start = (bf16[3,3,1536]{2,1,0:T(4,128)(2,1)S(1)}, bf16[3,3,1536]{2,1,0:T(4,128)(2,1)}, u32[]{:S(2)}) copy-start(bf16[3,3,1536]{2,1,0:T(4,128)(2,1)} %filter_ref.1) | copy-start | bytes 82948
  42.7 34.1 %copy-start.1 = (f32[1536]{0:T(1024)S(1)}, f32[1536]{0:T(1024)}, u32[]{:S(2)}) copy-start(f32[1536]{0:T(1024)} %param.18) | copy-start | bytes 18436
  42.7 34.1 %copy-start.2 = (f32[1536]{0:T(1024)S(1)}, f32[1536]{0:T(1024)}, u32[]{:S(2)}) copy-start(f32[1536]{0:T(1024)} %param.19) | copy-start | bytes 18436
  47.7 29.1 %collective-permute-start.3 = (f32[2,72,1536]{2,1,0:T(8,128)S(1)}, f32[2,72,1536]{2,1,0:T(8,128)S(1)}, u32[]{:S(2)}, u32[]{:S(2)}) collective-permute-start(f32[2,72,1536]{2,1,0:T(8,128)S(1)} %get-tuple-element.30), channel_id=1, source_target_pairs={{0,1},{1,0},{2,3},{3,2},{4,5},{5,4},{6,7},{7,6},{8,9},{9,8},{10,11... | collective-permute-start | bytes 2654216 | tf_op jit(solution)/shard_map/ppermute | solution.py:377
  47.8 29.0 %collective-permute-start.4 = (f32[2,72,1536]{2,1,0:T(8,128)S(1)}, f32[2,72,1536]{2,1,0:T(8,128)S(1)}, u32[]{:S(2)}, u32[]{:S(2)}) collective-permute-start(f32[2,72,1536]{2,1,0:T(8,128)S(1)} %get-tuple-element.31), channel_id=1, source_target_pairs={{1,2},{2,1},{3,4},{4,3},{5,6},{6,5},{9,10},{10,9},{11,12},{12,11},... | collective-permute-start | bytes 2654216 | tf_op jit(solution)/shard_map/ppermute | solution.py:378
  51.3 1.3 collective-permute-start.5
  76.8 31.2 %copy-start.5 = (f32[1536]{0:T(1024)S(1)}, f32[1536]{0:T(1024)}, u32[]{:S(2)}) copy-start(f32[1536]{0:T(1024)} %param.21) | copy-start | bytes 18436
  76.8 31.2 %copy-start.6 = (f32[1536]{0:T(1024)S(1)}, f32[1536]{0:T(1024)}, u32[]{:S(2)}) copy-start(f32[1536]{0:T(1024)} %param.22) | copy-start | bytes 18436
  82.4 1.3 collective-permute-start.6
  108.0 33.2 %copy-start.3 = (f32[2048]{0:T(1024)S(1)}, f32[2048]{0:T(1024)}, u32[]{:S(2)}) copy-start(f32[2048]{0:T(1024)} %param.24) | copy-start | bytes 24580
  108.0 33.2 %copy-start.4 = (f32[2048]{0:T(1024)S(1)}, f32[2048]{0:T(1024)}, u32[]{:S(2)}) copy-start(f32[2048]{0:T(1024)} %param.25) | copy-start | bytes 24580
  116.3 1.3 collective-permute-start.7

commit v3 on v2

--- a/solution.py
+++ b/solution.py
@@ -10,6 +10,7 @@
 
 RATE = 2
 LANES = 128
+OFFSET_ROWS = 8
 BATCH = ("batch_0", "batch_1")
 SPACE = ("space_0", "space_1")
 
@@ -67,7 +68,7 @@
 
 def dilated_rows(row_at, rows, taps, out_ref, lanes):
     total = squares = None
-    for place, row in enumerate(rows):
+    for place, row in sorted(enumerate(rows), key=lambda pair: (pair[1] % 2, pair[1])):
         value = dilated_row([row_at(row - RATE), row_at(row), row_at(row + RATE)], taps)
         out_ref[place, :, lanes] = value
         part, part_squares = summed_rows(value), summed_rows(value * value)
@@ -76,7 +77,10 @@
     return total, squares
 
 
-def inner_body(x_hbm, filter_hbm, out_ref, sums_ref, x_ref, filter_ref, arrived, filter_arrived):
+def inner_body(
+    x_hbm, filter_hbm, weight_hbm, out_ref, sums_ref, x_ref, filter_ref, weight_ref, arrived,
+    filter_arrived, weight_arrived,
+):
     count, _, depth = x_ref.shape
     wide = depth // arrived.shape[0]
 
@@ -90,6 +94,8 @@
     taps_copy.start()
     for place in range(arrived.shape[0]):
         piece(place).start()
+    weight_copy = pltpu.make_async_copy(weight_hbm, weight_ref, weight_arrived)
+    weight_copy.start()
     taps_copy.wait()
     for place in range(arrived.shape[0]):
         piece(place).wait()
@@ -98,13 +104,15 @@
         def _(block):
             lanes = pl.ds(pl.multiple_of(block * LANES, LANES), LANES)
             total, squares = dilated_rows(
-                lambda row: x_ref[row, :, lanes].astype(jnp.float32),
+                functools.cache(lambda row: x_ref[row, :, lanes].astype(jnp.float32)),
                 range(RATE, count - RATE),
                 taps_of(filter_ref, lanes),
                 out_ref,
                 lanes,
             )
             store_sums(sums_ref, lanes, total, squares)
+
+    weight_copy.wait()
 
 
 def edge_starts(count):
@@ -161,11 +169,24 @@
     return jnp.where(chip_holds, chip_ref[row, :, lanes], cross_ref[row, :, lanes]).astype(jnp.float32)
 
 
+def less_offset(row, offset):
+    last = jnp.broadcast_to(offset, (OFFSET_ROWS, offset.shape[1]))
+    return jnp.concatenate([row - offset, last], axis=0).astype(jnp.bfloat16)
+
+
+def restored_row(chip_ref, cross_ref, chip_holds, row, lanes):
+    value = halo_row(chip_ref, cross_ref, chip_holds, row, lanes)
+    cols = value.shape[0] - OFFSET_ROWS
+    return value[:cols] + value[cols : cols + 1]
+
+
 def third_body(
     pixels, u_ref, chip_ref, cross_ref, parts_ref, gain_ref, shift_ref, filter_ref,
-    out_ref, sums_ref, terms_ref,
+    weight_hbm, out_ref, sums_ref, weight_ref, terms_ref, arrived,
 ):
     count = u_ref.shape[0]
+    weight_copy = pltpu.make_async_copy(weight_hbm, weight_ref, arrived)
+    weight_copy.start()
     store_terms(terms_ref, parts_ref, gain_ref, shift_ref, pixels)
 
     @pl.loop(0, u_ref.shape[2] // LANES)
@@ -182,35 +203,29 @@
         @functools.cache
         def row_at(row):
             if row < 0:
-                value = halo_row(chip_ref, cross_ref, core == 1, row + RATE, lanes)
+                value = restored_row(chip_ref, cross_ref, core == 1, row + RATE, lanes)
                 value = value * (factor * above) + offset * above
             elif row >= count:
-                value = halo_row(chip_ref, cross_ref, core == 0, row - count, lanes)
+                value = restored_row(chip_ref, cross_ref, core == 0, row - count, lanes)
                 value = value * (factor * below) + offset * below
             else:
                 value = u_ref[row, :, lanes] * factor + offset
-            return jnp.maximum(value, 0.0).astype(jnp.bfloat16).astype(jnp.float32)
+            return jnp.maximum(value, 0.0)
 
         total, squares = dilated_rows(row_at, range(count), taps, out_ref, lanes)
         store_sums(sums_ref, lanes, total, squares)
 
+    weight_copy.wait()
+
 
 def project_body(pixels, places, n_parts, n_edges, *refs):
     part_refs = refs[:n_parts]
-    parts_ref, gain_ref, shift_ref, weight_hbm, out_ref, sums_ref = refs[n_parts : n_parts + 6]
+    parts_ref, gain_ref, shift_ref, weight_ref, out_ref, sums_ref = refs[n_parts : n_parts + 6]
     edge_refs = refs[n_parts + 6 : n_parts + 6 + n_edges]
-    terms_ref, act_ref, weight_ref, arrived = refs[n_parts + 6 + n_edges :]
+    terms_ref, act_ref = refs[n_parts + 6 + n_edges :]
     count, cols, width = out_ref.shape
     depth = act_ref.shape[1]
-    wide = width // arrived.shape[0]
-
-    def piece(block, lanes):
-        return pltpu.make_async_copy(
-            weight_hbm.at[:, lanes], weight_ref.at[:, lanes], arrived.at[block]
-        )
-
-    for block in range(arrived.shape[0]):
-        piece(block, pl.ds(block * wide, wide)).start()
+    wide = 512
     store_terms(terms_ref, parts_ref, gain_ref, shift_ref, pixels)
     pair = 2
     for u_ref, first_row in zip(part_refs, places):
@@ -227,16 +242,16 @@
                 value * factor + offset, 0.0
             ).astype(jnp.bfloat16)
 
-    @pl.loop(0, arrived.shape[0])
+    @pl.loop(0, width // wide)
     def _(block):
         lanes = pl.ds(pl.multiple_of(block * wide, wide), wide)
-        piece(block, lanes).wait()
         result = jnp.dot(act_ref[...], weight_ref[:, lanes], preferred_element_type=jnp.float32)
         store_sums(sums_ref, lanes, summed_rows(result), summed_rows(result * result))
-        result = result.reshape(count, cols, wide)
-        out_ref[:, :, lanes] = result
+        out_ref[:, :, lanes] = result.reshape(count, cols, wide)
+        offset = (sums_ref[0:1, lanes] / (count * cols)).astype(jnp.bfloat16).astype(jnp.float32)
         for edge_ref, start in zip(edge_refs, edge_starts(count)):
-            edge_ref[:, :, lanes] = out_ref[pl.ds(start, RATE), :, lanes]
+            for row in range(RATE):
+                edge_ref[row, :, lanes] = less_offset(out_ref[start + row, :, lanes], offset)
 
 
 def last_body(pixels, u_ref, parts_ref, gain_ref, shift_ref, out_ref, terms_ref):
@@ -249,7 +264,7 @@
     out_ref[0] = jnp.maximum(value * terms_ref[0:1] + terms_ref[1:2], 0.0).astype(jnp.bfloat16)
 
 
-def dilated_inner(x, weight):
+def dilated_inner(x, taps, weight):
     rows, cols, depth = x.shape[1:]
     inner = rows - 2 * RATE
     return pl.pallas_call(
@@ -258,16 +273,17 @@
             pltpu.VMEM((inner, cols, depth), jnp.float32),
             pltpu.VMEM((2, depth), jnp.float32),
             pltpu.VMEM((rows, cols, depth), x.dtype),
+            pltpu.VMEM(taps.shape, taps.dtype),
             pltpu.VMEM(weight.shape, weight.dtype),
         ],
-        in_specs=[HBM] * 2,
-        out_specs=[VMEM] * 4,
-        scratch_shapes=[pltpu.SemaphoreType.DMA((4,)), pltpu.SemaphoreType.DMA],
+        in_specs=[HBM] * 3,
+        out_specs=[VMEM] * 5,
+        scratch_shapes=[pltpu.SemaphoreType.DMA((4,))] + [pltpu.SemaphoreType.DMA] * 2,
         compiler_params=pltpu.CompilerParams(vmem_limit_bytes=12 << 20),
         cost_estimate=pl.CostEstimate(
             flops=20 * inner * cols * depth, bytes_accessed=6 * rows * cols * depth, transcendentals=0
         ),
-    )(x, weight)
+    )(x, taps, weight)
 
 
 def kept_in_hbm(array):
@@ -303,17 +319,15 @@
     cols, depth = pieces[0].shape[1:]
     width = weight.shape[1]
     outs = [((rows, cols, width), jnp.float32), ((2, width), jnp.float32)]
-    outs += [((RATE, cols, width), jnp.float32)] * edges
+    outs += [((RATE, cols + OFFSET_ROWS, width), jnp.bfloat16)] * edges
     return pl.pallas_call(
         functools.partial(project_body, pixels, places, len(pieces), edges),
         out_shape=[pltpu.VMEM(shape, dtype) for shape, dtype in outs],
-        in_specs=[VMEM] * (len(pieces) + 3) + [HBM],
+        in_specs=[VMEM] * (len(pieces) + 4),
         out_specs=[VMEM] * len(outs),
         scratch_shapes=[
             pltpu.VMEM((2, depth), jnp.float32),
             pltpu.VMEM((rows * cols, depth), jnp.bfloat16),
-            pltpu.VMEM((depth, width), jnp.bfloat16),
-            pltpu.SemaphoreType.DMA((width // 256,)),
         ],
         compiler_params=pltpu.CompilerParams(vmem_limit_bytes=24 << 20),
         cost_estimate=pl.CostEstimate(
@@ -324,17 +338,23 @@
     )(*pieces, parts, gain, shift, weight)
 
 
-def dilated_second(pixels, u, chip, cross, parts, gain, shift, weight):
+def dilated_second(pixels, u, chip, cross, parts, gain, shift, taps, weight):
     rows, cols, depth = u.shape
-    return kernel_call(
+    return pl.pallas_call(
         functools.partial(third_body, pixels),
-        [((rows, cols, depth), jnp.float32), ((2, depth), jnp.float32)],
-        7,
-        16 << 20,
-        scratch=[pltpu.VMEM((2, depth), jnp.float32)],
-        flops=26 * rows * cols * depth,
-        moved=8 * rows * cols * depth,
-    )(u, chip, cross, parts, gain, shift, weight)
+        out_shape=[
+            pltpu.VMEM((rows, cols, depth), jnp.float32),
+            pltpu.VMEM((2, depth), jnp.float32),
+            pltpu.VMEM(weight.shape, weight.dtype),
+        ],
+        in_specs=[VMEM] * 7 + [HBM],
+        out_specs=[VMEM] * 3,
+        scratch_shapes=[pltpu.VMEM((2, depth), jnp.float32), pltpu.SemaphoreType.DMA],
+        compiler_params=pltpu.CompilerParams(vmem_limit_bytes=16 << 20),
+        cost_estimate=pl.CostEstimate(
+            flops=26 * rows * cols * depth, bytes_accessed=8 * rows * cols * depth, transcendentals=0
+        ),
+    )(u, chip, cross, parts, gain, shift, taps, weight)
 
 
 def last_norm(pixels, u, parts, gain, shift):
@@ -399,17 +419,19 @@
     terms = [term.reshape(-1, LANES) for term in names]
     features, depth_one = kept_in_hbm(features), kept_in_hbm(depth_one)
     halo = from_neighbours(*edge_rows(features))
-    inner, inner_sums, x, taps = dilated_inner(features, depth_one)
+    inner, inner_sums, x, taps, weight = dilated_inner(features, depth_one, kept_in_hbm(point_one))
     edges, sums = dilated_edges(x, *halo, taps, inner_sums)
     parts = gathered_sums(sums)
     second, sums, chip, cross = project(
-        pixels, (edges, inner), (0, RATE), parts, *terms[0:2], kept_in_hbm(point_one), 2
+        pixels, (edges, inner), (0, RATE), parts, *terms[0:2], weight, 2
     )
     halo = from_neighbours(chip, cross)
     parts = gathered_sums(sums)
-    third, sums = dilated_second(pixels, second, *halo, parts, *terms[2:4], depth_two)
+    third, sums, weight = dilated_second(
+        pixels, second, *halo, parts, *terms[2:4], depth_two, kept_in_hbm(point_two)
+    )
     parts = gathered_sums(sums)
-    fourth, sums = project(pixels, (third,), (0,), parts, *terms[4:6], kept_in_hbm(point_two), 0)
+    fourth, sums = project(pixels, (third,), (0,), parts, *terms[4:6], weight, 0)
     parts = gathered_sums(sums)
     return last_norm(pixels, fourth, parts, *terms[6:8])
 

time: 144 us -> 138 us (0.958)
  blocking collectives: 102 us -> 98.1 us
  Pallas kernels: 27.7 us -> 24.8 us
    all_to_all x4, blocking collectives: 51.6 us -> 47.8 us  [gathered_sums(): parts = lax.all_to_all(copies, plane, 0, 0)]
    pallas_call x2, Pallas kernels: 13.3 us -> 10.8 us  [project(): pl.pallas_call(functools.partial(project_body, pixels, places, len(pieces...]
where the time goes in v3:
time: 138 us; the launch traced here: 137 us
  blocking collectives  98.1 us (71%)
  Pallas kernels  24.8 us (18%)
  starting transfers between devices  8.49 us (6%)
  waiting for transfers between devices  5.64 us (4%)
    all_to_all x4, blocking collectives, gathered_sums(): return lax.all_to_all(copies, line, 0, 0)  50.3 us
    all_to_all x4, blocking collectives, gathered_sums(): parts = lax.all_to_all(copies, plane, 0, 0)  47.8 us
    pallas_call x2, Pallas kernels, project(): pl.pallas_call(functools.partial(project_body, pixels, places, len(pieces...  10.8 us
    ppermute x2, starting transfers between devices, from_neighbours(): return (chip, lax.ppermute(cross, SPACE, ends))  7.83 us
    pallas_call x1, Pallas kernels, dilated_second(): pl.pallas_call(functools.partial(third_body, pixels), out_shape=[pltpu.VM...  5.28 us
    ppermute x4, waiting for transfers between devices, gathered_sums(): other = lax.ppermute(value, 'space_1', [(0, 1), (1, 0)])  4.56 us
    pallas_call x1, Pallas kernels, dilated_inner(): pl.pallas_call(inner_body, out_shape=[pltpu.VMEM((inner, cols, depth), jn...  3.3 us
  transfers between devices with their start and end apart: 8, of which 5 were waited for; matrix products, arithmetic and copies ran while one was open for 0% of the time, Pallas kernels for 2%

profile of v3, /device:TPU:2, one launch (start us, length us, event | category | flops | bytes accessed | tf_op | source)
XLA Modules:
  0.0 137.4 jit_solution(5734661160329036846)
XLA Ops:
  0.0 1.1 shard_map.128
  1.1 0.1 collective-permute-start
  1.2 0.0 copy-start.7
  1.2 0.0 copy-start.8
  1.2 4.4 %collective-permute-start.1 = (bf16[2,72,1024]{2,1,0:T(8,128)(2,1)S(1)}, bf16[2,72,1024]{2,1,0:T(8,128)(2,1)S(1)}, u32[]{:S(2)}, u32[]{:S(2)}) collective-permute-start(bf16[2,72,1024]{2,1,0:T(8,128)(2,1)S(1)} %get-tuple-element.25), channel_id=1, source_target_pairs={{1,2},{2,1},{3,4},{4,3},{5,6},{6,5},{9,10},{10,9},{11,12},{12,11},... | collective-permute-start | bytes 884744 | tf_op jit(solution)/shard_map/ppermute | solution.py:398
  5.6 3.3 %shard_map.127 = (f32[8,72,1024]{2,1,0:T(8,128)S(1)}, f32[2,1024]{1,0:T(2,128)S(1)}, bf16[12,72,1024]{2,1,0:T(8,128)(2,1)S(1)}, bf16[3,3,1024]{2,1,0:T(4,128)(2,1)S(1)}, bf16[1024,1536]{1,0:T(8,128)(2,1)S(1)}) custom-call(bf16[1,12,72,1024]{3,2,1,0:T(8,128)(2,1)} %x_hbm.3, bf16[3,3,1024]{2,1,0:T(4,128)(2,1)} %filter_hbm.1, bf16[1024,1536]{1,0:T(8,128)(2,1)} %weight_hbm.2), custom_call_target="tpu_custom_call" | custom-call | flops 11796480 | bytes 5308416 | tf_op jit(solution)/shard_map/pallas_call | solution.py:270
  8.9 0.0 collective-permute-done.chip_ref
  8.9 1.1 collective-permute-done.1.cross_ref
  10.0 1.4 %shard_map.129 = (f32[4,72,1024]{2,1,0:T(8,128)S(1)}, f32[2,1024]{1,0:T(2,128)S(1)}) custom-call(bf16[12,72,1024]{2,1,0:T(8,128)(2,1)S(1)} %get-tuple-element.23.x_ref, bf16[2,72,1024]{2,1,0:T(8,128)(2,1)S(1)} %collective-permute-done.chip_ref, bf16[2,72,1024]{2,1,0:T(8,128)(2,1)S(1)} %collective-permute-done.1.cross_ref, ...), custom_call_target="tpu_custom_call" | custom-call | flops 5898240 | bytes 2949120 | tf_op jit(solution)/shard_map/pallas_call | solution.py:307
  11.4 0.2 collective-permute-start.2
  11.6 1.1 collective-permute-done.2.other_ref
  12.7 13.4 %all_to_all.40.parts_ref = f32[16,2,1024]{2,1,0:T(2,128)S(1)} all-to-all(f32[16,2,1024]{2,1,0:T(2,128)S(1)} %shard_map.130), channel_id=1, replica_groups=mesh['batch_0'=8,'batch_1'=4,'space_0'=4,'space_1'=2] {'batch_1','space_0'}, dimensions={0} | all-to-all | bytes 262144 | tf_op jit(solution)/shard_map/all_to_all | solution.py:389
  26.1 0.1 shard_map.131
  26.1 16.6 %all_to_all.41.refs_2_ = f32[8,2,1024]{2,1,0:T(2,128)S(1)} all-to-all(f32[8,2,1024]{2,1,0:T(2,128)S(1)} %shard_map.131), channel_id=1, replica_groups=mesh['batch_0'=8,'batch_1'=4,'space_0'=4,'space_1'=2] {'batch_0'}, dimensions={0} | all-to-all | bytes 131072 | tf_op jit(solution)/shard_map/all_to_all | solution.py:392
  42.8 0.0 copy-done.7
  42.8 0.0 copy-done.8
  42.8 0.0 copy-start
  42.8 0.0 copy-start.1
  42.8 0.0 copy-start.2
  42.8 3.9 %shard_map.132 = (f32[12,72,1536]{2,1,0:T(8,128)S(1)}, f32[2,1536]{1,0:T(2,128)S(1)}, bf16[2,80,1536]{2,1,0:T(8,128)(2,1)S(1)}, bf16[2,80,1536]{2,1,0:T(8,128)(2,1)S(1)}) custom-call(f32[4,72,1024]{2,1,0:T(8,128)S(1)} %get-tuple-element.28.refs_0_, f32[8,72,1024]{2,1,0:T(8,128)S(1)} %get-tuple-element.29.refs_1_, f32[8,2,1024]{2,1,0:T(2,128)S(1)} %all_to_all.41.refs_2_, ...), custom_call_target="tpu_custom_call" | custom-call | flops 2717908992 | bytes 11993088 | tf_op jit(solution)/shard_map/pallas_call | solution.py:323
  46.7 0.1 collective-permute-start.3
  46.8 3.5 %collective-permute-start.4 = (bf16[2,80,1536]{2,1,0:T(8,128)(2,1)S(1)}, bf16[2,80,1536]{2,1,0:T(8,128)(2,1)S(1)}, u32[]{:S(2)}, u32[]{:S(2)}) collective-permute-start(bf16[2,80,1536]{2,1,0:T(8,128)(2,1)S(1)} %get-tuple-element.34), channel_id=1, source_target_pairs={{1,2},{2,1},{3,4},{4,3},{5,6},{6,5},{9,10},{10,9},{11,12},{12,11},... | collective-permute-start | bytes 1474568 | tf_op jit(solution)/shard_map/ppermute | solution.py:398
  50.3 0.1 collective-permute-start.5
  50.4 1.2 collective-permute-done.5.other_ref
  51.5 11.1 %all_to_all.42.parts_ref = f32[16,2,1536]{2,1,0:T(2,128)S(1)} all-to-all(f32[16,2,1536]{2,1,0:T(2,128)S(1)} %shard_map.133), channel_id=1, replica_groups=mesh['batch_0'=8,'batch_1'=4,'space_0'=4,'space_1'=2] {'batch_1','space_0'}, dimensions={0} | all-to-all | bytes 393216 | tf_op jit(solution)/shard_map/all_to_all | solution.py:389
  62.6 0.1 shard_map.134
  62.7 11.1 %all_to_all.43.parts_ref = f32[8,2,1536]{2,1,0:T(2,128)S(1)} all-to-all(f32[8,2,1536]{2,1,0:T(2,128)S(1)} %shard_map.134), channel_id=1, replica_groups=mesh['batch_0'=8,'batch_1'=4,'space_0'=4,'space_1'=2] {'batch_0'}, dimensions={0} | all-to-all | bytes 196608 | tf_op jit(solution)/shard_map/all_to_all | solution.py:392
  73.8 0.0 collective-permute-done.3.chip_ref
  73.8 0.0 collective-permute-done.4.cross_ref
  73.8 0.0 copy-done
  73.8 0.0 copy-done.1
  73.8 0.0 copy-done.2
  73.8 0.0 copy-start.5
  73.9 0.0 copy-start.6
  73.9 5.3 %shard_map.135 = (f32[12,72,1536]{2,1,0:T(8,128)S(1)}, f32[2,1536]{1,0:T(2,128)S(1)}, bf16[1536,2048]{1,0:T(8,128)(2,1)S(1)}) custom-call(f32[12,72,1536]{2,1,0:T(8,128)S(1)} %get-tuple-element.32.u_ref, bf16[2,80,1536]{2,1,0:T(8,128)(2,1)S(1)} %collective-permute-done.3.chip_ref, bf16[2,80,1536]{2,1,0:T(8,128)(2,1)S(1)} %collective-permute-done.4.cross_ref, ...), custom_call_target="tpu_custom_call" | custom-call | flops 34504704 | bytes 10616832 | tf_op jit(solution)/shard_map/pallas_call | solution.py:343
  79.1 0.1 collective-permute-start.6
  79.2 1.2 collective-permute-done.6.other_ref
  80.4 11.3 %all_to_all.44.parts_ref = f32[16,2,1536]{2,1,0:T(2,128)S(1)} all-to-all(f32[16,2,1536]{2,1,0:T(2,128)S(1)} %shard_map.136), channel_id=1, replica_groups=mesh['batch_0'=8,'batch_1'=4,'space_0'=4,'space_1'=2] {'batch_1','space_0'}, dimensions={0} | all-to-all | bytes 393216 | tf_op jit(solution)/shard_map/all_to_all | solution.py:389
  91.8 0.1 shard_map.137
  91.9 11.1 %all_to_all.45.refs_1_ = f32[8,2,1536]{2,1,0:T(2,128)S(1)} all-to-all(f32[8,2,1536]{2,1,0:T(2,128)S(1)} %shard_map.137), channel_id=1, replica_groups=mesh['batch_0'=8,'batch_1'=4,'space_0'=4,'space_1'=2] {'batch_0'}, dimensions={0} | all-to-all | bytes 196608 | tf_op jit(solution)/shard_map/all_to_all | solution.py:392
  103.0 0.0 copy-done.5
  103.0 0.0 copy-done.6
  103.0 0.0 copy-start.3
  103.0 0.0 copy-start.4
  103.0 6.9 %shard_map.138 = (f32[12,72,2048]{2,1,0:T(8,128)S(1)}, f32[2,2048]{1,0:T(2,128)S(1)}) custom-call(f32[12,72,1536]{2,1,0:T(8,128)S(1)} %get-tuple-element.36.refs_0_, f32[8,2,1536]{2,1,0:T(2,128)S(1)} %all_to_all.45.refs_1_, f32[12,128]{1,0:T(8,128)S(1)} %bitcast.12, f32[12,128]{1,0:T(8,128)S(1)} %bitcast.13, bf16[1536,2048]{1,0:T(8,128)(2,1)S(1)} %get-tuple-element.38.refs_4_), custom_call_target="tpu_custom_call" | custom-call | flops 5435817984 | bytes 18677760 | tf_op jit(solution)/shard_map/pallas_call | solution.py:323
  109.9 0.1 collective-permute-start.7
  110.0 1.2 collective-permute-done.7.other_ref
  111.2 12.0 %all_to_all.46.parts_ref = f32[16,2,2048]{2,1,0:T(2,128)S(1)} all-to-all(f32[16,2,2048]{2,1,0:T(2,128)S(1)} %shard_map.139), channel_id=1, replica_groups=mesh['batch_0'=8,'batch_1'=4,'space_0'=4,'space_1'=2] {'batch_1','space_0'}, dimensions={0} | all-to-all | bytes 524288 | tf_op jit(solution)/shard_map/all_to_all | solution.py:389
  123.2 0.1 shard_map.140
  123.3 11.5 %all_to_all.47.parts_ref = f32[8,2,2048]{2,1,0:T(2,128)S(1)} all-to-all(f32[8,2,2048]{2,1,0:T(2,128)S(1)} %shard_map.140), channel_id=1, replica_groups=mesh['batch_0'=8,'batch_1'=4,'space_0'=4,'space_1'=2] {'batch_0'}, dimensions={0} | all-to-all | bytes 262144 | tf_op jit(solution)/shard_map/all_to_all | solution.py:392
  134.8 0.0 copy-done.3
  134.8 0.0 copy-done.4
  134.8 2.6 %shard_map.141 = bf16[1,12,72,2048]{3,2,1,0:T(8,128)(2,1)} custom-call(f32[12,72,2048]{2,1,0:T(8,128)S(1)} %get-tuple-element.39.u_ref, f32[8,2,2048]{2,1,0:T(2,128)S(1)} %all_to_all.47.parts_ref, f32[16,128]{1,0:T(8,128)S(1)} %bitcast.10, f32[16,128]{1,0:T(8,128)S(1)} %bitcast.11), custom_call_target="tpu_custom_call" | custom-call | flops 5308416 | bytes 10616832 | tf_op jit(solution)/shard_map/pallas_call | solution.py:362
  (4 shorter events, 0.1 us)
Async XLA Ops:
  1.1 7.8 %collective-permute-start = (bf16[2,72,1024]{2,1,0:T(8,128)(2,1)S(1)}, bf16[2,72,1024]{2,1,0:T(8,128)(2,1)S(1)}, u32[]{:S(2)}, u32[]{:S(2)}) collective-permute-start(bf16[2,72,1024]{2,1,0:T(8,128)(2,1)S(1)} %get-tuple-element.24), channel_id=1, source_target_pairs={{0,1},{1,0},{2,3},{3,2},{4,5},{5,4},{6,7},{7,6},{8,9},{9,8},{10,11... | collective-permute-start | bytes 884744 | tf_op jit(solution)/shard_map/ppermute | solution.py:397
  1.2 41.6 %copy-start.7 = (f32[1024]{0:T(1024)S(1)}, f32[1024]{0:T(1024)}, u32[]{:S(2)}) copy-start(f32[1024]{0:T(1024)} %param.15) | copy-start | bytes 12292
  1.2 41.6 %copy-start.8 = (f32[1024]{0:T(1024)S(1)}, f32[1024]{0:T(1024)}, u32[]{:S(2)}) copy-start(f32[1024]{0:T(1024)} %param.16) | copy-start | bytes 12292
  1.2 8.8 %collective-permute-start.1 = (bf16[2,72,1024]{2,1,0:T(8,128)(2,1)S(1)}, bf16[2,72,1024]{2,1,0:T(8,128)(2,1)S(1)}, u32[]{:S(2)}, u32[]{:S(2)}) collective-permute-start(bf16[2,72,1024]{2,1,0:T(8,128)(2,1)S(1)} %get-tuple-element.25), channel_id=1, source_target_pairs={{1,2},{2,1},{3,4},{4,3},{5,6},{6,5},{9,10},{10,9},{11,12},{12,11},... | collective-permute-start | bytes 884744 | tf_op jit(solution)/shard_map/ppermute | solution.py:398
  11.4 1.3 collective-permute-start.2
  42.8 31.0 %copy-start = (bf16[3,3,1536]{2,1,0:T(4,128)(2,1)S(1)}, bf16[3,3,1536]{2,1,0:T(4,128)(2,1)}, u32[]{:S(2)}) copy-start(bf16[3,3,1536]{2,1,0:T(4,128)(2,1)} %filter_ref.1) | copy-start | bytes 82948
  42.8 31.0 %copy-start.1 = (f32[1536]{0:T(1024)S(1)}, f32[1536]{0:T(1024)}, u32[]{:S(2)}) copy-start(f32[1536]{0:T(1024)} %param.18) | copy-start | bytes 18436
  42.8 31.0 %copy-start.2 = (f32[1536]{0:T(1024)S(1)}, f32[1536]{0:T(1024)}, u32[]{:S(2)}) copy-start(f32[1536]{0:T(1024)} %param.19) | copy-start | bytes 18436
  46.7 27.1 %collective-permute-start.3 = (bf16[2,80,1536]{2,1,0:T(8,128)(2,1)S(1)}, bf16[2,80,1536]{2,1,0:T(8,128)(2,1)S(1)}, u32[]{:S(2)}, u32[]{:S(2)}) collective-permute-start(bf16[2,80,1536]{2,1,0:T(8,128)(2,1)S(1)} %get-tuple-element.33), channel_id=1, source_target_pairs={{0,1},{1,0},{2,3},{3,2},{4,5},{5,4},{6,7},{7,6},{8,9},{9,8},{10,11... | collective-permute-start | bytes 1474568 | tf_op jit(solution)/shard_map/ppermute | solution.py:397
  46.8 27.0 %collective-permute-start.4 = (bf16[2,80,1536]{2,1,0:T(8,128)(2,1)S(1)}, bf16[2,80,1536]{2,1,0:T(8,128)(2,1)S(1)}, u32[]{:S(2)}, u32[]{:S(2)}) collective-permute-start(bf16[2,80,1536]{2,1,0:T(8,128)(2,1)S(1)} %get-tuple-element.34), channel_id=1, source_target_pairs={{1,2},{2,1},{3,4},{4,3},{5,6},{6,5},{9,10},{10,9},{11,12},{12,11},... | collective-permute-start | bytes 1474568 | tf_op jit(solution)/shard_map/ppermute | solution.py:398
  50.3 1.3 collective-permute-start.5
  73.8 29.1 %copy-start.5 = (f32[1536]{0:T(1024)S(1)}, f32[1536]{0:T(1024)}, u32[]{:S(2)}) copy-start(f32[1536]{0:T(1024)} %param.21) | copy-start | bytes 18436
  73.9 29.1 %copy-start.6 = (f32[1536]{0:T(1024)S(1)}, f32[1536]{0:T(1024)}, u32[]{:S(2)}) copy-start(f32[1536]{0:T(1024)} %param.22) | copy-start | bytes 18436
  79.1 1.3 collective-permute-start.6
  103.0 31.8 %copy-start.3 = (f32[2048]{0:T(1024)S(1)}, f32[2048]{0:T(1024)}, u32[]{:S(2)}) copy-start(f32[2048]{0:T(1024)} %param.24) | copy-start | bytes 24580
  103.0 31.8 %copy-start.4 = (f32[2048]{0:T(1024)S(1)}, f32[2048]{0:T(1024)}, u32[]{:S(2)}) copy-start(f32[2048]{0:T(1024)} %param.25) | copy-start | bytes 24580
  109.9 1.3 collective-permute-start.7

commit v4 on v3

v4 whole, which is shorter than its diff:
```python
import functools

import jax
import jax.numpy as jnp
from jax import lax
from jax.experimental import pallas as pl
from jax.experimental.pallas import tpu as pltpu
from jax.sharding import Mesh
from jax.sharding import PartitionSpec as P

RATE = 2
LANES = 128
BATCH = ("batch_0", "batch_1")
SPACE = ("space_0", "space_1")

epsilon = 1e-05

VMEM = pl.BlockSpec(memory_space=pltpu.VMEM)
HBM = pl.BlockSpec(memory_space=pltpu.HBM)


def kernel_call(body, outs, n_in, limit, scratch=(), flops=0, moved=0):
    return pl.pallas_call(
        body,
        out_shape=[pltpu.VMEM(shape, dtype) for shape, dtype in outs],
        in_specs=[VMEM] * n_in,
        out_specs=[VMEM] * len(outs),
        scratch_shapes=list(scratch),
        compiler_params=pltpu.CompilerParams(vmem_limit_bytes=limit),
        cost_estimate=pl.CostEstimate(flops=flops, bytes_accessed=moved, transcendentals=0),
    )


def moved_down(row):
    gap = jnp.zeros((RATE, row.shape[1]), row.dtype)
    return jnp.concatenate([gap, row[: row.shape[0] - RATE]], axis=0)


def moved_up(row):
    gap = jnp.zeros((RATE, row.shape[1]), row.dtype)
    return jnp.concatenate([row[RATE:], gap], axis=0)


def taps_of(filter_ref, lanes):
    return [filter_ref[tap, :, lanes].astype(jnp.float32) for tap in range(3)]


def dilated_row(rows, taps):
    sides = []
    for tap_col in range(3):
        side = None
        for tap_row in range(3):
            term = rows[tap_row] * taps[tap_row][tap_col : tap_col + 1]
            side = term if side is None else side + term
        sides.append(side)
    return sides[1] + moved_down(sides[0]) + moved_up(sides[2])


def summed_rows(value):
    return jnp.sum(value.reshape(value.shape[0] // 8, 8, value.shape[1]), axis=0)


def store_sums(sums_ref, lanes, total, squares):
    sums_ref[0:1, lanes] = jnp.sum(total, axis=0, keepdims=True)
    sums_ref[1:2, lanes] = jnp.sum(squares, axis=0, keepdims=True)


def dilated_rows(row_at, rows, taps, out_ref, lanes):
    total = squares = None
    for place, row in sorted(enumerate(rows), key=lambda pair: (pair[1] % 2, pair[1])):
        value = dilated_row([row_at(row - RATE), row_at(row), row_at(row + RATE)], taps)
        out_ref[place, :, lanes] = value
        part, part_squares = summed_rows(value), summed_rows(value * value)
        total = part if total is None else total + part
        squares = part_squares if squares is None else squares + part_squares
    return total, squares


def inner_body(x_ref, filter_ref, weight_hbm, out_ref, sums_ref, weight_ref, arrived):
    count = x_ref.shape[0]
    weight_copy = pltpu.make_async_copy(weight_hbm, weight_ref, arrived)
    weight_copy.start()

    @pl.loop(0, x_ref.shape[2] // LANES)
    def _(block):
        lanes = pl.ds(pl.multiple_of(block * LANES, LANES), LANES)
        total, squares = dilated_rows(
            functools.cache(lambda row: x_ref[row, :, lanes].astype(jnp.float32)),
            range(RATE, count - RATE),
            taps_of(filter_ref, lanes),
            out_ref,
            lanes,
        )
        store_sums(sums_ref, lanes, total, squares)

    weight_copy.wait()


def edge_starts(count):
    core = lax.axis_index("space_1")
    return (
        (1 - core) * (count - 2 * RATE),
        core * (count - RATE),
        RATE + core * (count - 3 * RATE),
    )


def load_body(x_hbm, filter_hbm, chip_ref, near_ref, far_ref, x_ref, filter_ref, arrived):
    starts = edge_starts(x_hbm.shape[1])
    copies = [
        pltpu.make_async_copy(
            x_hbm.at[0, pl.ds(start, out_ref.shape[0])], out_ref, arrived.at[place]
        )
        for place, (start, out_ref) in enumerate(zip(starts, (chip_ref, near_ref, far_ref)))
    ]
    copies.append(pltpu.make_async_copy(x_hbm.at[0], x_ref, arrived.at[3]))
    copies.append(pltpu.make_async_copy(filter_hbm, filter_ref, arrived.at[4]))
    for copy in copies:
        copy.start()
    for copy in copies:
        copy.wait()


def halo_row(chip_ref, near_ref, far_ref, row, count, lanes):
    core = lax.axis_index("space_1")
    if row < 0:
        chip_holds, chip_row = core == 1, row + 2 * RATE
        cross_ref, cross_row = (near_ref, row + RATE) if row >= -RATE else (far_ref, row + 2 * RATE)
    else:
        chip_holds, chip_row = core == 0, row - count
        cross_ref, cross_row = (
            (near_ref, row - count) if row < count + RATE else (far_ref, row - count - RATE)
        )
    value = jnp.where(chip_holds, chip_ref[chip_row, :, lanes], cross_ref[cross_row, :, lanes])
    return value.astype(jnp.float32)


def edge_body(x_ref, chip_ref, near_ref, filter_ref, inner_ref, out_ref, sums_ref):
    count = x_ref.shape[0]

    @pl.loop(0, x_ref.shape[2] // LANES)
    def _(block):
        lanes = pl.ds(pl.multiple_of(block * LANES, LANES), LANES)

        @functools.cache
        def row_at(row):
            if 0 <= row < count:
                return x_ref[row, :, lanes].astype(jnp.float32)
            return halo_row(chip_ref, near_ref, None, row, count, lanes)

        rows = (*range(RATE), *range(count - RATE, count))
        total, squares = dilated_rows(row_at, rows, taps_of(filter_ref, lanes), out_ref, lanes)
        store_sums(sums_ref, lanes, total, squares)
        sums_ref[:, lanes] = sums_ref[:, lanes] + inner_ref[:, lanes]


def outer_body(x_ref, chip_ref, near_ref, far_ref, filter_ref, out_ref):
    count = x_ref.shape[0]

    @pl.loop(0, x_ref.shape[2] // LANES)
    def _(block):
        lanes = pl.ds(pl.multiple_of(block * LANES, LANES), LANES)
        taps = taps_of(filter_ref, lanes)

        @functools.cache
        def row_at(row):
            if 0 <= row < count:
                return x_ref[row, :, lanes].astype(jnp.float32)
            return halo_row(chip_ref, near_ref, far_ref, row, count, lanes)

        for place, row in enumerate((*range(-RATE, 0), *range(count, count + RATE))):
            rows = [row_at(row - RATE), row_at(row), row_at(row + RATE)]
            out_ref[place, :, lanes] = dilated_row(rows, taps)


def store_terms(terms_ref, parts_ref, gain_ref, shift_ref, pixels):
    for block in range(gain_ref.shape[0]):
        lanes = slice(block * LANES, (block + 1) * LANES)
        sums = jnp.sum(parts_ref[:, :, lanes], axis=0)
        average = sums[0:1] / pixels
        variance = sums[1:2] / pixels - average * average
        factor = gain_ref[block : block + 1] * lax.rsqrt(variance + epsilon)
        terms_ref[0:1, lanes] = factor
        terms_ref[1:2, lanes] = shift_ref[block : block + 1] - average * factor


def third_body(
    pixels, u_ref, outer_ref, parts_ref, gain_ref, shift_ref, filter_ref,
    weight_hbm, out_ref, sums_ref, weight_ref, terms_ref, arrived,
):
    count = u_ref.shape[0]
    weight_copy = pltpu.make_async_copy(weight_hbm, weight_ref, arrived)
    weight_copy.start()
    store_terms(terms_ref, parts_ref, gain_ref, shift_ref, pixels)

    @pl.loop(0, u_ref.shape[2] // LANES)
    def _(block):
        lanes = pl.ds(pl.multiple_of(block * LANES, LANES), LANES)
        taps = taps_of(filter_ref, lanes)
        factor = terms_ref[0:1, lanes]
        offset = terms_ref[1:2, lanes]
        strip = lax.axis_index(SPACE)
        above = (strip > 0).astype(jnp.float32)
        below = (strip < lax.axis_size(SPACE) - 1).astype(jnp.float32)

        @functools.cache
        def row_at(row):
            if row < 0:
                value = outer_ref[row + RATE, :, lanes]
                value = value * (factor * above) + offset * above
            elif row >= count:
                value = outer_ref[row - count + RATE, :, lanes]
                value = value * (factor * below) + offset * below
            else:
                value = u_ref[row, :, lanes] * factor + offset
            return jnp.maximum(value, 0.0).astype(jnp.bfloat16).astype(jnp.float32)

        total, squares = dilated_rows(row_at, range(count), taps, out_ref, lanes)
        store_sums(sums_ref, lanes, total, squares)

    weight_copy.wait()


def project_body(pixels, places, n_parts, *refs):
    part_refs = refs[:n_parts]
    parts_ref, gain_ref, shift_ref, weight_ref, out_ref, sums_ref = refs[n_parts : n_parts + 6]
    terms_ref, act_ref = refs[n_parts + 6 :]
    count, cols, width = out_ref.shape
    depth = act_ref.shape[1]
    wide = 512
    store_terms(terms_ref, parts_ref, gain_ref, shift_ref, pixels)
    pair = 2
    for u_ref, first_row in zip(part_refs, places):

        @pl.loop(0, u_ref.shape[0] // pair)
        def _(step):
            factor = terms_ref[0:1]
            offset = terms_ref[1:2]
            value = u_ref[pl.ds(step * pair, pair)].reshape(pair * cols, depth)
            row = first_row + step * pair
            if len(places) > 1 and first_row == 0:
                row = step * (count - pair)
            act_ref[pl.ds(pl.multiple_of(row * cols, pair * cols), pair * cols)] = jnp.maximum(
                value * factor + offset, 0.0
            ).astype(jnp.bfloat16)

    @pl.loop(0, width // wide)
    def _(block):
        lanes = pl.ds(pl.multiple_of(block * wide, wide), wide)
        result = jnp.dot(act_ref[...], weight_ref[:, lanes], preferred_element_type=jnp.float32)
        store_sums(sums_ref, lanes, summed_rows(result), summed_rows(result * result))
        out_ref[:, :, lanes] = result.reshape(count, cols, wide)


def outer_project_body(pixels, u_ref, parts_ref, gain_ref, shift_ref, weight_ref, out_ref, terms_ref, act_ref):
    count, cols, width = out_ref.shape
    wide = 512
    store_terms(terms_ref, parts_ref, gain_ref, shift_ref, pixels)
    value = u_ref[...].reshape(count * cols, u_ref.shape[2])
    act_ref[...] = jnp.maximum(value * terms_ref[0:1] + terms_ref[1:2], 0.0).astype(jnp.bfloat16)

    @pl.loop(0, width // wide)
    def _(block):
        lanes = pl.ds(pl.multiple_of(block * wide, wide), wide)
        result = jnp.dot(act_ref[...], weight_ref[:, lanes], preferred_element_type=jnp.float32)
        out_ref[:, :, lanes] = result.reshape(count, cols, wide)


def last_body(pixels, u_ref, parts_ref, gain_ref, shift_ref, out_hbm, terms_ref, rows_ref, sent):
    store_terms(terms_ref, parts_ref, gain_ref, shift_ref, pixels)

    def piece(row):
        return pltpu.make_async_copy(rows_ref.at[row], out_hbm.at[0, row], sent.at[row])

    @pl.loop(0, u_ref.shape[0])
    def _(row):
        value = u_ref[row] * terms_ref[0:1] + terms_ref[1:2]
        rows_ref[row] = jnp.maximum(value, 0.0).astype(jnp.bfloat16)
        piece(row).start()

    @pl.loop(0, u_ref.shape[0])
    def _(row):
        piece(row).wait()


def dilated_inner(x, taps, weight):
    rows, cols, depth = x.shape
    inner = rows - 2 * RATE
    return pl.pallas_call(
        inner_body,
        out_shape=[
            pltpu.VMEM((inner, cols, depth), jnp.float32),
            pltpu.VMEM((2, depth), jnp.float32),
            pltpu.VMEM(weight.shape, weight.dtype),
        ],
        in_specs=[VMEM] * 2 + [HBM],
        out_specs=[VMEM] * 3,
        scratch_shapes=[pltpu.SemaphoreType.DMA],
        compiler_params=pltpu.CompilerParams(vmem_limit_bytes=12 << 20),
        cost_estimate=pl.CostEstimate(
            flops=20 * inner * cols * depth, bytes_accessed=6 * rows * cols * depth, transcendentals=0
        ),
    )(x, taps, weight)


def kept_in_hbm(array):
    return pltpu.with_memory_space_constraint(array, pltpu.HBM)


def loaded(x, taps):
    edges = [(count,) + x.shape[2:] for count in (2 * RATE, RATE, RATE)]
    return pl.pallas_call(
        load_body,
        out_shape=[pltpu.VMEM(shape, x.dtype) for shape in (*edges, x.shape[1:], taps.shape)],
        in_specs=[HBM] * 2,
        out_specs=[VMEM] * 5,
        scratch_shapes=[pltpu.SemaphoreType.DMA((5,))],
        compiler_params=pltpu.CompilerParams(vmem_limit_bytes=4 << 20),
    )(x, taps)


def dilated_edges(x, chip, near, weight, inner_sums):
    cols, depth = x.shape[1:]
    return kernel_call(
        edge_body,
        [((2 * RATE, cols, depth), jnp.float32), ((2, depth), jnp.float32)],
        5,
        12 << 20,
        flops=40 * RATE * cols * depth,
        moved=20 * RATE * cols * depth,
    )(x, chip, near, weight, inner_sums)


def project(pixels, pieces, places, parts, gain, shift, weight):
    rows = sum(piece.shape[0] for piece in pieces)
    cols, depth = pieces[0].shape[1:]
    width = weight.shape[1]
    outs = [((rows, cols, width), jnp.float32), ((2, width), jnp.float32)]
    return pl.pallas_call(
        functools.partial(project_body, pixels, places, len(pieces)),
        out_shape=[pltpu.VMEM(shape, dtype) for shape, dtype in outs],
        in_specs=[VMEM] * (len(pieces) + 4),
        out_specs=[VMEM] * len(outs),
        scratch_shapes=[
            pltpu.VMEM((2, depth), jnp.float32),
            pltpu.VMEM((rows * cols, depth), jnp.bfloat16),
        ],
        compiler_params=pltpu.CompilerParams(vmem_limit_bytes=24 << 20),
        cost_estimate=pl.CostEstimate(
            flops=2 * rows * cols * depth * width,
            bytes_accessed=4 * rows * cols * (depth + width) + 2 * depth * width,
            transcendentals=0,
        ),
    )(*pieces, parts, gain, shift, weight)


def dilated_outer(x, chip, near, far, taps):
    cols, depth = x.shape[1:]
    (outer,) = kernel_call(
        outer_body,
        [((2 * RATE, cols, depth), jnp.float32)],
        5,
        8 << 20,
        flops=36 * RATE * cols * depth,
        moved=20 * RATE * cols * depth,
    )(x, chip, near, far, taps)
    return outer


def project_outer(pixels, u, parts, gain, shift, weight):
    rows, cols, depth = u.shape
    width = weight.shape[1]
    (outer,) = kernel_call(
        functools.partial(outer_project_body, pixels),
        [((rows, cols, width), jnp.float32)],
        5,
        12 << 20,
        scratch=[pltpu.VMEM((2, depth), jnp.float32), pltpu.VMEM((rows * cols, depth), jnp.bfloat16)],
        flops=2 * rows * cols * depth * width,
        moved=4 * rows * cols * (depth + width) + 2 * depth * width,
    )(u, parts, gain, shift, weight)
    return outer


def dilated_second(pixels, u, outer, parts, gain, shift, taps, weight):
    rows, cols, depth = u.shape
    return pl.pallas_call(
        functools.partial(third_body, pixels),
        out_shape=[
            pltpu.VMEM((rows, cols, depth), jnp.float32),
            pltpu.VMEM((2, depth), jnp.float32),
            pltpu.VMEM(weight.shape, weight.dtype),
        ],
        in_specs=[VMEM] * 6 + [HBM],
        out_specs=[VMEM] * 3,
        scratch_shapes=[pltpu.VMEM((2, depth), jnp.float32), pltpu.SemaphoreType.DMA],
        compiler_params=pltpu.CompilerParams(vmem_limit_bytes=16 << 20),
        cost_estimate=pl.CostEstimate(
            flops=26 * rows * cols * depth, bytes_accessed=8 * rows * cols * depth, transcendentals=0
        ),
    )(u, outer, parts, gain, shift, taps, weight)


def last_norm(pixels, u, parts, gain, shift):
    rows, cols, depth = u.shape
    return pl.pallas_call(
        functools.partial(last_body, pixels),
        out_shape=jax.ShapeDtypeStruct((1, rows, cols, depth), jnp.bfloat16),
        in_specs=[VMEM] * 4,
        out_specs=HBM,
        scratch_shapes=[
            pltpu.VMEM((2, depth), jnp.float32),
            pltpu.VMEM((rows, cols, depth), jnp.bfloat16),
            pltpu.SemaphoreType.DMA((rows,)),
        ],
        compiler_params=pltpu.CompilerParams(vmem_limit_bytes=16 << 20),
        cost_estimate=pl.CostEstimate(
            flops=3 * rows * cols * depth, bytes_accessed=6 * rows * cols * depth, transcendentals=0
        ),
    )(u, parts, gain, shift)


def pair_body(own_ref, other_ref, out_ref):
    out_ref[...] = jnp.broadcast_to((own_ref[...] + other_ref[...])[None], out_ref.shape)


def group_body(parts_ref, out_ref):
    out_ref[...] = jnp.broadcast_to(jnp.sum(parts_ref[...], axis=0)[None], out_ref.shape)


def gathered_sums(value, beside=None):
    plane, line = ("batch_1", "space_0"), ("batch_0",)
    other = lax.ppermute(value, "space_1", [(0, 1), (1, 0)])
    if beside is not None:
        other, beside = lax.optimization_barrier((other, beside))
    shape = (lax.axis_size(plane),) + value.shape
    (copies,) = kernel_call(pair_body, [(shape, jnp.float32)], 2, 2 << 20)(value, other)
    parts = lax.all_to_all(copies, plane, 0, 0)
    shape = (lax.axis_size(line),) + value.shape
    (copies,) = kernel_call(group_body, [(shape, jnp.float32)], 1, 2 << 20)(parts)
    return lax.all_to_all(copies, line, 0, 0), beside


def from_neighbours(chip, near, far):
    ends = [pair for i in range(1, lax.axis_size(SPACE) - 1, 2) for pair in ((i, i + 1), (i + 1, i))]
    near = lax.ppermute(near, SPACE, ends)
    chip = lax.ppermute(chip, "space_1", [(0, 1), (1, 0)])
    return chip, near, lax.ppermute(far, SPACE, ends)


def per_device(
    features,
    depth_one,
    gain_one,
    shift_one,
    point_one,
    gain_two,
    shift_two,
    depth_two,
    gain_three,
    shift_three,
    point_two,
    gain_four,
    shift_four,
):
    rows, cols = features.shape[1:3]
    pixels = rows * cols * lax.axis_size(BATCH) * lax.axis_size(SPACE)
    names = (gain_one, shift_one, gain_two, shift_two, gain_three, shift_three, gain_four, shift_four)
    terms = [term.reshape(-1, LANES) for term in names]
    chip, near, far, x, taps = loaded(kept_in_hbm(features), kept_in_hbm(depth_one))
    chip, near, far = from_neighbours(chip, near, far)
    inner, inner_sums, weight = dilated_inner(x, taps, kept_in_hbm(point_one))
    edges, sums = dilated_edges(x, chip, near, taps, inner_sums)
    parts, outer = gathered_sums(sums, dilated_outer(x, chip, near, far, taps))
    second, sums = project(pixels, (edges, inner), (0, RATE), parts, *terms[0:2], weight)
    outer = project_outer(pixels, outer, parts, *terms[0:2], weight)
    parts, outer = gathered_sums(sums, outer)
    third, sums, weight = dilated_second(
        pixels, second, outer, parts, *terms[2:4], depth_two, kept_in_hbm(point_two)
    )
    parts, _ = gathered_sums(sums)
    fourth, sums = project(pixels, (third,), (0,), parts, *terms[4:6], weight)
    parts, _ = gathered_sums(sums)
    return last_norm(pixels, fourth, parts, *terms[6:8])


def solution(mesh):
    finer = Mesh(mesh.devices.reshape(8, 4, 4, 2), ("batch_0", "batch_1", "space_0", "space_1"))
    placed = (P(BATCH, SPACE, None, None),) + (P(),) * 12
    return jax.shard_map(
        per_device,
        mesh=finer,
        in_specs=placed,
        out_specs=P(BATCH, SPACE, None, None),
        check_vma=False,
    )
```

time: 138 us -> 137 us (level)
  Pallas kernels: 24.8 us -> 26.8 us
  starting transfers between devices: 8.49 us -> 6.76 us
    pallas_call x2 -> x4, Pallas kernels: 3.66 us -> 6.87 us  [the longest x1 2.03 us: last_norm(): pl.pallas_call(functools.partial(last_body, pixels), out_shape=jax.ShapeD...]
    ppermute x4, waiting for transfers between devices: 4.56 us -> 2.34 us  [gathered_sums(): other = lax.ppermute(value, 'space_1', [(0, 1), (1, 0)])]
    ppermute x2, starting transfers between devices: 7.83 us -> 6.19 us  [the longest x1 4.27 us: from_neighbours(): near = lax.ppermute(near, SPACE, ends)]
  transfers between devices with their start and end apart: 8 -> 7, of which waited for: 5 -> 4; matrix products, arithmetic and copies ran while one was open for 0% -> 0% of each run, Pallas kernels for 2% -> 5%
where the time goes in v4:
time: 137 us
  blocking collectives  98.1 us (72%)
  Pallas kernels  26.8 us (20%)
  starting transfers between devices  6.76 us (5%)
  waiting for transfers between devices  4.74 us (3%)
    all_to_all x4, blocking collectives, gathered_sums(): return (lax.all_to_all(copies, line, 0, 0), beside)  50.3 us
    all_to_all x4, blocking collectives, gathered_sums(): parts = lax.all_to_all(copies, plane, 0, 0)  47.8 us
    pallas_call x2, Pallas kernels, project(): pl.pallas_call(functools.partial(project_body, pixels, places, len(pieces...  10.6 us
    pallas_call x1, Pallas kernels, dilated_second(): pl.pallas_call(functools.partial(third_body, pixels), out_shape=[pltpu.VM...  5.42 us
    ppermute x1, starting transfers between devices, from_neighbours(): near = lax.ppermute(near, SPACE, ends)  4.27 us
  transfers between devices with their start and end apart: 7, of which 4 were waited for; matrix products, arithmetic and copies ran while one was open for 0% of the time, Pallas kernels for 5%

profile of v4, /device:TPU:2, one launch (start us, length us, event | category | flops | bytes accessed | tf_op | source)
XLA Modules:
  0.0 136.7 jit_solution(1318028984272007821)
XLA Ops:
  0.0 2.0 %shard_map.127 = (bf16[4,72,1024]{2,1,0:T(8,128)(2,1)S(1)}, bf16[2,72,1024]{2,1,0:T(8,128)(2,1)S(1)}, bf16[2,72,1024]{2,1,0:T(8,128)(2,1)S(1)}, bf16[12,72,1024]{2,1,0:T(8,128)(2,1)S(1)}, bf16[3,3,1024]{2,1,0:T(4,128)(2,1)S(1)}) custom-call(bf16[1,12,72,1024]{3,2,1,0:T(8,128)(2,1)} %x_hbm.1, bf16[3,3,1024]{2,1,0:T(4,128)(2,1)} %filter_hbm.1), custom_call_target="tpu_custom_call" | custom-call | tf_op jit(solution)/shard_map/pallas_call | solution.py:312
  2.0 0.1 collective-permute-start
  2.1 4.3 %collective-permute-start.1 = (bf16[2,72,1024]{2,1,0:T(8,128)(2,1)S(1)}, bf16[2,72,1024]{2,1,0:T(8,128)(2,1)S(1)}, u32[]{:S(2)}, u32[]{:S(2)}) collective-permute-start(bf16[2,72,1024]{2,1,0:T(8,128)(2,1)S(1)} %get-tuple-element.28), channel_id=1, source_target_pairs={{1,2},{2,1},{3,4},{4,3},{5,6},{6,5},{9,10},{10,9},{11,12},{12,11},... | collective-permute-start | bytes 884744 | tf_op jit(solution)/shard_map/ppermute | solution.py:446
  6.4 1.9 %collective-permute-start.3 = (bf16[2,72,1024]{2,1,0:T(8,128)(2,1)S(1)}, bf16[2,72,1024]{2,1,0:T(8,128)(2,1)S(1)}, u32[]{:S(2)}, u32[]{:S(2)}) collective-permute-start(bf16[2,72,1024]{2,1,0:T(8,128)(2,1)S(1)} %get-tuple-element.34), channel_id=1, source_target_pairs={{1,2},{2,1},{3,4},{4,3},{5,6},{6,5},{9,10},{10,9},{11,12},{12,11},... | collective-permute-start | bytes 884744 | tf_op jit(solution)/shard_map/ppermute | solution.py:448
  8.3 2.1 %shard_map.128 = (f32[8,72,1024]{2,1,0:T(8,128)S(1)}, f32[2,1024]{1,0:T(2,128)S(1)}, bf16[1024,1536]{1,0:T(8,128)(2,1)S(1)}) custom-call(bf16[12,72,1024]{2,1,0:T(8,128)(2,1)S(1)} %get-tuple-element.26.x_ref, bf16[3,3,1024]{2,1,0:T(4,128)(2,1)S(1)} %get-tuple-element.29.filter_ref, bf16[1024,1536]{1,0:T(8,128)(2,1)} %weight_hbm.2), custom_call_target="tpu_custom_call" | custom-call | flops 11796480 | bytes 5308416 | tf_op jit(solution)/shard_map/pallas_call | solution.py:289
  10.4 0.4 collective-permute-done.1.near_ref
  10.8 0.0 collective-permute-done.chip_ref
  10.8 0.0 copy-start.5
  10.8 0.0 copy-start.6
  10.8 1.4 %shard_map.129 = (f32[4,72,1024]{2,1,0:T(8,128)S(1)}, f32[2,1024]{1,0:T(2,128)S(1)}) custom-call(bf16[12,72,1024]{2,1,0:T(8,128)(2,1)S(1)} %get-tuple-element.26.x_ref, bf16[4,72,1024]{2,1,0:T(8,128)(2,1)S(1)} %collective-permute-done.chip_ref, bf16[2,72,1024]{2,1,0:T(8,128)(2,1)S(1)} %collective-permute-done.1.near_ref, ...), custom_call_target="tpu_custom_call" | custom-call | flops 5898240 | bytes 2949120 | tf_op jit(solution)/shard_map/pallas_call | solution.py:324
  12.2 0.2 collective-permute-start.2
  12.4 2.0 %collective-permute-done.3.far_ref = bf16[2,72,1024]{2,1,0:T(8,128)(2,1)S(1)} collective-permute-done((bf16[2,72,1024]{2,1,0:T(8,128)(2,1)S(1)}, bf16[2,72,1024]{2,1,0:T(8,128)(2,1)S(1)}, u32[]{:S(2)}, u32[]{:S(2)}) %collective-permute-start.3) | collective-permute-done | bytes 294944 | tf_op jit(solution)/shard_map/ppermute | solution.py:448
  14.4 1.1 shard_map.130.u_ref
  15.5 0.0 collective-permute-done.2.other_ref
  15.6 12.8 %all_to_all.40.parts_ref = f32[16,2,1024]{2,1,0:T(2,128)S(1)} all-to-all(f32[16,2,1024]{2,1,0:T(2,128)S(1)} %shard_map.131), channel_id=1, replica_groups=mesh['batch_0'=8,'batch_1'=4,'space_0'=4,'space_1'=2] {'batch_1','space_0'}, dimensions={0} | all-to-all | bytes 262144 | tf_op jit(solution)/shard_map/all_to_all | solution.py:438
  28.3 0.1 shard_map.132
  28.4 16.6 %all_to_all.41.refs_2_.parts_ref = f32[8,2,1024]{2,1,0:T(2,128)S(1)} all-to-all(f32[8,2,1024]{2,1,0:T(2,128)S(1)} %shard_map.132), channel_id=1, replica_groups=mesh['batch_0'=8,'batch_1'=4,'space_0'=4,'space_1'=2] {'batch_0'}, dimensions={0} | all-to-all | bytes 131072 | tf_op jit(solution)/shard_map/all_to_all | solution.py:441
  45.0 0.0 copy-done.5
  45.0 0.0 copy-done.6
  45.1 3.7 %shard_map.133 = (f32[12,72,1536]{2,1,0:T(8,128)S(1)}, f32[2,1536]{1,0:T(2,128)S(1)}) custom-call(f32[4,72,1024]{2,1,0:T(8,128)S(1)} %get-tuple-element.31.refs_0_, f32[8,72,1024]{2,1,0:T(8,128)S(1)} %get-tuple-element.32.refs_1_, f32[8,2,1024]{2,1,0:T(2,128)S(1)} %all_to_all.41.refs_2_.parts_ref, f32[8,128]{1,0:T(8,128)S(1)} %bitcast.12, ...), custom_call_target="tpu_custom_call" | custom-call | flops 2717908992 | bytes 11993088 | tf_op jit(solution)/shard_map/pallas_call | solution.py:339
  48.8 0.0 copy-start
  48.8 0.0 copy-start.1
  48.8 0.0 copy-start.2
  48.8 0.1 collective-permute-start.4
  48.9 1.8 %shard_map.134.outer_ref = f32[4,72,1536]{2,1,0:T(8,128)S(1)} custom-call(f32[4,72,1024]{2,1,0:T(8,128)S(1)} %shard_map.130.u_ref, f32[8,2,1024]{2,1,0:T(2,128)S(1)} %all_to_all.41.refs_2_.parts_ref, f32[8,128]{1,0:T(8,128)S(1)} %bitcast.13, f32[8,128]{1,0:T(8,128)S(1)} %bitcast.15, bf16[1024,1536]{1,0:T(8,128)(2,1)S(1)} %get-tuple-element.36.refs_5_.weight_ref), custom_call_target="tpu_custom_call" | custom-call | flops 905969664 | bytes 6094848 | tf_op jit(solution)/shard_map/pallas_call | solution.py:373
  50.7 0.0 collective-permute-done.4.other_ref
  50.7 11.7 %all_to_all.42.parts_ref = f32[16,2,1536]{2,1,0:T(2,128)S(1)} all-to-all(f32[16,2,1536]{2,1,0:T(2,128)S(1)} %shard_map.135), channel_id=1, replica_groups=mesh['batch_0'=8,'batch_1'=4,'space_0'=4,'space_1'=2] {'batch_1','space_0'}, dimensions={0} | all-to-all | bytes 393216 | tf_op jit(solution)/shard_map/all_to_all | solution.py:438
  62.4 0.1 shard_map.136
  62.5 11.1 %all_to_all.43.parts_ref = f32[8,2,1536]{2,1,0:T(2,128)S(1)} all-to-all(f32[8,2,1536]{2,1,0:T(2,128)S(1)} %shard_map.136), channel_id=1, replica_groups=mesh['batch_0'=8,'batch_1'=4,'space_0'=4,'space_1'=2] {'batch_0'}, dimensions={0} | all-to-all | bytes 196608 | tf_op jit(solution)/shard_map/all_to_all | solution.py:441
  73.6 0.0 copy-done
  73.6 0.0 copy-done.1
  73.6 0.0 copy-done.2
  73.7 0.0 copy-start.7
  73.7 0.0 copy-start.8
  73.7 5.4 %shard_map.137 = (f32[12,72,1536]{2,1,0:T(8,128)S(1)}, f32[2,1536]{1,0:T(2,128)S(1)}, bf16[1536,2048]{1,0:T(8,128)(2,1)S(1)}) custom-call(f32[12,72,1536]{2,1,0:T(8,128)S(1)} %get-tuple-element.37.u_ref, f32[4,72,1536]{2,1,0:T(8,128)S(1)} %shard_map.134.outer_ref, f32[8,2,1536]{2,1,0:T(2,128)S(1)} %all_to_all.43.parts_ref, f32[12,128]{1,0:T(8,128)S(1)} %bitcast.8, ...), custom_call_target="tpu_custom_call" | custom-call | flops 34504704 | bytes 10616832 | tf_op jit(solution)/shard_map/pallas_call | solution.py:387
  79.1 0.1 collective-permute-start.5
  79.2 1.2 collective-permute-done.5.other_ref
  80.4 11.3 %all_to_all.44.parts_ref = f32[16,2,1536]{2,1,0:T(2,128)S(1)} all-to-all(f32[16,2,1536]{2,1,0:T(2,128)S(1)} %shard_map.138), channel_id=1, replica_groups=mesh['batch_0'=8,'batch_1'=4,'space_0'=4,'space_1'=2] {'batch_1','space_0'}, dimensions={0} | all-to-all | bytes 393216 | tf_op jit(solution)/shard_map/all_to_all | solution.py:438
  91.7 0.1 shard_map.139
  91.8 11.1 %all_to_all.45.refs_1_ = f32[8,2,1536]{2,1,0:T(2,128)S(1)} all-to-all(f32[8,2,1536]{2,1,0:T(2,128)S(1)} %shard_map.139), channel_id=1, replica_groups=mesh['batch_0'=8,'batch_1'=4,'space_0'=4,'space_1'=2] {'batch_0'}, dimensions={0} | all-to-all | bytes 196608 | tf_op jit(solution)/shard_map/all_to_all | solution.py:441
  102.9 0.0 copy-done.7
  102.9 0.0 copy-done.8
  102.9 0.0 copy-start.3
  102.9 0.0 copy-start.4
  102.9 6.9 %shard_map.140 = (f32[12,72,2048]{2,1,0:T(8,128)S(1)}, f32[2,2048]{1,0:T(2,128)S(1)}) custom-call(f32[12,72,1536]{2,1,0:T(8,128)S(1)} %get-tuple-element.42.refs_0_, f32[8,2,1536]{2,1,0:T(2,128)S(1)} %all_to_all.45.refs_1_, f32[12,128]{1,0:T(8,128)S(1)} %bitcast.16, f32[12,128]{1,0:T(8,128)S(1)} %bitcast.17, bf16[1536,2048]{1,0:T(8,128)(2,1)S(1)} %get-tuple-element.44.refs_4_), custom_call_target="tpu_custom_call" | custom-call | flops 5435817984 | bytes 18677760 | tf_op jit(solution)/shard_map/pallas_call | solution.py:339
  109.8 0.1 collective-permute-start.6
  109.9 1.2 collective-permute-done.6.other_ref
  111.1 12.0 %all_to_all.46.parts_ref = f32[16,2,2048]{2,1,0:T(2,128)S(1)} all-to-all(f32[16,2,2048]{2,1,0:T(2,128)S(1)} %shard_map.141), channel_id=1, replica_groups=mesh['batch_0'=8,'batch_1'=4,'space_0'=4,'space_1'=2] {'batch_1','space_0'}, dimensions={0} | all-to-all | bytes 524288 | tf_op jit(solution)/shard_map/all_to_all | solution.py:438
  123.1 0.1 shard_map.142
  123.2 11.5 %all_to_all.47.parts_ref = f32[8,2,2048]{2,1,0:T(2,128)S(1)} all-to-all(f32[8,2,2048]{2,1,0:T(2,128)S(1)} %shard_map.142), channel_id=1, replica_groups=mesh['batch_0'=8,'batch_1'=4,'space_0'=4,'space_1'=2] {'batch_0'}, dimensions={0} | all-to-all | bytes 262144 | tf_op jit(solution)/shard_map/all_to_all | solution.py:441
  134.7 0.0 copy-done.3
  134.7 0.0 copy-done.4
  134.7 2.0 %shard_map.143 = bf16[1,12,72,2048]{3,2,1,0:T(8,128)(2,1)} custom-call(f32[12,72,2048]{2,1,0:T(8,128)S(1)} %get-tuple-element.45.u_ref, f32[8,2,2048]{2,1,0:T(2,128)S(1)} %all_to_all.47.parts_ref, f32[16,128]{1,0:T(8,128)S(1)} %bitcast.10, f32[16,128]{1,0:T(8,128)S(1)} %bitcast.11), custom_call_target="tpu_custom_call" | custom-call | flops 5308416 | bytes 10616832 | tf_op jit(solution)/shard_map/pallas_call | solution.py:406
  (4 shorter events, 0.1 us)
Async XLA Ops:
  2.0 8.8 %collective-permute-start = (bf16[4,72,1024]{2,1,0:T(8,128)(2,1)S(1)}, bf16[4,72,1024]{2,1,0:T(8,128)(2,1)S(1)}, u32[]{:S(2)}, u32[]{:S(2)}) collective-permute-start(bf16[4,72,1024]{2,1,0:T(8,128)(2,1)S(1)} %get-tuple-element.27), channel_id=1, source_target_pairs={{0,1},{1,0},{2,3},{3,2},{4,5},{5,4},{6,7},{7,6},{8,9},{9,8},{10,11... | collective-permute-start | bytes 1769480 | tf_op jit(solution)/shard_map/ppermute | solution.py:447
  2.1 8.7 %collective-permute-start.1 = (bf16[2,72,1024]{2,1,0:T(8,128)(2,1)S(1)}, bf16[2,72,1024]{2,1,0:T(8,128)(2,1)S(1)}, u32[]{:S(2)}, u32[]{:S(2)}) collective-permute-start(bf16[2,72,1024]{2,1,0:T(8,128)(2,1)S(1)} %get-tuple-element.28), channel_id=1, source_target_pairs={{1,2},{2,1},{3,4},{4,3},{5,6},{6,5},{9,10},{10,9},{11,12},{12,11},... | collective-permute-start | bytes 884744 | tf_op jit(solution)/shard_map/ppermute | solution.py:446
  6.4 8.0 %collective-permute-start.3 = (bf16[2,72,1024]{2,1,0:T(8,128)(2,1)S(1)}, bf16[2,72,1024]{2,1,0:T(8,128)(2,1)S(1)}, u32[]{:S(2)}, u32[]{:S(2)}) collective-permute-start(bf16[2,72,1024]{2,1,0:T(8,128)(2,1)S(1)} %get-tuple-element.34), channel_id=1, source_target_pairs={{1,2},{2,1},{3,4},{4,3},{5,6},{6,5},{9,10},{10,9},{11,12},{12,11},... | collective-permute-start | bytes 884744 | tf_op jit(solution)/shard_map/ppermute | solution.py:448
  10.8 34.3 %copy-start.5 = (f32[1024]{0:T(1024)S(1)}, f32[1024]{0:T(1024)}, u32[]{:S(2)}) copy-start(f32[1024]{0:T(1024)} %param.15) | copy-start | bytes 12292
  10.8 34.3 %copy-start.6 = (f32[1024]{0:T(1024)S(1)}, f32[1024]{0:T(1024)}, u32[]{:S(2)}) copy-start(f32[1024]{0:T(1024)} %param.16) | copy-start | bytes 12292
  12.2 3.3 %collective-permute-start.2 = (f32[2,1024]{1,0:T(2,128)S(1)}, f32[2,1024]{1,0:T(2,128)S(1)}, u32[]{:S(2)}, u32[]{:S(2)}) collective-permute-start(f32[2,1024]{1,0:T(2,128)S(1)} %get-tuple-element.33.own_ref), channel_id=1, source_target_pairs={{0,1},{1,0},{2,3},{3,2},{4,5},{5,4},{6,7},{7,6},{8,9},{9,8},{10,11... | collective-permute-start | bytes 24584 | tf_op jit(solution)/shard_map/ppermute | solution.py:433
  48.8 24.8 %copy-start = (bf16[3,3,1536]{2,1,0:T(4,128)(2,1)S(1)}, bf16[3,3,1536]{2,1,0:T(4,128)(2,1)}, u32[]{:S(2)}) copy-start(bf16[3,3,1536]{2,1,0:T(4,128)(2,1)} %filter_ref.1) | copy-start | bytes 82948
  48.8 24.8 %copy-start.1 = (f32[1536]{0:T(1024)S(1)}, f32[1536]{0:T(1024)}, u32[]{:S(2)}) copy-start(f32[1536]{0:T(1024)} %param.18) | copy-start | bytes 18436
  48.8 24.8 %copy-start.2 = (f32[1536]{0:T(1024)S(1)}, f32[1536]{0:T(1024)}, u32[]{:S(2)}) copy-start(f32[1536]{0:T(1024)} %param.19) | copy-start | bytes 18436
  48.8 1.9 %collective-permute-start.4 = (f32[2,1536]{1,0:T(2,128)S(1)}, f32[2,1536]{1,0:T(2,128)S(1)}, u32[]{:S(2)}, u32[]{:S(2)}) collective-permute-start(f32[2,1536]{1,0:T(2,128)S(1)} %get-tuple-element.38.own_ref), channel_id=1, source_target_pairs={{0,1},{1,0},{2,3},{3,2},{4,5},{5,4},{6,7},{7,6},{8,9},{9,8},{10,11... | collective-permute-start | bytes 36872 | tf_op jit(solution)/shard_map/ppermute | solution.py:433
  73.7 29.3 %copy-start.7 = (f32[1536]{0:T(1024)S(1)}, f32[1536]{0:T(1024)}, u32[]{:S(2)}) copy-start(f32[1536]{0:T(1024)} %param.21) | copy-start | bytes 18436
  73.7 29.3 %copy-start.8 = (f32[1536]{0:T(1024)S(1)}, f32[1536]{0:T(1024)}, u32[]{:S(2)}) copy-start(f32[1536]{0:T(1024)} %param.22) | copy-start | bytes 18436
  79.1 1.3 collective-permute-start.5
  102.9 31.8 %copy-start.3 = (f32[2048]{0:T(1024)S(1)}, f32[2048]{0:T(1024)}, u32[]{:S(2)}) copy-start(f32[2048]{0:T(1024)} %param.24) | copy-start | bytes 24580
  102.9 31.8 %copy-start.4 = (f32[2048]{0:T(1024)S(1)}, f32[2048]{0:T(1024)}, u32[]{:S(2)}) copy-start(f32[2048]{0:T(1024)} %param.25) | copy-start | bytes 24580
  109.8 1.3 collective-permute-start.6

commit v5 on v4

--- a/solution.py
+++ b/solution.py
@@ -10,6 +10,7 @@
 
 RATE = 2
 LANES = 128
+PAD = 8
 BATCH = ("batch_0", "batch_1")
 SPACE = ("space_0", "space_1")
 
@@ -76,22 +77,40 @@
     return total, squares
 
 
-def inner_body(x_ref, filter_ref, weight_hbm, out_ref, sums_ref, weight_ref, arrived):
-    count = x_ref.shape[0]
-    weight_copy = pltpu.make_async_copy(weight_hbm, weight_ref, arrived)
+def inner_body(
+    x_hbm, filter_hbm, weight_hbm, out_ref, sums_ref, x_ref, filter_ref, weight_ref, arrived,
+    filter_arrived, weight_arrived,
+):
+    count, _, depth = x_ref.shape
+    wide = depth // arrived.shape[0]
+
+    def piece(place):
+        lanes = pl.ds(place * wide, wide)
+        return pltpu.make_async_copy(
+            x_hbm.at[0, :, :, lanes], x_ref.at[:, :, lanes], arrived.at[place]
+        )
+
+    taps_copy = pltpu.make_async_copy(filter_hbm, filter_ref, filter_arrived)
+    taps_copy.start()
+    for place in range(arrived.shape[0]):
+        piece(place).start()
+    weight_copy = pltpu.make_async_copy(weight_hbm, weight_ref, weight_arrived)
     weight_copy.start()
-
-    @pl.loop(0, x_ref.shape[2] // LANES)
-    def _(block):
-        lanes = pl.ds(pl.multiple_of(block * LANES, LANES), LANES)
-        total, squares = dilated_rows(
-            functools.cache(lambda row: x_ref[row, :, lanes].astype(jnp.float32)),
-            range(RATE, count - RATE),
-            taps_of(filter_ref, lanes),
-            out_ref,
-            lanes,
-        )
-        store_sums(sums_ref, lanes, total, squares)
+    taps_copy.wait()
+    for place in range(arrived.shape[0]):
+        piece(place).wait()
+
+        @pl.loop(place * wide // LANES, (place + 1) * wide // LANES)
+        def _(block):
+            lanes = pl.ds(pl.multiple_of(block * LANES, LANES), LANES)
+            total, squares = dilated_rows(
+                functools.cache(lambda row: x_ref[row, :, lanes].astype(jnp.float32)),
+                range(RATE, count - RATE),
+                taps_of(filter_ref, lanes),
+                out_ref,
+                lanes,
+            )
+            store_sums(sums_ref, lanes, total, squares)
 
     weight_copy.wait()
 
@@ -105,7 +124,7 @@
     )
 
 
-def load_body(x_hbm, filter_hbm, chip_ref, near_ref, far_ref, x_ref, filter_ref, arrived):
+def load_body(x_hbm, chip_ref, near_ref, far_ref, arrived):
     starts = edge_starts(x_hbm.shape[1])
     copies = [
         pltpu.make_async_copy(
@@ -113,8 +132,6 @@
         )
         for place, (start, out_ref) in enumerate(zip(starts, (chip_ref, near_ref, far_ref)))
     ]
-    copies.append(pltpu.make_async_copy(x_hbm.at[0], x_ref, arrived.at[3]))
-    copies.append(pltpu.make_async_copy(filter_hbm, filter_ref, arrived.at[4]))
     for copy in copies:
         copy.start()
     for copy in copies:
@@ -186,12 +203,16 @@
 
 def third_body(
     pixels, u_ref, outer_ref, parts_ref, gain_ref, shift_ref, filter_ref,
-    weight_hbm, out_ref, sums_ref, weight_ref, terms_ref, arrived,
+    weight_hbm, out_ref, sums_ref, weight_ref, terms_ref, padded_ref, arrived,
 ):
     count = u_ref.shape[0]
     weight_copy = pltpu.make_async_copy(weight_hbm, weight_ref, arrived)
     weight_copy.start()
     store_terms(terms_ref, parts_ref, gain_ref, shift_ref, pixels)
+    cols = u_ref.shape[1]
+    gap = jnp.zeros((count + 2 * RATE, PAD, LANES), jnp.float32)
+    padded_ref[:, :PAD] = gap
+    padded_ref[:, PAD + cols :] = gap
 
     @pl.loop(0, u_ref.shape[2] // LANES)
     def _(block):
@@ -203,7 +224,6 @@
         above = (strip > 0).astype(jnp.float32)
         below = (strip < lax.axis_size(SPACE) - 1).astype(jnp.float32)
 
-        @functools.cache
         def row_at(row):
             if row < 0:
                 value = outer_ref[row + RATE, :, lanes]
@@ -215,7 +235,20 @@
                 value = u_ref[row, :, lanes] * factor + offset
             return jnp.maximum(value, 0.0).astype(jnp.bfloat16).astype(jnp.float32)
 
-        total, squares = dilated_rows(row_at, range(count), taps, out_ref, lanes)
+        for row in range(-RATE, count + RATE):
+            padded_ref[row + RATE, PAD : PAD + cols] = row_at(row)
+        total = squares = 0.0
+        for row in range(count):
+            value = None
+            for tap_row in range(3):
+                for tap_col in range(3):
+                    first_col = PAD + (tap_col - 1) * RATE
+                    term = padded_ref[row + tap_row * RATE, first_col : first_col + cols]
+                    term = term * taps[tap_row][tap_col : tap_col + 1]
+                    value = term if value is None else value + term
+            out_ref[row, :, lanes] = value
+            total = total + summed_rows(value)
+            squares = squares + summed_rows(value * value)
         store_sums(sums_ref, lanes, total, squares)
 
     weight_copy.wait()
@@ -284,18 +317,20 @@
 
 
 def dilated_inner(x, taps, weight):
-    rows, cols, depth = x.shape
+    rows, cols, depth = x.shape[1:]
     inner = rows - 2 * RATE
     return pl.pallas_call(
         inner_body,
         out_shape=[
             pltpu.VMEM((inner, cols, depth), jnp.float32),
             pltpu.VMEM((2, depth), jnp.float32),
+            pltpu.VMEM((rows, cols, depth), x.dtype),
+            pltpu.VMEM(taps.shape, taps.dtype),
             pltpu.VMEM(weight.shape, weight.dtype),
         ],
-        in_specs=[VMEM] * 2 + [HBM],
-        out_specs=[VMEM] * 3,
-        scratch_shapes=[pltpu.SemaphoreType.DMA],
+        in_specs=[HBM] * 3,
+        out_specs=[VMEM] * 5,
+        scratch_shapes=[pltpu.SemaphoreType.DMA((4,))] + [pltpu.SemaphoreType.DMA] * 2,
         compiler_params=pltpu.CompilerParams(vmem_limit_bytes=12 << 20),
         cost_estimate=pl.CostEstimate(
             flops=20 * inner * cols * depth, bytes_accessed=6 * rows * cols * depth, transcendentals=0
@@ -307,16 +342,16 @@
     return pltpu.with_memory_space_constraint(array, pltpu.HBM)
 
 
-def loaded(x, taps):
+def edge_rows(x):
     edges = [(count,) + x.shape[2:] for count in (2 * RATE, RATE, RATE)]
     return pl.pallas_call(
         load_body,
-        out_shape=[pltpu.VMEM(shape, x.dtype) for shape in (*edges, x.shape[1:], taps.shape)],
-        in_specs=[HBM] * 2,
-        out_specs=[VMEM] * 5,
-        scratch_shapes=[pltpu.SemaphoreType.DMA((5,))],
+        out_shape=[pltpu.VMEM(shape, x.dtype) for shape in edges],
+        in_specs=[HBM],
+        out_specs=[VMEM] * 3,
+        scratch_shapes=[pltpu.SemaphoreType.DMA((3,))],
         compiler_params=pltpu.CompilerParams(vmem_limit_bytes=4 << 20),
-    )(x, taps)
+    )(x)
 
 
 def dilated_edges(x, chip, near, weight, inner_sums):
@@ -393,7 +428,11 @@
         ],
         in_specs=[VMEM] * 6 + [HBM],
         out_specs=[VMEM] * 3,
-        scratch_shapes=[pltpu.VMEM((2, depth), jnp.float32), pltpu.SemaphoreType.DMA],
+        scratch_shapes=[
+            pltpu.VMEM((2, depth), jnp.float32),
+            pltpu.VMEM((rows + 2 * RATE, cols + 2 * PAD, LANES), jnp.float32),
+            pltpu.SemaphoreType.DMA,
+        ],
         compiler_params=pltpu.CompilerParams(vmem_limit_bytes=16 << 20),
         cost_estimate=pl.CostEstimate(
             flops=26 * rows * cols * depth, bytes_accessed=8 * rows * cols * depth, transcendentals=0
@@ -467,9 +506,11 @@
     pixels = rows * cols * lax.axis_size(BATCH) * lax.axis_size(SPACE)
     names = (gain_one, shift_one, gain_two, shift_two, gain_three, shift_three, gain_four, shift_four)
     terms = [term.reshape(-1, LANES) for term in names]
-    chip, near, far, x, taps = loaded(kept_in_hbm(features), kept_in_hbm(depth_one))
-    chip, near, far = from_neighbours(chip, near, far)
-    inner, inner_sums, weight = dilated_inner(x, taps, kept_in_hbm(point_one))
+    features = kept_in_hbm(features)
+    chip, near, far = from_neighbours(*edge_rows(features))
+    inner, inner_sums, x, taps, weight = dilated_inner(
+        features, kept_in_hbm(depth_one), kept_in_hbm(point_one)
+    )
     edges, sums = dilated_edges(x, chip, near, taps, inner_sums)
     parts, outer = gathered_sums(sums, dilated_outer(x, chip, near, far, taps))
     second, sums = project(pixels, (edges, inner), (0, RATE), parts, *terms[0:2], weight)

time: 137 us -> 136 us (level)
  transfers between devices with their start and end apart: 7 -> 7, of which waited for: 4 -> 3; matrix products, arithmetic and copies ran while one was open for 0% -> 0% of each run, Pallas kernels for 5% -> 6%
where the time goes in v5:
time: 136 us
  blocking collectives  98.1 us (72%)
  Pallas kernels  27.1 us (20%)
  starting transfers between devices  6.65 us (5%)
  waiting for transfers between devices  3.57 us (3%)
    all_to_all x4, blocking collectives, gathered_sums(): return (lax.all_to_all(copies, line, 0, 0), beside)  50.3 us
    all_to_all x4, blocking collectives, gathered_sums(): parts = lax.all_to_all(copies, plane, 0, 0)  47.8 us
    pallas_call x2, Pallas kernels, project(): pl.pallas_call(functools.partial(project_body, pixels, places, len(pieces...  10.6 us
    pallas_call x1, Pallas kernels, dilated_second(): pl.pallas_call(functools.partial(third_body, pixels), out_shape=[pltpu.VM...  5.14 us
    ppermute x1, starting transfers between devices, from_neighbours(): near = lax.ppermute(near, SPACE, ends)  4.27 us
    pallas_call x1, Pallas kernels, dilated_inner(): pl.pallas_call(inner_body, out_shape=[pltpu.VMEM((inner, cols, depth), jn...  3.3 us
  transfers between devices with their start and end apart: 7, of which 3 were waited for; matrix products, arithmetic and copies ran while one was open for 0% of the time, Pallas kernels for 6%

profile of v5, /device:TPU:2, one launch (start us, length us, event | category | flops | bytes accessed | tf_op | source)
XLA Modules:
  0.0 135.7 jit_solution(11744887138236129115)
XLA Ops:
  0.0 1.3 shard_map.128
  1.3 0.1 collective-permute-start
  1.4 4.3 %collective-permute-start.1 = (bf16[2,72,1024]{2,1,0:T(8,128)(2,1)S(1)}, bf16[2,72,1024]{2,1,0:T(8,128)(2,1)S(1)}, u32[]{:S(2)}, u32[]{:S(2)}) collective-permute-start(bf16[2,72,1024]{2,1,0:T(8,128)(2,1)S(1)} %get-tuple-element.28), channel_id=1, source_target_pairs={{1,2},{2,1},{3,4},{4,3},{5,6},{6,5},{9,10},{10,9},{11,12},{12,11},... | collective-permute-start | bytes 884744 | tf_op jit(solution)/shard_map/ppermute | solution.py:485
  5.6 1.9 %collective-permute-start.3 = (bf16[2,72,1024]{2,1,0:T(8,128)(2,1)S(1)}, bf16[2,72,1024]{2,1,0:T(8,128)(2,1)S(1)}, u32[]{:S(2)}, u32[]{:S(2)}) collective-permute-start(bf16[2,72,1024]{2,1,0:T(8,128)(2,1)S(1)} %get-tuple-element.34), channel_id=1, source_target_pairs={{1,2},{2,1},{3,4},{4,3},{5,6},{6,5},{9,10},{10,9},{11,12},{12,11},... | collective-permute-start | bytes 884744 | tf_op jit(solution)/shard_map/ppermute | solution.py:487
  7.6 3.3 %shard_map.127 = (f32[8,72,1024]{2,1,0:T(8,128)S(1)}, f32[2,1024]{1,0:T(2,128)S(1)}, bf16[12,72,1024]{2,1,0:T(8,128)(2,1)S(1)}, bf16[3,3,1024]{2,1,0:T(4,128)(2,1)S(1)}, bf16[1024,1536]{1,0:T(8,128)(2,1)S(1)}) custom-call(bf16[1,12,72,1024]{3,2,1,0:T(8,128)(2,1)} %x_hbm.3, bf16[3,3,1024]{2,1,0:T(4,128)(2,1)} %filter_hbm.1, bf16[1024,1536]{1,0:T(8,128)(2,1)} %weight_hbm.2), custom_call_target="tpu_custom_call" | custom-call | flops 11796480 | bytes 5308416 | tf_op jit(solution)/shard_map/pallas_call | solution.py:322
  10.9 0.0 collective-permute-done.1.near_ref
  10.9 0.0 collective-permute-done.chip_ref
  10.9 0.0 copy-start.5
  10.9 0.0 copy-start.6
  10.9 1.4 %shard_map.129 = (f32[4,72,1024]{2,1,0:T(8,128)S(1)}, f32[2,1024]{1,0:T(2,128)S(1)}) custom-call(bf16[12,72,1024]{2,1,0:T(8,128)(2,1)S(1)} %get-tuple-element.26.x_ref, bf16[4,72,1024]{2,1,0:T(8,128)(2,1)S(1)} %collective-permute-done.chip_ref, bf16[2,72,1024]{2,1,0:T(8,128)(2,1)S(1)} %collective-permute-done.1.near_ref, ...), custom_call_target="tpu_custom_call" | custom-call | flops 5898240 | bytes 2949120 | tf_op jit(solution)/shard_map/pallas_call | solution.py:359
  12.4 0.1 collective-permute-start.2
  12.5 1.2 collective-permute-done.3.far_ref
  13.7 1.1 shard_map.130.u_ref
  14.8 0.0 collective-permute-done.2.other_ref
  14.8 12.8 %all_to_all.40.parts_ref = f32[16,2,1024]{2,1,0:T(2,128)S(1)} all-to-all(f32[16,2,1024]{2,1,0:T(2,128)S(1)} %shard_map.131), channel_id=1, replica_groups=mesh['batch_0'=8,'batch_1'=4,'space_0'=4,'space_1'=2] {'batch_1','space_0'}, dimensions={0} | all-to-all | bytes 262144 | tf_op jit(solution)/shard_map/all_to_all | solution.py:477
  27.6 0.1 shard_map.132
  27.7 16.6 %all_to_all.41.refs_2_.parts_ref = f32[8,2,1024]{2,1,0:T(2,128)S(1)} all-to-all(f32[8,2,1024]{2,1,0:T(2,128)S(1)} %shard_map.132), channel_id=1, replica_groups=mesh['batch_0'=8,'batch_1'=4,'space_0'=4,'space_1'=2] {'batch_0'}, dimensions={0} | all-to-all | bytes 131072 | tf_op jit(solution)/shard_map/all_to_all | solution.py:480
  44.3 0.0 copy-done.5
  44.3 0.0 copy-done.6
  44.3 3.7 %shard_map.133 = (f32[12,72,1536]{2,1,0:T(8,128)S(1)}, f32[2,1536]{1,0:T(2,128)S(1)}) custom-call(f32[4,72,1024]{2,1,0:T(8,128)S(1)} %get-tuple-element.31.refs_0_, f32[8,72,1024]{2,1,0:T(8,128)S(1)} %get-tuple-element.32.refs_1_, f32[8,2,1024]{2,1,0:T(2,128)S(1)} %all_to_all.41.refs_2_.parts_ref, f32[8,128]{1,0:T(8,128)S(1)} %bitcast.12, ...), custom_call_target="tpu_custom_call" | custom-call | flops 2717908992 | bytes 11993088 | tf_op jit(solution)/shard_map/pallas_call | solution.py:374
  48.0 0.0 copy-start
  48.1 0.0 copy-start.1
  48.1 0.0 copy-start.2
  48.1 0.1 collective-permute-start.4
  48.2 1.8 %shard_map.134.outer_ref = f32[4,72,1536]{2,1,0:T(8,128)S(1)} custom-call(f32[4,72,1024]{2,1,0:T(8,128)S(1)} %shard_map.130.u_ref, f32[8,2,1024]{2,1,0:T(2,128)S(1)} %all_to_all.41.refs_2_.parts_ref, f32[8,128]{1,0:T(8,128)S(1)} %bitcast.13, f32[8,128]{1,0:T(8,128)S(1)} %bitcast.15, bf16[1024,1536]{1,0:T(8,128)(2,1)S(1)} %get-tuple-element.36.refs_5_.weight_ref), custom_call_target="tpu_custom_call" | custom-call | flops 905969664 | bytes 6094848 | tf_op jit(solution)/shard_map/pallas_call | solution.py:408
  49.9 0.0 collective-permute-done.4.other_ref
  50.0 11.7 %all_to_all.42.parts_ref = f32[16,2,1536]{2,1,0:T(2,128)S(1)} all-to-all(f32[16,2,1536]{2,1,0:T(2,128)S(1)} %shard_map.135), channel_id=1, replica_groups=mesh['batch_0'=8,'batch_1'=4,'space_0'=4,'space_1'=2] {'batch_1','space_0'}, dimensions={0} | all-to-all | bytes 393216 | tf_op jit(solution)/shard_map/all_to_all | solution.py:477
  61.7 0.1 shard_map.136
  61.8 11.1 %all_to_all.43.parts_ref = f32[8,2,1536]{2,1,0:T(2,128)S(1)} all-to-all(f32[8,2,1536]{2,1,0:T(2,128)S(1)} %shard_map.136), channel_id=1, replica_groups=mesh['batch_0'=8,'batch_1'=4,'space_0'=4,'space_1'=2] {'batch_0'}, dimensions={0} | all-to-all | bytes 196608 | tf_op jit(solution)/shard_map/all_to_all | solution.py:480
  72.9 0.0 copy-done
  72.9 0.0 copy-done.1
  72.9 0.0 copy-done.2
  72.9 0.0 copy-start.7
  72.9 0.0 copy-start.8
  72.9 5.1 %shard_map.137 = (f32[12,72,1536]{2,1,0:T(8,128)S(1)}, f32[2,1536]{1,0:T(2,128)S(1)}, bf16[1536,2048]{1,0:T(8,128)(2,1)S(1)}) custom-call(f32[12,72,1536]{2,1,0:T(8,128)S(1)} %get-tuple-element.37.u_ref, f32[4,72,1536]{2,1,0:T(8,128)S(1)} %shard_map.134.outer_ref, f32[8,2,1536]{2,1,0:T(2,128)S(1)} %all_to_all.43.parts_ref, f32[12,128]{1,0:T(8,128)S(1)} %bitcast.8, ...), custom_call_target="tpu_custom_call" | custom-call | flops 34504704 | bytes 10616832 | tf_op jit(solution)/shard_map/pallas_call | solution.py:422
  78.1 0.1 collective-permute-start.5
  78.2 1.2 collective-permute-done.5.other_ref
  79.4 11.3 %all_to_all.44.parts_ref = f32[16,2,1536]{2,1,0:T(2,128)S(1)} all-to-all(f32[16,2,1536]{2,1,0:T(2,128)S(1)} %shard_map.138), channel_id=1, replica_groups=mesh['batch_0'=8,'batch_1'=4,'space_0'=4,'space_1'=2] {'batch_1','space_0'}, dimensions={0} | all-to-all | bytes 393216 | tf_op jit(solution)/shard_map/all_to_all | solution.py:477
  90.7 0.1 shard_map.139
  90.8 11.1 %all_to_all.45.refs_1_ = f32[8,2,1536]{2,1,0:T(2,128)S(1)} all-to-all(f32[8,2,1536]{2,1,0:T(2,128)S(1)} %shard_map.139), channel_id=1, replica_groups=mesh['batch_0'=8,'batch_1'=4,'space_0'=4,'space_1'=2] {'batch_0'}, dimensions={0} | all-to-all | bytes 196608 | tf_op jit(solution)/shard_map/all_to_all | solution.py:480
  101.9 0.0 copy-done.7
  101.9 0.0 copy-done.8
  101.9 0.0 copy-start.3
  101.9 0.0 copy-start.4
  101.9 6.9 %shard_map.140 = (f32[12,72,2048]{2,1,0:T(8,128)S(1)}, f32[2,2048]{1,0:T(2,128)S(1)}) custom-call(f32[12,72,1536]{2,1,0:T(8,128)S(1)} %get-tuple-element.42.refs_0_, f32[8,2,1536]{2,1,0:T(2,128)S(1)} %all_to_all.45.refs_1_, f32[12,128]{1,0:T(8,128)S(1)} %bitcast.16, f32[12,128]{1,0:T(8,128)S(1)} %bitcast.17, bf16[1536,2048]{1,0:T(8,128)(2,1)S(1)} %get-tuple-element.44.refs_4_), custom_call_target="tpu_custom_call" | custom-call | flops 5435817984 | bytes 18677760 | tf_op jit(solution)/shard_map/pallas_call | solution.py:374
  108.8 0.1 collective-permute-start.6
  108.9 1.2 collective-permute-done.6.other_ref
  110.1 12.0 %all_to_all.46.parts_ref = f32[16,2,2048]{2,1,0:T(2,128)S(1)} all-to-all(f32[16,2,2048]{2,1,0:T(2,128)S(1)} %shard_map.141), channel_id=1, replica_groups=mesh['batch_0'=8,'batch_1'=4,'space_0'=4,'space_1'=2] {'batch_1','space_0'}, dimensions={0} | all-to-all | bytes 524288 | tf_op jit(solution)/shard_map/all_to_all | solution.py:477
  122.1 0.1 shard_map.142
  122.2 11.5 %all_to_all.47.parts_ref = f32[8,2,2048]{2,1,0:T(2,128)S(1)} all-to-all(f32[8,2,2048]{2,1,0:T(2,128)S(1)} %shard_map.142), channel_id=1, replica_groups=mesh['batch_0'=8,'batch_1'=4,'space_0'=4,'space_1'=2] {'batch_0'}, dimensions={0} | all-to-all | bytes 262144 | tf_op jit(solution)/shard_map/all_to_all | solution.py:480
  133.7 0.0 copy-done.3
  133.7 0.0 copy-done.4
  133.7 2.0 %shard_map.143 = bf16[1,12,72,2048]{3,2,1,0:T(8,128)(2,1)} custom-call(f32[12,72,2048]{2,1,0:T(8,128)S(1)} %get-tuple-element.45.u_ref, f32[8,2,2048]{2,1,0:T(2,128)S(1)} %all_to_all.47.parts_ref, f32[16,128]{1,0:T(8,128)S(1)} %bitcast.10, f32[16,128]{1,0:T(8,128)S(1)} %bitcast.11), custom_call_target="tpu_custom_call" | custom-call | flops 5308416 | bytes 10616832 | tf_op jit(solution)/shard_map/pallas_call | solution.py:445
  (4 shorter events, 0.1 us)
Async XLA Ops:
  1.3 9.6 %collective-permute-start = (bf16[4,72,1024]{2,1,0:T(8,128)(2,1)S(1)}, bf16[4,72,1024]{2,1,0:T(8,128)(2,1)S(1)}, u32[]{:S(2)}, u32[]{:S(2)}) collective-permute-start(bf16[4,72,1024]{2,1,0:T(8,128)(2,1)S(1)} %get-tuple-element.27), channel_id=1, source_target_pairs={{0,1},{1,0},{2,3},{3,2},{4,5},{5,4},{6,7},{7,6},{8,9},{9,8},{10,11... | collective-permute-start | bytes 1769480 | tf_op jit(solution)/shard_map/ppermute | solution.py:486
  1.4 9.5 %collective-permute-start.1 = (bf16[2,72,1024]{2,1,0:T(8,128)(2,1)S(1)}, bf16[2,72,1024]{2,1,0:T(8,128)(2,1)S(1)}, u32[]{:S(2)}, u32[]{:S(2)}) collective-permute-start(bf16[2,72,1024]{2,1,0:T(8,128)(2,1)S(1)} %get-tuple-element.28), channel_id=1, source_target_pairs={{1,2},{2,1},{3,4},{4,3},{5,6},{6,5},{9,10},{10,9},{11,12},{12,11},... | collective-permute-start | bytes 884744 | tf_op jit(solution)/shard_map/ppermute | solution.py:485
  5.6 8.0 %collective-permute-start.3 = (bf16[2,72,1024]{2,1,0:T(8,128)(2,1)S(1)}, bf16[2,72,1024]{2,1,0:T(8,128)(2,1)S(1)}, u32[]{:S(2)}, u32[]{:S(2)}) collective-permute-start(bf16[2,72,1024]{2,1,0:T(8,128)(2,1)S(1)} %get-tuple-element.34), channel_id=1, source_target_pairs={{1,2},{2,1},{3,4},{4,3},{5,6},{6,5},{9,10},{10,9},{11,12},{12,11},... | collective-permute-start | bytes 884744 | tf_op jit(solution)/shard_map/ppermute | solution.py:487
  10.9 33.4 %copy-start.5 = (f32[1024]{0:T(1024)S(1)}, f32[1024]{0:T(1024)}, u32[]{:S(2)}) copy-start(f32[1024]{0:T(1024)} %param.15) | copy-start | bytes 12292
  10.9 33.4 %copy-start.6 = (f32[1024]{0:T(1024)S(1)}, f32[1024]{0:T(1024)}, u32[]{:S(2)}) copy-start(f32[1024]{0:T(1024)} %param.16) | copy-start | bytes 12292
  12.4 2.4 %collective-permute-start.2 = (f32[2,1024]{1,0:T(2,128)S(1)}, f32[2,1024]{1,0:T(2,128)S(1)}, u32[]{:S(2)}, u32[]{:S(2)}) collective-permute-start(f32[2,1024]{1,0:T(2,128)S(1)} %get-tuple-element.33.own_ref), channel_id=1, source_target_pairs={{0,1},{1,0},{2,3},{3,2},{4,5},{5,4},{6,7},{7,6},{8,9},{9,8},{10,11... | collective-permute-start | bytes 24584 | tf_op jit(solution)/shard_map/ppermute | solution.py:472
  48.0 24.8 %copy-start = (bf16[3,3,1536]{2,1,0:T(4,128)(2,1)S(1)}, bf16[3,3,1536]{2,1,0:T(4,128)(2,1)}, u32[]{:S(2)}) copy-start(bf16[3,3,1536]{2,1,0:T(4,128)(2,1)} %filter_ref.1) | copy-start | bytes 82948
  48.1 24.8 %copy-start.1 = (f32[1536]{0:T(1024)S(1)}, f32[1536]{0:T(1024)}, u32[]{:S(2)}) copy-start(f32[1536]{0:T(1024)} %param.18) | copy-start | bytes 18436
  48.1 24.8 %copy-start.2 = (f32[1536]{0:T(1024)S(1)}, f32[1536]{0:T(1024)}, u32[]{:S(2)}) copy-start(f32[1536]{0:T(1024)} %param.19) | copy-start | bytes 18436
  48.1 1.9 %collective-permute-start.4 = (f32[2,1536]{1,0:T(2,128)S(1)}, f32[2,1536]{1,0:T(2,128)S(1)}, u32[]{:S(2)}, u32[]{:S(2)}) collective-permute-start(f32[2,1536]{1,0:T(2,128)S(1)} %get-tuple-element.38.own_ref), channel_id=1, source_target_pairs={{0,1},{1,0},{2,3},{3,2},{4,5},{5,4},{6,7},{7,6},{8,9},{9,8},{10,11... | collective-permute-start | bytes 36872 | tf_op jit(solution)/shard_map/ppermute | solution.py:472
  72.9 29.0 %copy-start.7 = (f32[1536]{0:T(1024)S(1)}, f32[1536]{0:T(1024)}, u32[]{:S(2)}) copy-start(f32[1536]{0:T(1024)} %param.21) | copy-start | bytes 18436
  72.9 29.0 %copy-start.8 = (f32[1536]{0:T(1024)S(1)}, f32[1536]{0:T(1024)}, u32[]{:S(2)}) copy-start(f32[1536]{0:T(1024)} %param.22) | copy-start | bytes 18436
  78.1 1.3 collective-permute-start.5
  101.9 31.8 %copy-start.3 = (f32[2048]{0:T(1024)S(1)}, f32[2048]{0:T(1024)}, u32[]{:S(2)}) copy-start(f32[2048]{0:T(1024)} %param.24) | copy-start | bytes 24580
  101.9 31.8 %copy-start.4 = (f32[2048]{0:T(1024)S(1)}, f32[2048]{0:T(1024)}, u32[]{:S(2)}) copy-start(f32[2048]{0:T(1024)} %param.25) | copy-start | bytes 24580
  108.8 1.3 collective-permute-start.6

commit v6 on v5

--- a/solution.py
+++ b/solution.py
@@ -254,47 +254,51 @@
     weight_copy.wait()
 
 
-def project_body(pixels, places, n_parts, *refs):
+def project_body(pixels, blocks, n_parts, *refs):
     part_refs = refs[:n_parts]
     parts_ref, gain_ref, shift_ref, weight_ref, out_ref, sums_ref = refs[n_parts : n_parts + 6]
-    terms_ref, act_ref = refs[n_parts + 6 :]
-    count, cols, width = out_ref.shape
-    depth = act_ref.shape[1]
-    wide = 512
+    terms_ref, act_ref, totals_ref = refs[n_parts + 6 :]
+    cols, width = out_ref.shape[1:]
+    rows = act_ref.shape[1] // cols
+    wide = width // 2
     store_terms(terms_ref, parts_ref, gain_ref, shift_ref, pixels)
-    pair = 2
-    for u_ref, first_row in zip(part_refs, places):
-
-        @pl.loop(0, u_ref.shape[0] // pair)
-        def _(step):
-            factor = terms_ref[0:1]
-            offset = terms_ref[1:2]
-            value = u_ref[pl.ds(step * pair, pair)].reshape(pair * cols, depth)
-            row = first_row + step * pair
-            if len(places) > 1 and first_row == 0:
-                row = step * (count - pair)
-            act_ref[pl.ds(pl.multiple_of(row * cols, pair * cols), pair * cols)] = jnp.maximum(
-                value * factor + offset, 0.0
-            ).astype(jnp.bfloat16)
-
-    @pl.loop(0, width // wide)
-    def _(block):
-        lanes = pl.ds(pl.multiple_of(block * wide, wide), wide)
-        result = jnp.dot(act_ref[...], weight_ref[:, lanes], preferred_element_type=jnp.float32)
-        store_sums(sums_ref, lanes, summed_rows(result), summed_rows(result * result))
-        out_ref[:, :, lanes] = result.reshape(count, cols, wide)
+    totals_ref[...] = jnp.zeros_like(totals_ref)
+
+    def norm(step):
+        part, first_row, _ = blocks[step]
+        value = part_refs[part][first_row : first_row + rows].reshape(rows * cols, act_ref.shape[2])
+        act_ref[step % 2] = jnp.maximum(value * terms_ref[0:1] + terms_ref[1:2], 0.0).astype(
+            jnp.bfloat16
+        )
+
+    norm(0)
+    for step, (_, _, spans) in enumerate(blocks):
+        if step + 1 < len(blocks):
+            norm(step + 1)
+        for first_lane in range(0, width, wide):
+            lanes = slice(first_lane, first_lane + wide)
+            result = jnp.dot(
+                act_ref[step % 2], weight_ref[:, lanes], preferred_element_type=jnp.float32
+            )
+            placed = result.reshape(rows, cols, wide)
+            done = 0
+            for out_row, count in spans:
+                out_ref[out_row : out_row + count, :, lanes] = placed[done : done + count]
+                done += count
+            totals_ref[0, :, lanes] += summed_rows(result)
+            totals_ref[1, :, lanes] += summed_rows(result * result)
+    store_sums(sums_ref, slice(None), totals_ref[0], totals_ref[1])
 
 
 def outer_project_body(pixels, u_ref, parts_ref, gain_ref, shift_ref, weight_ref, out_ref, terms_ref, act_ref):
     count, cols, width = out_ref.shape
-    wide = 512
+    wide = width // 2
     store_terms(terms_ref, parts_ref, gain_ref, shift_ref, pixels)
     value = u_ref[...].reshape(count * cols, u_ref.shape[2])
     act_ref[...] = jnp.maximum(value * terms_ref[0:1] + terms_ref[1:2], 0.0).astype(jnp.bfloat16)
 
-    @pl.loop(0, width // wide)
-    def _(block):
-        lanes = pl.ds(pl.multiple_of(block * wide, wide), wide)
+    for first_lane in range(0, width, wide):
+        lanes = slice(first_lane, first_lane + wide)
         result = jnp.dot(act_ref[...], weight_ref[:, lanes], preferred_element_type=jnp.float32)
         out_ref[:, :, lanes] = result.reshape(count, cols, wide)
 
@@ -366,19 +370,20 @@
     )(x, chip, near, weight, inner_sums)
 
 
-def project(pixels, pieces, places, parts, gain, shift, weight):
+def project(pixels, pieces, blocks, parts, gain, shift, weight):
     rows = sum(piece.shape[0] for piece in pieces)
     cols, depth = pieces[0].shape[1:]
     width = weight.shape[1]
     outs = [((rows, cols, width), jnp.float32), ((2, width), jnp.float32)]
     return pl.pallas_call(
-        functools.partial(project_body, pixels, places, len(pieces)),
+        functools.partial(project_body, pixels, blocks, len(pieces)),
         out_shape=[pltpu.VMEM(shape, dtype) for shape, dtype in outs],
         in_specs=[VMEM] * (len(pieces) + 4),
         out_specs=[VMEM] * len(outs),
         scratch_shapes=[
             pltpu.VMEM((2, depth), jnp.float32),
-            pltpu.VMEM((rows * cols, depth), jnp.bfloat16),
+            pltpu.VMEM((2, rows // len(blocks) * cols, depth), jnp.bfloat16),
+            pltpu.VMEM((2, 8, width), jnp.float32),
         ],
         compiler_params=pltpu.CompilerParams(vmem_limit_bytes=24 << 20),
         cost_estimate=pl.CostEstimate(
@@ -508,19 +513,23 @@
     terms = [term.reshape(-1, LANES) for term in names]
     features = kept_in_hbm(features)
     chip, near, far = from_neighbours(*edge_rows(features))
+    step = 2 * RATE
+    in_order = [(0, row, [(row, step)]) for row in range(0, rows, step)]
+    edges_first = [(0, 0, [(0, RATE), (rows - RATE, RATE)])]
+    edges_first += [(1, row, [(row + RATE, step)]) for row in range(0, rows - step, step)]
     inner, inner_sums, x, taps, weight = dilated_inner(
         features, kept_in_hbm(depth_one), kept_in_hbm(point_one)
     )
     edges, sums = dilated_edges(x, chip, near, taps, inner_sums)
     parts, outer = gathered_sums(sums, dilated_outer(x, chip, near, far, taps))
-    second, sums = project(pixels, (edges, inner), (0, RATE), parts, *terms[0:2], weight)
+    second, sums = project(pixels, (edges, inner), edges_first, parts, *terms[0:2], weight)
     outer = project_outer(pixels, outer, parts, *terms[0:2], weight)
     parts, outer = gathered_sums(sums, outer)
     third, sums, weight = dilated_second(
         pixels, second, outer, parts, *terms[2:4], depth_two, kept_in_hbm(point_two)
     )
     parts, _ = gathered_sums(sums)
-    fourth, sums = project(pixels, (third,), (0,), parts, *terms[4:6], weight)
+    fourth, sums = project(pixels, (third,), in_order, parts, *terms[4:6], weight)
     parts, _ = gathered_sums(sums)
     return last_norm(pixels, fourth, parts, *terms[6:8])
 

time: 136 us -> 134 us (0.985)
  Pallas kernels: 27.1 us -> 24.5 us
    pallas_call x2, Pallas kernels: 10.6 us -> 8.74 us  [project(): pl.pallas_call(functools.partial(project_body, pixels, blocks, len(pieces...]
  transfers between devices with their start and end apart: 7 -> 7, of which waited for: 3 -> 3; matrix products, arithmetic and copies ran while one was open for 0% -> 0% of each run, Pallas kernels for 6% -> 5%
where the time goes in v6:
time: 134 us; the launch traced here: 133 us
  blocking collectives  98.1 us (73%)
  Pallas kernels  24.5 us (18%)
  starting transfers between devices  6.65 us (5%)
  waiting for transfers between devices  3.61 us (3%)
    all_to_all x4, blocking collectives, gathered_sums(): return (lax.all_to_all(copies, line, 0, 0), beside)  50.3 us
    all_to_all x4, blocking collectives, gathered_sums(): parts = lax.all_to_all(copies, plane, 0, 0)  47.8 us
    pallas_call x2, Pallas kernels, project(): pl.pallas_call(functools.partial(project_body, pixels, blocks, len(pieces...  8.74 us
    pallas_call x1, Pallas kernels, dilated_second(): pl.pallas_call(functools.partial(third_body, pixels), out_shape=[pltpu.VM...  5.14 us
    ppermute x1, starting transfers between devices, from_neighbours(): near = lax.ppermute(near, SPACE, ends)  4.27 us
    pallas_call x1, Pallas kernels, dilated_inner(): pl.pallas_call(inner_body, out_shape=[pltpu.VMEM((inner, cols, depth), jn...  3.3 us
  transfers between devices with their start and end apart: 7, of which 3 were waited for; matrix products, arithmetic and copies ran while one was open for 0% of the time, Pallas kernels for 5%

profile of v6, /device:TPU:2, one launch (start us, length us, event | category | flops | bytes accessed | tf_op | source)
XLA Modules:
  0.0 133.4 jit_solution(4845206478350646605)
XLA Ops:
  0.0 1.3 shard_map.128
  1.3 0.1 collective-permute-start
  1.4 4.3 %collective-permute-start.1 = (bf16[2,72,1024]{2,1,0:T(8,128)(2,1)S(1)}, bf16[2,72,1024]{2,1,0:T(8,128)(2,1)S(1)}, u32[]{:S(2)}, u32[]{:S(2)}) collective-permute-start(bf16[2,72,1024]{2,1,0:T(8,128)(2,1)S(1)} %get-tuple-element.28), channel_id=1, source_target_pairs={{1,2},{2,1},{3,4},{4,3},{5,6},{6,5},{9,10},{10,9},{11,12},{12,11},... | collective-permute-start | bytes 884744 | tf_op jit(solution)/shard_map/ppermute | solution.py:490
  5.6 1.9 %collective-permute-start.3 = (bf16[2,72,1024]{2,1,0:T(8,128)(2,1)S(1)}, bf16[2,72,1024]{2,1,0:T(8,128)(2,1)S(1)}, u32[]{:S(2)}, u32[]{:S(2)}) collective-permute-start(bf16[2,72,1024]{2,1,0:T(8,128)(2,1)S(1)} %get-tuple-element.34), channel_id=1, source_target_pairs={{1,2},{2,1},{3,4},{4,3},{5,6},{6,5},{9,10},{10,9},{11,12},{12,11},... | collective-permute-start | bytes 884744 | tf_op jit(solution)/shard_map/ppermute | solution.py:492
  7.6 3.3 %shard_map.127 = (f32[8,72,1024]{2,1,0:T(8,128)S(1)}, f32[2,1024]{1,0:T(2,128)S(1)}, bf16[12,72,1024]{2,1,0:T(8,128)(2,1)S(1)}, bf16[3,3,1024]{2,1,0:T(4,128)(2,1)S(1)}, bf16[1024,1536]{1,0:T(8,128)(2,1)S(1)}) custom-call(bf16[1,12,72,1024]{3,2,1,0:T(8,128)(2,1)} %x_hbm.3, bf16[3,3,1024]{2,1,0:T(4,128)(2,1)} %filter_hbm.1, bf16[1024,1536]{1,0:T(8,128)(2,1)} %weight_hbm.2), custom_call_target="tpu_custom_call" | custom-call | flops 11796480 | bytes 5308416 | tf_op jit(solution)/shard_map/pallas_call | solution.py:326
  10.9 0.0 collective-permute-done.1.near_ref
  10.9 0.0 collective-permute-done.chip_ref
  10.9 0.0 copy-start.5
  10.9 0.0 copy-start.6
  10.9 1.4 %shard_map.129 = (f32[4,72,1024]{2,1,0:T(8,128)S(1)}, f32[2,1024]{1,0:T(2,128)S(1)}) custom-call(bf16[12,72,1024]{2,1,0:T(8,128)(2,1)S(1)} %get-tuple-element.26.x_ref, bf16[4,72,1024]{2,1,0:T(8,128)(2,1)S(1)} %collective-permute-done.chip_ref, bf16[2,72,1024]{2,1,0:T(8,128)(2,1)S(1)} %collective-permute-done.1.near_ref, ...), custom_call_target="tpu_custom_call" | custom-call | flops 5898240 | bytes 2949120 | tf_op jit(solution)/shard_map/pallas_call | solution.py:363
  12.4 0.1 collective-permute-start.2
  12.5 1.2 collective-permute-done.3.far_ref
  13.7 1.1 shard_map.130.u_ref
  14.8 0.0 collective-permute-done.2.other_ref
  14.8 12.8 %all_to_all.40.parts_ref = f32[16,2,1024]{2,1,0:T(2,128)S(1)} all-to-all(f32[16,2,1024]{2,1,0:T(2,128)S(1)} %shard_map.131), channel_id=1, replica_groups=mesh['batch_0'=8,'batch_1'=4,'space_0'=4,'space_1'=2] {'batch_1','space_0'}, dimensions={0} | all-to-all | bytes 262144 | tf_op jit(solution)/shard_map/all_to_all | solution.py:482
  27.6 0.1 shard_map.132
  27.7 16.6 %all_to_all.41.refs_2_.parts_ref = f32[8,2,1024]{2,1,0:T(2,128)S(1)} all-to-all(f32[8,2,1024]{2,1,0:T(2,128)S(1)} %shard_map.132), channel_id=1, replica_groups=mesh['batch_0'=8,'batch_1'=4,'space_0'=4,'space_1'=2] {'batch_0'}, dimensions={0} | all-to-all | bytes 131072 | tf_op jit(solution)/shard_map/all_to_all | solution.py:485
  44.3 0.0 copy-done.5
  44.3 0.0 copy-done.6
  44.3 3.0 %shard_map.133 = (f32[12,72,1536]{2,1,0:T(8,128)S(1)}, f32[2,1536]{1,0:T(2,128)S(1)}) custom-call(f32[4,72,1024]{2,1,0:T(8,128)S(1)} %get-tuple-element.31.refs_0_, f32[8,72,1024]{2,1,0:T(8,128)S(1)} %get-tuple-element.32.refs_1_, f32[8,2,1024]{2,1,0:T(2,128)S(1)} %all_to_all.41.refs_2_.parts_ref, f32[8,128]{1,0:T(8,128)S(1)} %bitcast.12, ...), custom_call_target="tpu_custom_call" | custom-call | flops 2717908992 | bytes 11993088 | tf_op jit(solution)/shard_map/pallas_call | solution.py:378
  47.3 0.0 copy-start
  47.3 0.0 copy-start.1
  47.3 0.0 copy-start.2
  47.3 0.1 collective-permute-start.4
  47.4 1.1 shard_map.134.outer_ref
  48.5 0.0 collective-permute-done.4.other_ref
  48.6 11.7 %all_to_all.42.parts_ref = f32[16,2,1536]{2,1,0:T(2,128)S(1)} all-to-all(f32[16,2,1536]{2,1,0:T(2,128)S(1)} %shard_map.135), channel_id=1, replica_groups=mesh['batch_0'=8,'batch_1'=4,'space_0'=4,'space_1'=2] {'batch_1','space_0'}, dimensions={0} | all-to-all | bytes 393216 | tf_op jit(solution)/shard_map/all_to_all | solution.py:482
  60.3 0.1 shard_map.136
  60.4 11.1 %all_to_all.43.parts_ref = f32[8,2,1536]{2,1,0:T(2,128)S(1)} all-to-all(f32[8,2,1536]{2,1,0:T(2,128)S(1)} %shard_map.136), channel_id=1, replica_groups=mesh['batch_0'=8,'batch_1'=4,'space_0'=4,'space_1'=2] {'batch_0'}, dimensions={0} | all-to-all | bytes 196608 | tf_op jit(solution)/shard_map/all_to_all | solution.py:485
  71.5 0.0 copy-done
  71.5 0.0 copy-done.1
  71.5 0.0 copy-done.2
  71.5 0.0 copy-start.7
  71.5 0.0 copy-start.8
  71.5 5.1 %shard_map.137 = (f32[12,72,1536]{2,1,0:T(8,128)S(1)}, f32[2,1536]{1,0:T(2,128)S(1)}, bf16[1536,2048]{1,0:T(8,128)(2,1)S(1)}) custom-call(f32[12,72,1536]{2,1,0:T(8,128)S(1)} %get-tuple-element.37.u_ref, f32[4,72,1536]{2,1,0:T(8,128)S(1)} %shard_map.134.outer_ref, f32[8,2,1536]{2,1,0:T(2,128)S(1)} %all_to_all.43.parts_ref, f32[12,128]{1,0:T(8,128)S(1)} %bitcast.8, ...), custom_call_target="tpu_custom_call" | custom-call | flops 34504704 | bytes 10616832 | tf_op jit(solution)/shard_map/pallas_call | solution.py:427
  76.7 0.1 collective-permute-start.5
  76.8 1.2 collective-permute-done.5.other_ref
  77.9 11.3 %all_to_all.44.parts_ref = f32[16,2,1536]{2,1,0:T(2,128)S(1)} all-to-all(f32[16,2,1536]{2,1,0:T(2,128)S(1)} %shard_map.138), channel_id=1, replica_groups=mesh['batch_0'=8,'batch_1'=4,'space_0'=4,'space_1'=2] {'batch_1','space_0'}, dimensions={0} | all-to-all | bytes 393216 | tf_op jit(solution)/shard_map/all_to_all | solution.py:482
  89.3 0.1 shard_map.139
  89.4 11.1 %all_to_all.45.refs_1_ = f32[8,2,1536]{2,1,0:T(2,128)S(1)} all-to-all(f32[8,2,1536]{2,1,0:T(2,128)S(1)} %shard_map.139), channel_id=1, replica_groups=mesh['batch_0'=8,'batch_1'=4,'space_0'=4,'space_1'=2] {'batch_0'}, dimensions={0} | all-to-all | bytes 196608 | tf_op jit(solution)/shard_map/all_to_all | solution.py:485
  100.5 0.0 copy-done.7
  100.5 0.0 copy-done.8
  100.5 0.0 copy-start.3
  100.5 0.0 copy-start.4
  100.5 5.8 %shard_map.140 = (f32[12,72,2048]{2,1,0:T(8,128)S(1)}, f32[2,2048]{1,0:T(2,128)S(1)}) custom-call(f32[12,72,1536]{2,1,0:T(8,128)S(1)} %get-tuple-element.42.refs_0_, f32[8,2,1536]{2,1,0:T(2,128)S(1)} %all_to_all.45.refs_1_, f32[12,128]{1,0:T(8,128)S(1)} %bitcast.16, f32[12,128]{1,0:T(8,128)S(1)} %bitcast.17, bf16[1536,2048]{1,0:T(8,128)(2,1)S(1)} %get-tuple-element.44.refs_4_), custom_call_target="tpu_custom_call" | custom-call | flops 5435817984 | bytes 18677760 | tf_op jit(solution)/shard_map/pallas_call | solution.py:378
  106.3 0.1 collective-permute-start.6
  106.4 1.2 collective-permute-done.6.other_ref
  107.6 12.0 %all_to_all.46.parts_ref = f32[16,2,2048]{2,1,0:T(2,128)S(1)} all-to-all(f32[16,2,2048]{2,1,0:T(2,128)S(1)} %shard_map.141), channel_id=1, replica_groups=mesh['batch_0'=8,'batch_1'=4,'space_0'=4,'space_1'=2] {'batch_1','space_0'}, dimensions={0} | all-to-all | bytes 524288 | tf_op jit(solution)/shard_map/all_to_all | solution.py:482
  119.6 0.1 shard_map.142
  119.7 11.5 %all_to_all.47.parts_ref = f32[8,2,2048]{2,1,0:T(2,128)S(1)} all-to-all(f32[8,2,2048]{2,1,0:T(2,128)S(1)} %shard_map.142), channel_id=1, replica_groups=mesh['batch_0'=8,'batch_1'=4,'space_0'=4,'space_1'=2] {'batch_0'}, dimensions={0} | all-to-all | bytes 262144 | tf_op jit(solution)/shard_map/all_to_all | solution.py:485
  131.2 0.0 copy-done.3
  131.2 0.0 copy-done.4
  131.2 2.0 %shard_map.143 = bf16[1,12,72,2048]{3,2,1,0:T(8,128)(2,1)} custom-call(f32[12,72,2048]{2,1,0:T(8,128)S(1)} %get-tuple-element.45.u_ref, f32[8,2,2048]{2,1,0:T(2,128)S(1)} %all_to_all.47.parts_ref, f32[16,128]{1,0:T(8,128)S(1)} %bitcast.10, f32[16,128]{1,0:T(8,128)S(1)} %bitcast.11), custom_call_target="tpu_custom_call" | custom-call | flops 5308416 | bytes 10616832 | tf_op jit(solution)/shard_map/pallas_call | solution.py:450
  (4 shorter events, 0.1 us)
Async XLA Ops:
  1.3 9.6 %collective-permute-start = (bf16[4,72,1024]{2,1,0:T(8,128)(2,1)S(1)}, bf16[4,72,1024]{2,1,0:T(8,128)(2,1)S(1)}, u32[]{:S(2)}, u32[]{:S(2)}) collective-permute-start(bf16[4,72,1024]{2,1,0:T(8,128)(2,1)S(1)} %get-tuple-element.27), channel_id=1, source_target_pairs={{0,1},{1,0},{2,3},{3,2},{4,5},{5,4},{6,7},{7,6},{8,9},{9,8},{10,11... | collective-permute-start | bytes 1769480 | tf_op jit(solution)/shard_map/ppermute | solution.py:491
  1.4 9.5 %collective-permute-start.1 = (bf16[2,72,1024]{2,1,0:T(8,128)(2,1)S(1)}, bf16[2,72,1024]{2,1,0:T(8,128)(2,1)S(1)}, u32[]{:S(2)}, u32[]{:S(2)}) collective-permute-start(bf16[2,72,1024]{2,1,0:T(8,128)(2,1)S(1)} %get-tuple-element.28), channel_id=1, source_target_pairs={{1,2},{2,1},{3,4},{4,3},{5,6},{6,5},{9,10},{10,9},{11,12},{12,11},... | collective-permute-start | bytes 884744 | tf_op jit(solution)/shard_map/ppermute | solution.py:490
  5.6 8.0 %collective-permute-start.3 = (bf16[2,72,1024]{2,1,0:T(8,128)(2,1)S(1)}, bf16[2,72,1024]{2,1,0:T(8,128)(2,1)S(1)}, u32[]{:S(2)}, u32[]{:S(2)}) collective-permute-start(bf16[2,72,1024]{2,1,0:T(8,128)(2,1)S(1)} %get-tuple-element.34), channel_id=1, source_target_pairs={{1,2},{2,1},{3,4},{4,3},{5,6},{6,5},{9,10},{10,9},{11,12},{12,11},... | collective-permute-start | bytes 884744 | tf_op jit(solution)/shard_map/ppermute | solution.py:492
  10.9 33.4 %copy-start.5 = (f32[1024]{0:T(1024)S(1)}, f32[1024]{0:T(1024)}, u32[]{:S(2)}) copy-start(f32[1024]{0:T(1024)} %param.15) | copy-start | bytes 12292
  10.9 33.4 %copy-start.6 = (f32[1024]{0:T(1024)S(1)}, f32[1024]{0:T(1024)}, u32[]{:S(2)}) copy-start(f32[1024]{0:T(1024)} %param.16) | copy-start | bytes 12292
  12.4 2.4 %collective-permute-start.2 = (f32[2,1024]{1,0:T(2,128)S(1)}, f32[2,1024]{1,0:T(2,128)S(1)}, u32[]{:S(2)}, u32[]{:S(2)}) collective-permute-start(f32[2,1024]{1,0:T(2,128)S(1)} %get-tuple-element.33.own_ref), channel_id=1, source_target_pairs={{0,1},{1,0},{2,3},{3,2},{4,5},{5,4},{6,7},{7,6},{8,9},{9,8},{10,11... | collective-permute-start | bytes 24584 | tf_op jit(solution)/shard_map/ppermute | solution.py:477
  47.3 24.2 %copy-start = (bf16[3,3,1536]{2,1,0:T(4,128)(2,1)S(1)}, bf16[3,3,1536]{2,1,0:T(4,128)(2,1)}, u32[]{:S(2)}) copy-start(bf16[3,3,1536]{2,1,0:T(4,128)(2,1)} %filter_ref.1) | copy-start | bytes 82948
  47.3 24.2 %copy-start.1 = (f32[1536]{0:T(1024)S(1)}, f32[1536]{0:T(1024)}, u32[]{:S(2)}) copy-start(f32[1536]{0:T(1024)} %param.18) | copy-start | bytes 18436
  47.3 24.2 %copy-start.2 = (f32[1536]{0:T(1024)S(1)}, f32[1536]{0:T(1024)}, u32[]{:S(2)}) copy-start(f32[1536]{0:T(1024)} %param.19) | copy-start | bytes 18436
  47.3 1.3 collective-permute-start.4
  71.5 29.0 %copy-start.7 = (f32[1536]{0:T(1024)S(1)}, f32[1536]{0:T(1024)}, u32[]{:S(2)}) copy-start(f32[1536]{0:T(1024)} %param.21) | copy-start | bytes 18436
  71.5 29.0 %copy-start.8 = (f32[1536]{0:T(1024)S(1)}, f32[1536]{0:T(1024)}, u32[]{:S(2)}) copy-start(f32[1536]{0:T(1024)} %param.22) | copy-start | bytes 18436
  76.7 1.3 collective-permute-start.5
  100.5 30.7 %copy-start.3 = (f32[2048]{0:T(1024)S(1)}, f32[2048]{0:T(1024)}, u32[]{:S(2)}) copy-start(f32[2048]{0:T(1024)} %param.24) | copy-start | bytes 24580
  100.5 30.7 %copy-start.4 = (f32[2048]{0:T(1024)S(1)}, f32[2048]{0:T(1024)}, u32[]{:S(2)}) copy-start(f32[2048]{0:T(1024)} %param.25) | copy-start | bytes 24580
  106.3 1.3 collective-permute-start.6

commit v7 on v6

--- a/solution.py
+++ b/solution.py
@@ -100,7 +100,7 @@
     for place in range(arrived.shape[0]):
         piece(place).wait()
 
-        @pl.loop(place * wide // LANES, (place + 1) * wide // LANES)
+        @pl.loop(place * wide // LANES, (place + 1) * wide // LANES, unroll=2)
         def _(block):
             lanes = pl.ds(pl.multiple_of(block * LANES, LANES), LANES)
             total, squares = dilated_rows(
@@ -155,7 +155,7 @@
 def edge_body(x_ref, chip_ref, near_ref, filter_ref, inner_ref, out_ref, sums_ref):
     count = x_ref.shape[0]
 
-    @pl.loop(0, x_ref.shape[2] // LANES)
+    @pl.loop(0, x_ref.shape[2] // LANES, unroll=2)
     def _(block):
         lanes = pl.ds(pl.multiple_of(block * LANES, LANES), LANES)
 
@@ -174,7 +174,7 @@
 def outer_body(x_ref, chip_ref, near_ref, far_ref, filter_ref, out_ref):
     count = x_ref.shape[0]
 
-    @pl.loop(0, x_ref.shape[2] // LANES)
+    @pl.loop(0, x_ref.shape[2] // LANES, unroll=2)
     def _(block):
         lanes = pl.ds(pl.multiple_of(block * LANES, LANES), LANES)
         taps = taps_of(filter_ref, lanes)
@@ -214,7 +214,7 @@
     padded_ref[:, :PAD] = gap
     padded_ref[:, PAD + cols :] = gap
 
-    @pl.loop(0, u_ref.shape[2] // LANES)
+    @pl.loop(0, u_ref.shape[2] // LANES, unroll=2)
     def _(block):
         lanes = pl.ds(pl.multiple_of(block * LANES, LANES), LANES)
         taps = taps_of(filter_ref, lanes)
@@ -309,7 +309,7 @@
     def piece(row):
         return pltpu.make_async_copy(rows_ref.at[row], out_hbm.at[0, row], sent.at[row])
 
-    @pl.loop(0, u_ref.shape[0])
+    @pl.loop(0, u_ref.shape[0], unroll=3)
     def _(row):
         value = u_ref[row] * terms_ref[0:1] + terms_ref[1:2]
         rows_ref[row] = jnp.maximum(value, 0.0).astype(jnp.bfloat16)

time: 134 us -> 134 us (level)
  no operation moved by 1% of the time
where the time goes in v7:
time: 134 us; the launch traced here: 133 us
  blocking collectives  98.1 us (73%)
  Pallas kernels  24.2 us (18%)
  starting transfers between devices  6.65 us (5%)
  waiting for transfers between devices  3.79 us (3%)
    all_to_all x4, blocking collectives, gathered_sums(): return (lax.all_to_all(copies, line, 0, 0), beside)  50.3 us
    all_to_all x4, blocking collectives, gathered_sums(): parts = lax.all_to_all(copies, plane, 0, 0)  47.8 us
    pallas_call x2, Pallas kernels, project(): pl.pallas_call(functools.partial(project_body, pixels, blocks, len(pieces...  8.74 us
    pallas_call x1, Pallas kernels, dilated_second(): pl.pallas_call(functools.partial(third_body, pixels), out_shape=[pltpu.VM...  5.05 us
    ppermute x1, starting transfers between devices, from_neighbours(): near = lax.ppermute(near, SPACE, ends)  4.27 us
    pallas_call x1, Pallas kernels, dilated_inner(): pl.pallas_call(inner_body, out_shape=[pltpu.VMEM((inner, cols, depth), jn...  3.25 us
  transfers between devices with their start and end apart: 7, of which 3 were waited for; matrix products, arithmetic and copies ran while one was open for 0% of the time, Pallas kernels for 5%

profile of v7, /device:TPU:2, one launch (start us, length us, event | category | flops | bytes accessed | tf_op | source)
XLA Modules:
  0.0 133.2 jit_solution(7078094829322277719)
XLA Ops:
  0.0 1.3 shard_map.128
  1.3 0.1 collective-permute-start
  1.4 4.3 %collective-permute-start.1 = (bf16[2,72,1024]{2,1,0:T(8,128)(2,1)S(1)}, bf16[2,72,1024]{2,1,0:T(8,128)(2,1)S(1)}, u32[]{:S(2)}, u32[]{:S(2)}) collective-permute-start(bf16[2,72,1024]{2,1,0:T(8,128)(2,1)S(1)} %get-tuple-element.28), channel_id=1, source_target_pairs={{1,2},{2,1},{3,4},{4,3},{5,6},{6,5},{9,10},{10,9},{11,12},{12,11},... | collective-permute-start | bytes 884744 | tf_op jit(solution)/shard_map/ppermute | solution.py:490
  5.6 1.9 %collective-permute-start.3 = (bf16[2,72,1024]{2,1,0:T(8,128)(2,1)S(1)}, bf16[2,72,1024]{2,1,0:T(8,128)(2,1)S(1)}, u32[]{:S(2)}, u32[]{:S(2)}) collective-permute-start(bf16[2,72,1024]{2,1,0:T(8,128)(2,1)S(1)} %get-tuple-element.34), channel_id=1, source_target_pairs={{1,2},{2,1},{3,4},{4,3},{5,6},{6,5},{9,10},{10,9},{11,12},{12,11},... | collective-permute-start | bytes 884744 | tf_op jit(solution)/shard_map/ppermute | solution.py:492
  7.6 3.2 %shard_map.127 = (f32[8,72,1024]{2,1,0:T(8,128)S(1)}, f32[2,1024]{1,0:T(2,128)S(1)}, bf16[12,72,1024]{2,1,0:T(8,128)(2,1)S(1)}, bf16[3,3,1024]{2,1,0:T(4,128)(2,1)S(1)}, bf16[1024,1536]{1,0:T(8,128)(2,1)S(1)}) custom-call(bf16[1,12,72,1024]{3,2,1,0:T(8,128)(2,1)} %x_hbm.3, bf16[3,3,1024]{2,1,0:T(4,128)(2,1)} %filter_hbm.1, bf16[1024,1536]{1,0:T(8,128)(2,1)} %weight_hbm.2), custom_call_target="tpu_custom_call" | custom-call | flops 11796480 | bytes 5308416 | tf_op jit(solution)/shard_map/pallas_call | solution.py:326
  10.8 0.0 collective-permute-done.1.near_ref
  10.8 0.0 collective-permute-done.chip_ref
  10.8 0.0 copy-start.5
  10.9 0.0 copy-start.6
  10.9 1.3 shard_map.129
  12.2 0.1 collective-permute-start.2
  12.3 1.4 %collective-permute-done.3.far_ref = bf16[2,72,1024]{2,1,0:T(8,128)(2,1)S(1)} collective-permute-done((bf16[2,72,1024]{2,1,0:T(8,128)(2,1)S(1)}, bf16[2,72,1024]{2,1,0:T(8,128)(2,1)S(1)}, u32[]{:S(2)}, u32[]{:S(2)}) %collective-permute-start.3) | collective-permute-done | bytes 294944 | tf_op jit(solution)/shard_map/ppermute | solution.py:492
  13.7 1.0 shard_map.130.u_ref
  14.7 0.0 collective-permute-done.2.other_ref
  14.8 12.8 %all_to_all.40.parts_ref = f32[16,2,1024]{2,1,0:T(2,128)S(1)} all-to-all(f32[16,2,1024]{2,1,0:T(2,128)S(1)} %shard_map.131), channel_id=1, replica_groups=mesh['batch_0'=8,'batch_1'=4,'space_0'=4,'space_1'=2] {'batch_1','space_0'}, dimensions={0} | all-to-all | bytes 262144 | tf_op jit(solution)/shard_map/all_to_all | solution.py:482
  27.5 0.1 shard_map.132
  27.6 16.6 %all_to_all.41.refs_2_.parts_ref = f32[8,2,1024]{2,1,0:T(2,128)S(1)} all-to-all(f32[8,2,1024]{2,1,0:T(2,128)S(1)} %shard_map.132), channel_id=1, replica_groups=mesh['batch_0'=8,'batch_1'=4,'space_0'=4,'space_1'=2] {'batch_0'}, dimensions={0} | all-to-all | bytes 131072 | tf_op jit(solution)/shard_map/all_to_all | solution.py:485
  44.2 0.0 copy-done.5
  44.2 0.0 copy-done.6
  44.3 3.0 %shard_map.133 = (f32[12,72,1536]{2,1,0:T(8,128)S(1)}, f32[2,1536]{1,0:T(2,128)S(1)}) custom-call(f32[4,72,1024]{2,1,0:T(8,128)S(1)} %get-tuple-element.31.refs_0_, f32[8,72,1024]{2,1,0:T(8,128)S(1)} %get-tuple-element.32.refs_1_, f32[8,2,1024]{2,1,0:T(2,128)S(1)} %all_to_all.41.refs_2_.parts_ref, f32[8,128]{1,0:T(8,128)S(1)} %bitcast.12, ...), custom_call_target="tpu_custom_call" | custom-call | flops 2717908992 | bytes 11993088 | tf_op jit(solution)/shard_map/pallas_call | solution.py:378
  47.2 0.0 copy-start
  47.2 0.0 copy-start.1
  47.2 0.0 copy-start.2
  47.3 0.1 collective-permute-start.4
  47.4 1.1 shard_map.134.outer_ref
  48.5 0.0 collective-permute-done.4.other_ref
  48.5 11.7 %all_to_all.42.parts_ref = f32[16,2,1536]{2,1,0:T(2,128)S(1)} all-to-all(f32[16,2,1536]{2,1,0:T(2,128)S(1)} %shard_map.135), channel_id=1, replica_groups=mesh['batch_0'=8,'batch_1'=4,'space_0'=4,'space_1'=2] {'batch_1','space_0'}, dimensions={0} | all-to-all | bytes 393216 | tf_op jit(solution)/shard_map/all_to_all | solution.py:482
  60.2 0.1 shard_map.136
  60.3 11.1 %all_to_all.43.parts_ref = f32[8,2,1536]{2,1,0:T(2,128)S(1)} all-to-all(f32[8,2,1536]{2,1,0:T(2,128)S(1)} %shard_map.136), channel_id=1, replica_groups=mesh['batch_0'=8,'batch_1'=4,'space_0'=4,'space_1'=2] {'batch_0'}, dimensions={0} | all-to-all | bytes 196608 | tf_op jit(solution)/shard_map/all_to_all | solution.py:485
  71.4 0.0 copy-done
  71.4 0.0 copy-done.1
  71.4 0.0 copy-done.2
  71.4 0.0 copy-start.7
  71.5 0.0 copy-start.8
  71.5 5.1 %shard_map.137 = (f32[12,72,1536]{2,1,0:T(8,128)S(1)}, f32[2,1536]{1,0:T(2,128)S(1)}, bf16[1536,2048]{1,0:T(8,128)(2,1)S(1)}) custom-call(f32[12,72,1536]{2,1,0:T(8,128)S(1)} %get-tuple-element.37.u_ref, f32[4,72,1536]{2,1,0:T(8,128)S(1)} %shard_map.134.outer_ref, f32[8,2,1536]{2,1,0:T(2,128)S(1)} %all_to_all.43.parts_ref, f32[12,128]{1,0:T(8,128)S(1)} %bitcast.8, ...), custom_call_target="tpu_custom_call" | custom-call | flops 34504704 | bytes 10616832 | tf_op jit(solution)/shard_map/pallas_call | solution.py:427
  76.5 0.1 collective-permute-start.5
  76.6 1.2 collective-permute-done.5.other_ref
  77.8 11.3 %all_to_all.44.parts_ref = f32[16,2,1536]{2,1,0:T(2,128)S(1)} all-to-all(f32[16,2,1536]{2,1,0:T(2,128)S(1)} %shard_map.138), channel_id=1, replica_groups=mesh['batch_0'=8,'batch_1'=4,'space_0'=4,'space_1'=2] {'batch_1','space_0'}, dimensions={0} | all-to-all | bytes 393216 | tf_op jit(solution)/shard_map/all_to_all | solution.py:482
  89.1 0.1 shard_map.139
  89.2 11.1 %all_to_all.45.refs_1_ = f32[8,2,1536]{2,1,0:T(2,128)S(1)} all-to-all(f32[8,2,1536]{2,1,0:T(2,128)S(1)} %shard_map.139), channel_id=1, replica_groups=mesh['batch_0'=8,'batch_1'=4,'space_0'=4,'space_1'=2] {'batch_0'}, dimensions={0} | all-to-all | bytes 196608 | tf_op jit(solution)/shard_map/all_to_all | solution.py:485
  100.3 0.0 copy-done.7
  100.3 0.0 copy-done.8
  100.3 0.0 copy-start.3
  100.3 0.0 copy-start.4
  100.4 5.8 %shard_map.140 = (f32[12,72,2048]{2,1,0:T(8,128)S(1)}, f32[2,2048]{1,0:T(2,128)S(1)}) custom-call(f32[12,72,1536]{2,1,0:T(8,128)S(1)} %get-tuple-element.42.refs_0_, f32[8,2,1536]{2,1,0:T(2,128)S(1)} %all_to_all.45.refs_1_, f32[12,128]{1,0:T(8,128)S(1)} %bitcast.16, f32[12,128]{1,0:T(8,128)S(1)} %bitcast.17, bf16[1536,2048]{1,0:T(8,128)(2,1)S(1)} %get-tuple-element.44.refs_4_), custom_call_target="tpu_custom_call" | custom-call | flops 5435817984 | bytes 18677760 | tf_op jit(solution)/shard_map/pallas_call | solution.py:378
  106.1 0.1 collective-permute-start.6
  106.2 1.2 collective-permute-done.6.other_ref
  107.4 12.0 %all_to_all.46.parts_ref = f32[16,2,2048]{2,1,0:T(2,128)S(1)} all-to-all(f32[16,2,2048]{2,1,0:T(2,128)S(1)} %shard_map.141), channel_id=1, replica_groups=mesh['batch_0'=8,'batch_1'=4,'space_0'=4,'space_1'=2] {'batch_1','space_0'}, dimensions={0} | all-to-all | bytes 524288 | tf_op jit(solution)/shard_map/all_to_all | solution.py:482
  119.4 0.1 shard_map.142
  119.6 11.5 %all_to_all.47.parts_ref = f32[8,2,2048]{2,1,0:T(2,128)S(1)} all-to-all(f32[8,2,2048]{2,1,0:T(2,128)S(1)} %shard_map.142), channel_id=1, replica_groups=mesh['batch_0'=8,'batch_1'=4,'space_0'=4,'space_1'=2] {'batch_0'}, dimensions={0} | all-to-all | bytes 262144 | tf_op jit(solution)/shard_map/all_to_all | solution.py:485
  131.0 0.0 copy-done.3
  131.0 0.0 copy-done.4
  131.0 2.0 %shard_map.143 = bf16[1,12,72,2048]{3,2,1,0:T(8,128)(2,1)} custom-call(f32[12,72,2048]{2,1,0:T(8,128)S(1)} %get-tuple-element.45.u_ref, f32[8,2,2048]{2,1,0:T(2,128)S(1)} %all_to_all.47.parts_ref, f32[16,128]{1,0:T(8,128)S(1)} %bitcast.10, f32[16,128]{1,0:T(8,128)S(1)} %bitcast.11), custom_call_target="tpu_custom_call" | custom-call | flops 5308416 | bytes 10616832 | tf_op jit(solution)/shard_map/pallas_call | solution.py:450
  (4 shorter events, 0.1 us)
Async XLA Ops:
  1.3 9.6 %collective-permute-start = (bf16[4,72,1024]{2,1,0:T(8,128)(2,1)S(1)}, bf16[4,72,1024]{2,1,0:T(8,128)(2,1)S(1)}, u32[]{:S(2)}, u32[]{:S(2)}) collective-permute-start(bf16[4,72,1024]{2,1,0:T(8,128)(2,1)S(1)} %get-tuple-element.27), channel_id=1, source_target_pairs={{0,1},{1,0},{2,3},{3,2},{4,5},{5,4},{6,7},{7,6},{8,9},{9,8},{10,11... | collective-permute-start | bytes 1769480 | tf_op jit(solution)/shard_map/ppermute | solution.py:491
  1.4 9.5 %collective-permute-start.1 = (bf16[2,72,1024]{2,1,0:T(8,128)(2,1)S(1)}, bf16[2,72,1024]{2,1,0:T(8,128)(2,1)S(1)}, u32[]{:S(2)}, u32[]{:S(2)}) collective-permute-start(bf16[2,72,1024]{2,1,0:T(8,128)(2,1)S(1)} %get-tuple-element.28), channel_id=1, source_target_pairs={{1,2},{2,1},{3,4},{4,3},{5,6},{6,5},{9,10},{10,9},{11,12},{12,11},... | collective-permute-start | bytes 884744 | tf_op jit(solution)/shard_map/ppermute | solution.py:490
  5.6 8.0 %collective-permute-start.3 = (bf16[2,72,1024]{2,1,0:T(8,128)(2,1)S(1)}, bf16[2,72,1024]{2,1,0:T(8,128)(2,1)S(1)}, u32[]{:S(2)}, u32[]{:S(2)}) collective-permute-start(bf16[2,72,1024]{2,1,0:T(8,128)(2,1)S(1)} %get-tuple-element.34), channel_id=1, source_target_pairs={{1,2},{2,1},{3,4},{4,3},{5,6},{6,5},{9,10},{10,9},{11,12},{12,11},... | collective-permute-start | bytes 884744 | tf_op jit(solution)/shard_map/ppermute | solution.py:492
  10.8 33.4 %copy-start.5 = (f32[1024]{0:T(1024)S(1)}, f32[1024]{0:T(1024)}, u32[]{:S(2)}) copy-start(f32[1024]{0:T(1024)} %param.15) | copy-start | bytes 12292
  10.9 33.4 %copy-start.6 = (f32[1024]{0:T(1024)S(1)}, f32[1024]{0:T(1024)}, u32[]{:S(2)}) copy-start(f32[1024]{0:T(1024)} %param.16) | copy-start | bytes 12292
  12.2 2.5 %collective-permute-start.2 = (f32[2,1024]{1,0:T(2,128)S(1)}, f32[2,1024]{1,0:T(2,128)S(1)}, u32[]{:S(2)}, u32[]{:S(2)}) collective-permute-start(f32[2,1024]{1,0:T(2,128)S(1)} %get-tuple-element.33.own_ref), channel_id=1, source_target_pairs={{0,1},{1,0},{2,3},{3,2},{4,5},{5,4},{6,7},{7,6},{8,9},{9,8},{10,11... | collective-permute-start | bytes 24584 | tf_op jit(solution)/shard_map/ppermute | solution.py:477
  47.2 24.2 %copy-start = (bf16[3,3,1536]{2,1,0:T(4,128)(2,1)S(1)}, bf16[3,3,1536]{2,1,0:T(4,128)(2,1)}, u32[]{:S(2)}) copy-start(bf16[3,3,1536]{2,1,0:T(4,128)(2,1)} %filter_ref.1) | copy-start | bytes 82948
  47.2 24.2 %copy-start.1 = (f32[1536]{0:T(1024)S(1)}, f32[1536]{0:T(1024)}, u32[]{:S(2)}) copy-start(f32[1536]{0:T(1024)} %param.18) | copy-start | bytes 18436
  47.2 24.2 %copy-start.2 = (f32[1536]{0:T(1024)S(1)}, f32[1536]{0:T(1024)}, u32[]{:S(2)}) copy-start(f32[1536]{0:T(1024)} %param.19) | copy-start | bytes 18436
  47.3 1.3 collective-permute-start.4
  71.4 28.9 %copy-start.7 = (f32[1536]{0:T(1024)S(1)}, f32[1536]{0:T(1024)}, u32[]{:S(2)}) copy-start(f32[1536]{0:T(1024)} %param.21) | copy-start | bytes 18436
  71.5 28.9 %copy-start.8 = (f32[1536]{0:T(1024)S(1)}, f32[1536]{0:T(1024)}, u32[]{:S(2)}) copy-start(f32[1536]{0:T(1024)} %param.22) | copy-start | bytes 18436
  76.5 1.3 collective-permute-start.5
  100.3 30.7 %copy-start.3 = (f32[2048]{0:T(1024)S(1)}, f32[2048]{0:T(1024)}, u32[]{:S(2)}) copy-start(f32[2048]{0:T(1024)} %param.24) | copy-start | bytes 24580
  100.3 30.7 %copy-start.4 = (f32[2048]{0:T(1024)S(1)}, f32[2048]{0:T(1024)}, u32[]{:S(2)}) copy-start(f32[2048]{0:T(1024)} %param.25) | copy-start | bytes 24580
  106.1 1.3 collective-permute-start.6
